TPU v7x, 32 devices: a whole 2x2x4 slice. The times are simulated.
32 devices in a mesh: groups: 2 (over x), leaf: 16 (over z, y, core).
Axes of the slice: x: 2, y: 2, z: 4, core: 2. Of those that a mesh axis runs over, the one named last changes fastest.
Arguments:
- points: float32 [256, 64, 256], P(('groups', 'leaf')), parts along dimension 0, may hold values from -6 to 6
- right_side: float32 [256, 256], P(('groups', 'leaf')), parts along dimension 0, may hold values from -6 to 6
- near_mask: int32 [256, 2], P(('groups', 'leaf')), parts along dimension 0, may hold values from 0 to 1, as said below
- far_dest: int32 [256, 4], P(('groups', 'leaf')), parts along dimension 0, may hold values from 0 to 15, all different within a row; in each aligned block of 8 rows (0 to 7, 8 to 15, ...) at most 4 rows name the same one
- far_leaf: int32 [256, 4], P(('groups', 'leaf')), parts along dimension 0, may hold values from 0 to 7
- skeleton: int32 [256, 128], P(('groups', 'leaf')), parts along dimension 0, may hold values from 0 to 255, as said below
- top_index: int32 [32, 128], P(('groups', 'leaf')), parts along dimension 0, may hold values from 0 to 2047, as said below
Outputs:
- solution_field: float32 [256, 256], P(('groups', 'leaf')), parts along dimension 0
- residual: float32 [256, 256], P(('groups', 'leaf')), parts along dimension 0
There are 2 independent parts, one for each index of `groups`. A program takes and returns all parts, laid end to end along the dimension named above; each array names one. Nothing has to cross between parts.
Inputs may be any that keep to these rules, and one draw needn't show every extreme that they name: `near_mask`: each device's 8 rows hold at most 8 ones, and some device holds exactly 8. `skeleton`: entries within a row are distinct. `top_index`: entries within a row are distinct. `far_dest`: entries within a row are distinct; within the rows of one device no device number appears more than 4 times, and some number appears exactly 4 times.
All inputs are finite; a program needn't handle non-finite values.
Results may differ from a plain program's by a relative error of at most 0.0003.
Values sent between devices are 32-bit elements; how exact they have to be, the bound alone decides.
No kernel may reach another device: no remote copies, remote signals or barrier semaphores. Data moves between devices by JAX's collectives and lax.ppermute only.
A program may use at most 64 MiB of HBM per device.

v0:
```python
import jax
import jax.numpy as jnp
from jax import lax
from jax.sharding import PartitionSpec as P

ITERS = 2


HIGHEST = lax.Precision.HIGHEST


def passed_along(block, axis, distance):
    devices = range(lax.axis_size(axis))
    route = [((i - distance) % len(devices), i) for i in devices]
    return lax.ppermute(block, axis, route)


def kernel_block(first_set, second_set):
    scale = 2.0 / first_set.shape[-2]
    cross_dots = jnp.einsum("...dm,...dn->...mn", first_set, second_set, precision=HIGHEST)
    first_sq = jnp.sum(first_set * first_set, axis=-2)
    second_sq = jnp.sum(second_set * second_set, axis=-2)
    distance = first_sq[..., :, None] + second_sq[..., None, :] - 2.0 * cross_dots
    return jnp.exp(-scale * distance)


def on_device(points, right_side, near_mask, far_dest, far_leaf, skeleton, top_index):
    leaves, features, leaf_size = points.shape
    reach = near_mask.shape[1]
    fan_out = far_dest.shape[1]
    skel_rank = skeleton.shape[1]
    top_rank = top_index.shape[1]
    devices = lax.axis_size("leaf")
    capacity = max(2, (2 * leaves * fan_out + devices - 1) // devices)
    slot_total = devices * capacity
    following = passed_along(points[:reach], "leaf", -1)
    extended = jnp.concatenate([points, following], 0)
    flat_mask = near_mask.reshape(-1)
    pair_first = jnp.repeat(jnp.arange(leaves, dtype=jnp.int32), reach)
    pair_second = pair_first + 1 + jnp.tile(jnp.arange(reach, dtype=jnp.int32), leaves)
    slot_weight = flat_mask.astype(jnp.float32)
    near_blocks = pair_first.shape[0] // reach
    bin_ids = jnp.arange(leaves + reach, dtype=jnp.int32)
    first_hot = (pair_first[:, None] == bin_ids[None, :]).astype(jnp.float32) * slot_weight[:, None]
    second_hot = (pair_second[:, None] == bin_ids[None, :]).astype(jnp.float32) * slot_weight[
        :, None
    ]

    def near_apply(values):
        upcoming = passed_along(values[:reach], "leaf", -1)
        wide = jnp.concatenate([values, upcoming], 0)

        def near_one_block(block):
            first_ids, second_ids = block
            tiles = kernel_block(extended[first_ids], extended[second_ids])
            forward = jnp.einsum("smn,sn->sm", tiles, wide[second_ids], precision=HIGHEST)
            backward = jnp.einsum("smn,sm->sn", tiles, wide[first_ids], precision=HIGHEST)
            return (forward, backward)

        forward, backward = lax.map(
            near_one_block,
            (pair_first.reshape(near_blocks, reach), pair_second.reshape(near_blocks, reach)),
        )
        sums = jnp.einsum("sb,sn->bn", first_hot, forward.reshape(-1, leaf_size), precision=HIGHEST)
        sums = sums + jnp.einsum(
            "sb,sn->bn", second_hot, backward.reshape(-1, leaf_size), precision=HIGHEST
        )
        returned = passed_along(sums[leaves:], "leaf", 1)
        returned = jnp.pad(returned, ((0, leaves - reach), (0, 0)))

        def self_block(pair):
            return jnp.dot(kernel_block(pair[0], pair[0]), pair[1], precision=HIGHEST)

        diagonal = lax.map(self_block, (points, values))
        return sums[:leaves] + returned + diagonal

    item_count = leaves * fan_out
    item_dest = far_dest.reshape(-1)
    item_ids = jnp.arange(item_count, dtype=jnp.int32)
    earlier = (item_ids[None, :] < item_ids[:, None]) & (item_dest[None, :] == item_dest[:, None])
    item_slot = item_dest * capacity + jnp.sum(earlier, 1)
    placed = item_slot[None, :] == jnp.arange(slot_total, dtype=jnp.int32)[:, None]
    filled = jnp.any(placed, 1)
    slot_item = jnp.sum(jnp.where(placed, item_ids[None, :], 0), 1)
    slot_leaf = slot_item // fan_out
    target_code = (
        jnp.where(filled, far_leaf.reshape(-1)[slot_item], -1)
        .astype(jnp.float32)
        .reshape(devices, capacity)
    )
    skel_points = jnp.take_along_axis(
        points, jnp.broadcast_to(skeleton[:, None, :], (leaves, features, skel_rank)), axis=2
    )
    send_points = skel_points[slot_leaf].reshape(devices, capacity, features, skel_rank)
    remote_points, codes = (
        lax.all_to_all(send_points, "leaf", split_axis=0, concat_axis=0, tiled=True),
        lax.all_to_all(target_code, "leaf", split_axis=0, concat_axis=0, tiled=True),
    )
    remote_points = remote_points.reshape(slot_total, features, skel_rank)
    target = codes.reshape(-1).astype(jnp.int32)
    leaf_ids = jnp.arange(leaves, dtype=jnp.int32)
    target_hot = (target[:, None] == leaf_ids[None, :]).astype(jnp.float32)
    target_leaf = jnp.clip(target, 0, leaves - 1)
    sender_hot = ((slot_leaf[:, None] == leaf_ids[None, :]) & filled[:, None]).astype(jnp.float32)
    projections = kernel_block(points, skel_points)
    self_skel = kernel_block(skel_points, skel_points)
    far_blocks = 8
    block_rows = slot_total // far_blocks

    def far_apply(values):
        coeffs = jnp.einsum("lns,ln->ls", projections, values, precision=HIGHEST)
        sent = coeffs[slot_leaf].reshape(devices, capacity, skel_rank)
        got = lax.all_to_all(sent, "leaf", split_axis=0, concat_axis=0, tiled=True).reshape(
            slot_total, skel_rank
        )
        mine = coeffs[target_leaf]

        def far_one_block(block):
            target_ids, remote, incoming_q, own_q = block
            tiles = kernel_block(skel_points[target_ids], remote)
            inward = jnp.einsum("smn,sn->sm", tiles, incoming_q, precision=HIGHEST)
            outward = jnp.einsum("smn,sm->sn", tiles, own_q, precision=HIGHEST)
            return (inward, outward)

        inward, outward = lax.map(
            far_one_block,
            (
                target_leaf.reshape(far_blocks, block_rows),
                remote_points.reshape(far_blocks, block_rows, features, skel_rank),
                got.reshape(far_blocks, block_rows, skel_rank),
                mine.reshape(far_blocks, block_rows, skel_rank),
            ),
        )
        back = lax.all_to_all(
            outward.reshape(devices, capacity, skel_rank),
            "leaf",
            split_axis=0,
            concat_axis=0,
            tiled=True,
        ).reshape(slot_total, skel_rank)
        gathered = jnp.einsum(
            "rl,rs->ls", target_hot, inward.reshape(slot_total, skel_rank), precision=HIGHEST
        )
        gathered = gathered + jnp.einsum("rl,rs->ls", sender_hot, back, precision=HIGHEST)
        gathered = gathered + jnp.einsum("lst,lt->ls", self_skel, coeffs, precision=HIGHEST)
        return jnp.einsum("lns,ls->ln", projections, gathered, precision=HIGHEST)

    flat_points = jnp.transpose(points, (1, 0, 2)).reshape(features, leaves * leaf_size)
    chosen_top = flat_points[:, top_index[0]]
    all_top = lax.all_gather(chosen_top[None], "leaf", axis=0, tiled=True)
    basis = kernel_block(flat_points, chosen_top)

    def top_apply(values):
        coarse = jnp.dot(values.reshape(-1), basis, precision=HIGHEST)
        piece = lax.all_gather(coarse[None], "leaf", axis=0, tiled=True)
        rows = piece.shape[0]
        tiles = kernel_block(jnp.broadcast_to(chosen_top, (rows, features, top_rank)), all_top)
        mixed = jnp.einsum("rmn,rn->m", tiles, piece, precision=HIGHEST)
        return jnp.dot(basis, mixed, precision=HIGHEST).reshape(leaves, leaf_size)

    def operate(values):
        return (
            values
            + 0.25 * near_apply(values)
            + 0.125 * far_apply(values)
            + 0.25 * top_apply(values)
        )

    def two_products(vector, image):
        return lax.psum((jnp.sum(vector * vector), jnp.sum(vector * image)), "leaf")

    solution_field = jnp.zeros_like(right_side)
    residual = right_side
    image = operate(residual)
    norm_now, product = two_products(residual, image)
    alpha = norm_now / product
    direction, along = (residual, image)
    for step in range(ITERS):
        solution_field = solution_field + alpha * direction
        residual = residual - alpha * along
        if step + 1 < ITERS:
            image = operate(residual)
            norm_next, product = two_products(residual, image)
            ratio = norm_next / norm_now
            alpha = norm_next / (product - ratio * norm_next / alpha)
            direction = residual + ratio * direction
            along = image + ratio * along
            norm_now = norm_next
    return (solution_field, residual)


def solution(mesh):
    in_specs = (
        P(("groups", "leaf"), None, None),
        P(("groups", "leaf"), None),
        P(("groups", "leaf"), None),
        P(("groups", "leaf"), None),
        P(("groups", "leaf"), None),
        P(("groups", "leaf"), None),
        P(("groups", "leaf"), None),
    )
    out_specs = (P(("groups", "leaf"), None), P(("groups", "leaf"), None))
    return jax.shard_map(
        on_device, mesh=mesh, in_specs=in_specs, out_specs=out_specs, check_vma=False
    )
```

profile of v0, /device:TPU:0, one launch (start us, length us, event | category | flops | bytes accessed | tf_op | source)
XLA Modules:
  0.0 1105.5 jit_solution(18212841420925934913)
XLA Ops:
  4.3 7.4 all-to-all-start
  13.3 4.3 collective-permute-start
  23.6 644.6 %gather_fusion.17 = f32[65536]{0:T(1024)S(1)} fusion(f32[8,64,256]{2,1,0:T(8,128)S(1)} %copy-done, s32[65536]{0:T(1024)S(1)} %bitcast.434), kind=kCustom, calls=%fused_computation.17 | custom fusion | bytes 1310720 | tf_op jit(solution)/shard_map/jit(take_along_axis)/gather | solution.py:91
  677.0 6.8 while.69
  688.6 4.1 all-to-all-start.2
  701.0 23.5 %all-gather = f32[1024,128]{1,0:T(8,128)S(1)} all-gather(f32[64,128]{1,0:T(8,128)} %copy.33), channel_id=2, replica_groups=mesh['groups'=2,'leaf'=16] {'leaf'}, dimensions={0}, use_global_device_ids=true | all-gather | bytes 557056 | tf_op jit(solution)/shard_map/all_gather | solution.py:150
  727.5 17.6 %all-gather.3 = f32[16,1,128]{2,1,0:T(1,128)S(1)} all-gather(f32[1,1,128]{2,1,0:T(1,128)S(1)} %convolution_bitcast_fusion.3), channel_id=3, replica_groups=mesh['groups'=2,'leaf'=16] {'leaf'}, dimensions={0}, use_global_device_ids=true | all-gather | bytes 8704 | tf_op jit(solution)/shard_map/all_gather | solution.py:155
  752.9 4.4 all-to-all-start.1
  757.4 37.7 %while.68 = (s32[]{:T(128)}, f32[8,2,256]{2,1,0:T(2,128)S(1)}, f32[8,2,256]{2,1,0:T(2,128)S(1)}, s32[8,2]{1,0:T(8,128)S(1)}, f32[10,64,256]{2,1,0:T(8,128)S(1)},...) while((s32[]{:T(128)}, f32[8,2,256]{2,1,0:T(2,128)S(1)}, f32[8,2,256]{2,1,0:T(2,128)S(1)}, ...), condition=%wide.region_5.6_spmd, body=%wide.region_2.5_spmd.sunk | while | flops 104465424 | bytes 2662577 | solution.py:60
  799.6 56.8 %while.70 = (s32[]{:T(128)}, f32[8,8,128]{2,1,0:T(8,128)}, f32[8,8,128]{2,1,0:T(8,128)}, s32[8,8]{1,0:T(8,128)}, f32[8,64,128]{2,1,0:T(8,128)S(1)}, /*index=5*/f...) while((s32[]{:T(128)}, f32[8,8,128]{2,1,0:T(8,128)}, ...), condition=%wide.region_17.18_spmd, body=%wide.region_14.17_spmd.sunk | while | flops 104594456 | bytes 3216621 | solution.py:125
  801.9 2.0 fusion.286
  809.0 2.0 fusion.286
  816.1 2.0 fusion.286
  823.2 2.0 fusion.286
  830.3 2.0 fusion.286
  837.4 2.0 fusion.286
  844.4 2.0 fusion.286
  851.5 2.0 fusion.286
  856.4 11.4 %all-to-all-start.3 = ((f32[16,4,128]{2,1,0:T(4,128)}), f32[16,4,128]{2,1,0:T(4,128)}, u32[]{:S(2)}, u32[]{:S(2)}) async-start(f32[16,4,128]{2,1,0:T(4,128)} %bitcast.75), calls=%async_computation.3 | async-start | bytes 65536 | tf_op jit(solution)/shard_map/all_to_all | solution.py:134
  869.4 5.1 all-to-all-done.3
  878.1 30.3 %all-reduce.3 = (f32[]{:T(128)}, f32[]{:T(128)}) all-reduce(f32[]{:T(128)} %get-tuple-element.221, f32[]{:T(128)} %get-tuple-element.220), channel_id=1, replica_groups=mesh['groups'=2,'leaf'=16] {'leaf'}, use_global_device_ids=true, to_apply=%region_1.0 | all-reduce | flops 2 | bytes 16 | tf_op jit(solution)/shard_map/psum | solution.py:170
  912.0 2.6 fusion.118
  915.9 4.2 all-to-all-start.4
  921.7 21.7 %all-gather.4 = f32[16,1,128]{2,1,0:T(1,128)S(1)} all-gather(f32[1,1,128]{2,1,0:T(1,128)S(1)} %convolution_bitcast_fusion.1), channel_id=4, replica_groups=mesh['groups'=2,'leaf'=16] {'leaf'}, dimensions={0}, use_global_device_ids=true | all-gather | bytes 8704 | tf_op jit(solution)/shard_map/all_gather | solution.py:155
  943.4 2.1 convolution_bitcast_fusion
  946.8 12.4 %while.72 = (s32[]{:T(128)}, f32[8,256]{1,0:T(8,128)S(1)}, f32[8,64,256]{2,1,0:T(8,128)S(1)}, f32[8,256]{1,0:T(8,128)}, s32[]{:T(128)}, /*index=5*/s32[]{:T(128)}) while((s32[]{:T(128)}, f32[8,256]{1,0:T(8,128)S(1)}, f32[8,64,256]{2,1,0:T(8,128)S(1)}, f32[8,256]{1,0:T(8,128)}, s32[]{:T(128)}, /*index=5*/s32[]{:T(128)}) %tuple.133), condition=%wide.region_31.32_spmd, body=%wide.region_29.31_spmd.sunk | while | flops 51412736 | bytes 663121 | solution.py:74
  960.6 37.7 %while.71 = (s32[]{:T(128)}, f32[8,2,256]{2,1,0:T(2,128)S(1)}, f32[8,2,256]{2,1,0:T(2,128)S(1)}, s32[8,2]{1,0:T(8,128)S(1)}, f32[10,64,256]{2,1,0:T(8,128)S(1)},...) while((s32[]{:T(128)}, f32[8,2,256]{2,1,0:T(2,128)S(1)}, f32[8,2,256]{2,1,0:T(2,128)S(1)}, ...), condition=%wide.region_28.29_spmd, body=%wide.region_25.28_spmd.sunk | while | flops 104465424 | bytes 2662577 | solution.py:60
  999.9 56.7 %while.73 = (s32[]{:T(128)}, f32[8,8,128]{2,1,0:T(8,128)S(1)}, f32[8,8,128]{2,1,0:T(8,128)}, s32[8,8]{1,0:T(8,128)}, f32[8,64,128]{2,1,0:T(8,128)S(1)}, /*index=...) while((s32[]{:T(128)}, f32[8,8,128]{2,1,0:T(8,128)S(1)}, ...), condition=%wide.region_35.36_spmd, body=%wide.region_32.35_spmd.sunk | while | flops 104594456 | bytes 3216621 | solution.py:125
  1044.7 2.0 fusion.314
  1056.6 5.5 all-to-all-start.5
  1062.4 6.4 all-to-all-done.5
  1070.3 30.3 %all-reduce.2 = (f32[]{:T(128)}, f32[]{:T(128)}) all-reduce(f32[]{:T(128)} %get-tuple-element.219, f32[]{:T(128)} %get-tuple-element.218), channel_id=1, replica_groups=mesh['groups'=2,'leaf'=16] {'leaf'}, use_global_device_ids=true, to_apply=%region_24.25 | all-reduce | flops 2 | bytes 16 | tf_op jit(solution)/shard_map/psum | solution.py:170
  (640 shorter events, 253.2 us)
Async XLA Ops:
  0.6 22.9 %copy-start.10 = (s32[8,128]{1,0:T(8,128)S(1)}, s32[8,128]{1,0:T(8,128)}, u32[]{:S(2)}) copy-start(s32[8,128]{1,0:T(8,128)} %param.24) | copy-start | bytes 12292
  4.3 684.3 %all-to-all-start = ((f32[16,1,4]{2,1,0:T(1,128)}), f32[16,1,4]{2,1,0:T(1,128)}, u32[]{:S(2)}, u32[]{:S(2)}) async-start(f32[16,1,4]{2,1,0:T(1,128)} %bitcast.63), calls=%async_computation | async-start | bytes 16384 | tf_op jit(solution)/shard_map/all_to_all | solution.py:97
  13.3 738.7 %collective-permute-start = (f32[2,64,256]{2,1,0:T(8,128)}, f32[2,64,256]{2,1,0:T(8,128)}, u32[]{:S(2)}, u32[]{:S(2)}) collective-permute-start(f32[2,64,256]{2,1,0:T(8,128)} %slice.21), channel_id=1, source_target_pairs={{1,0},{2,1},{3,2},{4,3},{5,4},{6,5},{7,6},{8,7},{9,8},{10,9},{11,1... | collective-permute-start | bytes 393224 | tf_op jit(solution)/shard_map/ppermute | solution.py:15
  18.9 732.4 %collective-permute-start.1 = (f32[2,256]{1,0:T(2,128)}, f32[2,256]{1,0:T(2,128)}, u32[]{:S(2)}, u32[]{:S(2)}) collective-permute-start(f32[2,256]{1,0:T(2,128)} %slice.22), channel_id=1, source_target_pairs={{1,0},{2,1},{3,2},{4,3},{5,4},{6,5},{7,6},{8,7},{9,8},{10,9},{11,1... | collective-permute-start | bytes 6152 | tf_op jit(solution)/shard_map/ppermute | solution.py:15
  688.6 64.3 %all-to-all-start.2 = ((f32[16,4,128]{2,1,0:T(4,128)}), f32[16,4,128]{2,1,0:T(4,128)}, u32[]{:S(2)}, u32[]{:S(2)}) async-start(f32[16,4,128]{2,1,0:T(4,128)} %bitcast.462), calls=%async_computation.2 | async-start | bytes 65536 | tf_op jit(solution)/shard_map/all_to_all | solution.py:113
  701.0 25.6 %copy-start.12 = (f32[1,1,8,256]{3,1,2,0:T(1,128)S(1)}, f32[1,1,8,256]{3,1,2,0:T(1,128)}, u32[]{:S(2)}) copy-start(f32[1,1,8,256]{3,1,2,0:T(1,128)} %copy.66) | copy-start | bytes 24580
  701.0 44.1 %copy-start.8 = (f32[64,128]{1,0:T(8,128)S(1)}, f32[64,128]{1,0:T(8,128)}, u32[]{:S(2)}) copy-start(f32[64,128]{1,0:T(8,128)} %copy.33) | copy-start | bytes 98308
  701.0 44.1 %copy-start.18 = (f32[128]{0:T(128)S(1)}, f32[128]{0:T(128)}, u32[]{:S(2)}) copy-start(f32[128]{0:T(128)} %multiply_reduce_fusion.10) | copy-start | bytes 1540
  726.6 22.1 %copy-start.1 = (f32[2048,128]{0,1:T(8,128)}, f32[2048,128]{0,1:T(8,128)S(1)}, u32[]{:S(2)}) copy-start(f32[2048,128]{0,1:T(8,128)S(1)} %fusion.65) | copy-start | bytes 3145732
  727.5 21.8 %copy-start.15 = (s32[16,4]{1,0:T(8,128)S(1)}, s32[16,4]{1,0:T(8,128)}, u32[]{:S(2)}) copy-start(s32[16,4]{1,0:T(8,128)} %get-tuple-element.223) | copy-start | bytes 772
  727.5 22.5 %copy-start.14 = (s32[16,4]{1,0:T(8,128)S(1)}, s32[16,4]{1,0:T(8,128)}, u32[]{:S(2)}) copy-start(s32[16,4]{1,0:T(8,128)} %get-tuple-element.222) | copy-start | bytes 772
  752.9 45.5 %all-to-all-start.1 = ((f32[16,4,64,128]{3,2,1,0:T(8,128)}), f32[16,4,64,128]{3,2,1,0:T(8,128)}, u32[]{:S(2)}, u32[]{:S(2)}) async-start(f32[16,4,64,128]{3,2,1,0:T(8,128)} %bitcast.439), calls=%async_computation.1 | async-start | bytes 4194304 | tf_op jit(solution)/shard_map/all_to_all | solution.py:96
  757.3 37.7 %copy-start.23 = (s32[16]{0:T(128)S(1)}, s32[16]{0:T(128)}, u32[]{:S(2)}) copy-start(s32[16]{0:T(128)} %copy-done.22) | copy-start | bytes 196
  757.4 37.7 %copy-start.26 = (f32[16]{0:T(128)S(1)}, f32[16]{0:T(128)}, u32[]{:S(2)}) copy-start(f32[16]{0:T(128)} %convert_element_type.54) | copy-start | bytes 196
  757.4 38.0 %copy-start.31 = (s32[16]{0:T(128)S(1)}, s32[16]{0:T(128)}, u32[]{:S(2)}) copy-start(s32[16]{0:T(128)} %add_add_fusion) | copy-start | bytes 196
  796.3 79.9 %collective-permute-start.2 = (f32[2,256]{1,0:T(2,128)}, f32[2,256]{1,0:T(2,128)}, u32[]{:S(2)}, u32[]{:S(2)}) collective-permute-start(f32[2,256]{1,0:T(2,128)} %slice.66), channel_id=1, source_target_pairs={{15,0},{0,1},{1,2},{2,3},{3,4},{4,5},{5,6},{6,7},{7,8},{8,9},{9,10... | collective-permute-start | bytes 6152 | tf_op jit(solution)/shard_map/ppermute | solution.py:15
  799.6 74.8 %copy-start.19 = (f32[8,1,128]{2,1,0:T(1,128)S(1)}, f32[8,1,128]{2,1,0:T(1,128)}, u32[]{:S(2)}) copy-start(f32[8,1,128]{2,1,0:T(1,128)} %fusion.120) | copy-start | bytes 12292
  856.4 64.4 %copy-start.2 = (f32[2048,128]{0,1:T(8,128)S(1)}, f32[2048,128]{0,1:T(8,128)}, u32[]{:S(2)}) copy-start(f32[2048,128]{0,1:T(8,128)} %copy-done.1) | copy-start | bytes 3145732
  856.4 18.1 %all-to-all-start.3 = ((f32[16,4,128]{2,1,0:T(4,128)}), f32[16,4,128]{2,1,0:T(4,128)}, u32[]{:S(2)}, u32[]{:S(2)}) async-start(f32[16,4,128]{2,1,0:T(4,128)} %bitcast.75), calls=%async_computation.3 | async-start | bytes 65536 | tf_op jit(solution)/shard_map/all_to_all | solution.py:134
  911.0 48.8 %collective-permute-start.3 = (f32[2,256]{1,0:T(2,128)}, f32[2,256]{1,0:T(2,128)}, u32[]{:S(2)}, u32[]{:S(2)}) collective-permute-start(f32[2,256]{1,0:T(2,128)} %slice.67), channel_id=1, source_target_pairs={{1,0},{2,1},{3,2},{4,3},{5,4},{6,5},{7,6},{8,7},{9,8},{10,9},{11,1... | collective-permute-start | bytes 6152 | tf_op jit(solution)/shard_map/ppermute | solution.py:15
  915.9 83.4 %all-to-all-start.4 = ((f32[16,4,128]{2,1,0:T(4,128)}), f32[16,4,128]{2,1,0:T(4,128)}, u32[]{:S(2)}, u32[]{:S(2)}) async-start(f32[16,4,128]{2,1,0:T(4,128)} %bitcast.461), calls=%async_computation.4 | async-start | bytes 65536 | tf_op jit(solution)/shard_map/all_to_all | solution.py:113
  960.6 37.7 %copy-start.24 = (s32[16]{0:T(128)S(1)}, s32[16]{0:T(128)}, u32[]{:S(2)}) copy-start(s32[16]{0:T(128)} %copy-done.22) | copy-start | bytes 196
  960.6 37.7 %copy-start.27 = (f32[16]{0:T(128)S(1)}, f32[16]{0:T(128)}, u32[]{:S(2)}) copy-start(f32[16]{0:T(128)} %convert_element_type.54) | copy-start | bytes 196
  960.6 38.0 %copy-start.32 = (s32[16]{0:T(128)S(1)}, s32[16]{0:T(128)}, u32[]{:S(2)}) copy-start(s32[16]{0:T(128)} %add_add_fusion) | copy-start | bytes 196
  998.9 70.8 %collective-permute-start.4 = (f32[2,256]{1,0:T(2,128)S(1)}, f32[2,256]{1,0:T(2,128)S(1)}, u32[]{:S(2)}, u32[]{:S(2)}) collective-permute-start(f32[2,256]{1,0:T(2,128)S(1)} %slice.69), channel_id=1, source_target_pairs={{15,0},{0,1},{1,2},{2,3},{3,4},{4,5},{5,6},{6,7},{7,8},{8,9},{9,10... | collective-permute-start | bytes 6152 | tf_op jit(solution)/shard_map/ppermute | solution.py:15
  999.9 62.2 %copy-start.25 = (s32[64]{0:T(128)S(1)}, s32[64]{0:T(128)}, u32[]{:S(2)}) copy-start(s32[64]{0:T(128)} %convert_element_type.59) | copy-start | bytes 772
  999.9 68.9 %copy-start.20 = (f32[8,1,128]{2,1,0:T(1,128)S(1)}, f32[8,1,128]{2,1,0:T(1,128)}, u32[]{:S(2)}) copy-start(f32[8,1,128]{2,1,0:T(1,128)} %fusion.118) | copy-start | bytes 12292
  999.9 68.9 %copy-start.30 = (pred[64]{0:T(512)(128)(4,1)S(1)}, pred[64]{0:T(512)(128)(4,1)}, u32[]{:S(2)}) copy-start(pred[64]{0:T(512)(128)(4,1)} %copy-done.29) | copy-start | bytes 196
  999.9 68.9 %copy-start.33 = (s32[64]{0:T(128)S(1)}, s32[64]{0:T(128)}, u32[]{:S(2)}) copy-start(s32[64]{0:T(128)} %and_select_fusion) | copy-start | bytes 772
  999.9 69.8 %copy-start.7 = (f32[8,256]{1,0:T(8,128)S(1)}, f32[8,256]{1,0:T(8,128)}, u32[]{:S(2)}) copy-start(f32[8,256]{1,0:T(8,128)} %get-tuple-element.719) | copy-start | bytes 24580
  999.9 105.0 %copy-start.9 = (f32[8,256]{1,0:T(8,128)S(1)}, f32[8,256]{1,0:T(8,128)}, u32[]{:S(2)}) copy-start(f32[8,256]{1,0:T(8,128)} %get-tuple-element.305) | copy-start | bytes 24580
  1056.6 12.2 %all-to-all-start.5 = ((f32[16,4,128]{2,1,0:T(4,128)}), f32[16,4,128]{2,1,0:T(4,128)S(1)}, u32[]{:S(2)}, u32[]{:S(2)}) async-start(f32[16,4,128]{2,1,0:T(4,128)} %bitcast.106), calls=%async_computation.5 | async-start | bytes 65536 | tf_op jit(solution)/shard_map/all_to_all | solution.py:134
  (13 other events, 92.8 us)
where the time goes:
time: 1110 us
  local copies, waits for them, and re-layouts  738 us (66%)
  matrix products  124 us (11%)
  blocking collectives  123 us (11%)
  other arithmetic  56.5 us (5%)
  starting transfers between devices  42.3 us (4%)
  waiting for transfers between devices  13.3 us (1%)
    gather x1, local copies, waits for them, and re-layouts, on_device(): jnp.take_along_axis(points, jnp.broadcast_to(skeleton[:, None, :], (leave...  645 us
    psum x2, blocking collectives, two_products(): return lax.psum((jnp.sum(vector * vector), jnp.sum(vector * image)), 'leaf')  60.6 us
    dot_general x52, matrix products, kernel_block(): jnp.einsum('...dm,...dn->...mn', first_set, second_set, precision=HIGHEST)  56.9 us
    all_gather x2, blocking collectives, top_apply(): piece = lax.all_gather(coarse[None], 'leaf', axis=0, tiled=True)  39.4 us
    all_gather x1, blocking collectives, on_device(): all_top = lax.all_gather(chosen_top[None], 'leaf', axis=0, tiled=True)  23.5 us
  transfers between devices with their start and end apart: 11, of which 3 were waited for; matrix products, arithmetic and copies ran while one was open for 82% of the time, Pallas kernels for 0%

commit v1 on v0

v1 whole, which is shorter than its diff:
```python
import functools
import math

import jax
import jax.numpy as jnp
from jax import lax
from jax.experimental import pallas as pl
from jax.experimental.pallas import tpu as pltpu
from jax.sharding import PartitionSpec as P

F32 = jnp.float32
BF16 = jnp.bfloat16
VMEM_LIMIT = 48 * 1024 * 1024
UNROLL = 4


def contract_first(left, right):
    return lax.dot_general(left, right, (((0,), (0,)), ((), ())), preferred_element_type=F32)


def halves(x):
    high = x.astype(BF16)
    return high, (x - high.astype(F32)).astype(BF16)


def thirds(x):
    high = x.astype(BF16)
    rest = x - high.astype(F32)
    middle = rest.astype(BF16)
    return high, middle, (rest - middle.astype(F32)).astype(BF16)


def norm_rows(x, factor, first):
    norm = jnp.sum(x * x, axis=0, keepdims=True) * factor
    high, middle, low = [piece.astype(F32) for piece in thirds(norm)]
    row = lax.broadcasted_iota(jnp.int32, (16, x.shape[1]), 0)
    rows = jnp.where(row < 6, 1.0, 0.0)
    for place, piece in ((first, high), (first + 1, middle), (first + 2, low)):
        rows = jnp.where(row == place, piece, rows)
    return rows.astype(BF16)


def unit(features):
    return 2.0 / features * math.log2(math.e)


def right_form(x):
    high, low = halves(x)
    return jnp.concatenate([high, high, low, norm_rows(x, -unit(x.shape[0]), 0)], axis=0)


def left_form(x):
    high, low = halves(x * (2.0 * unit(x.shape[0])))
    return jnp.concatenate([high, low, high, norm_rows(x, -unit(x.shape[0]), 3)], axis=0)


def tile_of(left, right):
    return jnp.exp2(contract_first(left, right))


def folded(tile, row):
    total = tile[:, :128] * row[:, :128]
    for start in range(128, tile.shape[1], 128):
        total = total + tile[:, start:start + 128] * row[:, start:start + 128]
    return total


def as_row(matrix):
    return jnp.sum(matrix.T, axis=0, keepdims=True)


def down(row):
    return jnp.broadcast_to(row, (128, row.shape[1])).T


def wide(column_matrix, columns):
    return jnp.concatenate([column_matrix] * (columns // 128), axis=1)


def prepare_kernel(points, values, mask, skeleton, top, piece, to_skel, to_top, lefts, first, last, rights):
    leaves, features, size = points.shape
    reach = first.shape[0]
    rank = skeleton.shape[1]
    pad = first.shape[1] - features - 1 - reach
    for r in range(reach):
        first[r, :features, :] = points[r]
        last[r, :features, :] = points[leaves - reach + r]
        first[r, features:, :] = jnp.broadcast_to(values[r:r + 1, :], (first.shape[1] - features, size))
        own = leaves - reach + r
        rows = [values[own:own + 1, :]]
        rows += [jnp.full((1, size), mask[own, s].astype(F32)) for s in range(reach)]
        last[r, features:, :] = jnp.concatenate(rows + [jnp.zeros((pad, size), F32)], axis=0)
    top_total = jnp.zeros((3 * features, rank), F32)
    spot = lax.broadcasted_iota(jnp.int32, (size, rank), 0)
    for l in range(leaves):
        x = points[l]
        chosen = jnp.concatenate(
            [spot == skeleton[l:l + 1, :], spot == top[...] - l * size], axis=1
        )
        picked = jnp.dot(
            jnp.concatenate(thirds(x), axis=0),
            jnp.where(chosen, 1.0, 0.0).astype(BF16),
            preferred_element_type=F32,
        )
        skel = picked[:, :rank]
        skel = skel[:features] + skel[features:2 * features] + skel[2 * features:]
        piece[l * features:(l + 1) * features, :] = skel
        lefts[l] = left_form(skel)
        rights[l] = right_form(x)
        top_total = top_total + picked[:, rank:]
    chosen_top = top_total[:features] + top_total[features:2 * features] + top_total[2 * features:]
    piece[leaves * features:(leaves + 1) * features, :] = chosen_top
    lefts[leaves] = left_form(chosen_top)
    coarse = jnp.zeros((rank, 128), F32)
    for l in range(leaves):
        both = tile_of(jnp.concatenate([lefts[l], lefts[leaves]], axis=1), rights[l])
        to_skel[l] = both[:rank]
        to_top[l] = both[rank:]
        row = values[l:l + 1, :]
        piece[(leaves + 1) * features + l:(leaves + 1) * features + l + 1, :] = as_row(
            folded(both[:rank], row)
        )
        coarse = coarse + folded(both[rank:], row)
    base = (leaves + 1) * features + leaves
    piece[base:base + 8, :] = jnp.broadcast_to(as_row(coarse), (8, rank))


def near_kernel(packed, points, values, mask, following, preceding, value_next, value_prev, out, lefts, rights, downs, across, along):
    leaves, features, size = points.shape
    reach = following.shape[0]

    def block(e):
        if e < reach:
            return preceding[e, :features, :]
        if e < reach + leaves:
            return points[e - reach]
        return following[e - reach - leaves, :features, :]

    def row_of(e):
        if reach <= e < reach + leaves:
            return values[e - reach:e - reach + 1, :]
        place = e if e < reach else e - reach - leaves
        if packed:
            return (preceding if e < reach else following)[place, features:features + 1, :]
        return (value_prev if e < reach else value_next)[place:place + 1, :]

    for e in range(leaves + 2 * reach):
        x = block(e)
        if e < leaves + reach:
            lefts[e] = left_form(x)
            downs[e] = down(row_of(e))
        if e >= reach:
            rights[e] = right_form(x)

    def backward(tile, a):
        product = tile * wide(downs[a], size)
        return jnp.sum(product.reshape(size // 8, 8, size), axis=0)

    for l in range(leaves):
        e = l + reach
        along[l] = backward(tile_of(lefts[e], rights[e]), e)
        across[l] = jnp.zeros((size, 128), F32)
    for a in range(leaves + reach):
        for r in range(reach):
            b = a + 1 + r
            own_a, own_b = reach <= a, reach <= b < reach + leaves
            if own_a:
                @pl.when(mask[a - reach, r] != 0)
                def _(a=a, b=b, own_b=own_b):
                    tile = tile_of(lefts[a], rights[b])
                    across[a - reach] += folded(tile, row_of(b))
                    if own_b:
                        along[b - reach] += backward(tile, a)
            elif own_b:
                weight = preceding[a, features + 1 + r:features + 2 + r, :]
                along[b - reach] += weight * backward(tile_of(lefts[a], rights[b]), a)
    for l in range(leaves):
        out[l:l + 1, :] = as_row(across[l]) + jnp.sum(along[l], axis=0, keepdims=True)


def make_list(axis, leaves, fan_out, dest, leaf, targets, sources, count):
    me = lax.axis_index(axis)
    mine = leaves * fan_out

    def clear(n, carry):
        targets[n] = leaves
        sources[n] = 0
        return carry

    lax.fori_loop(0, targets.shape[0], clear, 0)

    def own(n, carry):
        targets[n] = n // fan_out
        sources[n] = dest[me * mine + n] * leaves + leaf[me * mine + n]
        return carry

    lax.fori_loop(0, mine, own, 0)

    def itself(n, carry):
        targets[mine + n] = n
        sources[mine + n] = me * leaves + n
        return carry

    lax.fori_loop(0, leaves, itself, 0)

    def received(n, filled):
        here = dest[n] == me

        @pl.when(here)
        def _():
            targets[filled] = leaf[n]
            sources[filled] = n // fan_out

        return filled + here.astype(jnp.int32)

    count[0] = lax.fori_loop(0, dest.shape[0], received, mine + leaves)


def far_and_top(targets, sources, count, gathered, coefficients, lefts, to_skel, to_top, sums):
    leaves, rank, size = to_skel.shape
    features = (gathered.shape[1] - 16) // (leaves + 1)
    rows = coefficients.shape[1] - 16
    devices = gathered.shape[0]
    sums[...] = jnp.zeros_like(sums)

    def step(g, carry):
        found = []
        for k in range(UNROLL):
            n = g * UNROLL + k
            target, source = targets[n], sources[n]
            device, place = source // leaves, source % leaves
            start = pl.multiple_of(place * features, features)
            tile = tile_of(lefts[target], right_form(gathered[device, pl.ds(start, features), :]))
            found.append((target, tile * coefficients[device, pl.ds(rows + place, 1), :]))
        for target, product in found:
            sums[target] += product
        return carry

    lax.fori_loop(0, (count[0] + UNROLL - 1) // UNROLL, step, 0)

    def top_step(e, total):
        tile = tile_of(lefts[leaves], right_form(gathered[e, leaves * features:(leaves + 1) * features, :]))
        return total + tile * coefficients[e, rows + leaves:rows + leaves + 1, :]

    mixed = lax.fori_loop(0, devices, top_step, jnp.zeros((rank, rank), F32), unroll=4)
    mixed = jnp.sum(mixed, axis=1, keepdims=True)
    far, top = [], []
    for l in range(leaves):
        far.append(jnp.sum(to_skel[l] * jnp.sum(sums[l], axis=1, keepdims=True), axis=0, keepdims=True))
        top.append(jnp.sum(to_top[l] * mixed, axis=0, keepdims=True))
    return jnp.concatenate(far, axis=0), jnp.concatenate(top, axis=0)


def total_of(x):
    return jnp.sum(jnp.sum(x, axis=1, keepdims=True), axis=0, keepdims=True)


def in_lanes(*numbers):
    lane = lax.broadcasted_iota(jnp.int32, (1, 128), 1)
    row = jnp.zeros((1, 128), F32)
    for place, number in enumerate(numbers):
        row = jnp.where(lane == place, number, row)
    return row


def first_kernel(targets, sources, count, gathered, lefts, to_skel, to_top, values, near, image, head, tail, payload, sums):
    leaves, rank, size = to_skel.shape
    reach = head.shape[0]
    far, top = far_and_top(
        targets, sources, count, gathered, gathered, lefts, to_skel, to_top, sums
    )
    start = values[...]
    result = start + 0.25 * near[...] + 0.125 * far + 0.25 * top
    image[...] = result
    head[...] = result[:reach]
    tail[...] = result[leaves - reach:]
    coarse = jnp.zeros((rank, 128), F32)
    rows = []
    for l in range(leaves):
        row = result[l:l + 1, :]
        rows.append(as_row(folded(to_skel[l], row)))
        coarse = coarse + folded(to_top[l], row)
    rows.append(as_row(coarse))
    rows.append(in_lanes(total_of(start * start), total_of(start * result)))
    rows.append(jnp.zeros((16 - leaves - 2, 128), F32))
    payload[...] = jnp.concatenate(rows, axis=0)


def second_kernel(targets, sources, count, gathered, everyone, lefts, to_skel, to_top, values, image, near, residual, along, numbers, sums):
    leaves = to_skel.shape[0]
    far, top = far_and_top(
        targets, sources, count, gathered, everyone, lefts, to_skel, to_top, sums
    )
    start, first = values[...], image[...]
    second = first + 0.25 * near[...] + 0.125 * far + 0.25 * top
    scalars = jnp.sum(everyone[:, leaves + 1, :], axis=0, keepdims=True)
    norm, product = scalars[:, 0:1], scalars[:, 1:2]
    alpha = norm / product
    left = start - alpha * first
    image_left = first - alpha * second
    residual[...] = left
    along[...] = image_left
    row = in_lanes(total_of(left * left), total_of(left * image_left), norm, alpha)
    numbers[...] = jnp.broadcast_to(row, numbers.shape)


def last_kernel(everyone, numbers, values, image, residual, along, solution_field, final):
    scalars = jnp.sum(everyone[:, 0, :], axis=0, keepdims=True)
    norm_next, product = scalars[:, 0:1], scalars[:, 1:2]
    norm, alpha = numbers[0:1, 2:3], numbers[0:1, 3:4]
    ratio = norm_next / norm
    step = norm_next / (product - ratio * norm_next / alpha)
    start, left = values[...], residual[...]
    solution_field[...] = alpha * start + step * (left + ratio * start)
    final[...] = left - step * (along[...] + ratio * image[...])


def shape(*dims, dtype=F32):
    return jax.ShapeDtypeStruct(dims, dtype)


SMEM = pl.BlockSpec(memory_space=pltpu.SMEM)
VMEM = pl.BlockSpec(memory_space=pltpu.VMEM)


def kernel_call(body, name, inputs, outputs, scratch=()):
    out_specs, out_shapes = zip(*outputs)
    return pl.pallas_call(
        body,
        in_specs=list(inputs),
        out_specs=list(out_specs),
        out_shape=list(out_shapes),
        scratch_shapes=list(scratch),
        compiler_params=pltpu.CompilerParams(vmem_limit_bytes=VMEM_LIMIT),
        name=name,
    )


def passed_along(block, axis, distance):
    size = lax.axis_size(axis)
    return lax.ppermute(block, axis, [((i - distance) % size, i) for i in range(size)])


def everyones(block, axis):
    size = lax.axis_size(axis)
    return lax.all_to_all(
        jnp.broadcast_to(block[None], (size,) + block.shape), axis, split_axis=0, concat_axis=0, tiled=True
    )


def on_device(points, right_side, near_mask, far_dest, far_leaf, skeleton, top_index):
    leaves, features, size = points.shape
    reach = near_mask.shape[1]
    fan_out = far_dest.shape[1]
    rank = skeleton.shape[1]
    devices = lax.axis_size("leaf")
    capacity = max(2, (2 * leaves * fan_out + devices - 1) // devices)
    depth = 3 * features + 16
    piece_rows = (leaves + 1) * features + 16
    halo_rows = features + 8

    piece, to_skel, to_top, lefts, first, last = kernel_call(
        prepare_kernel,
        "prepare",
        [VMEM, VMEM, SMEM, VMEM, VMEM],
        [
            (VMEM, shape(piece_rows, rank)),
            (VMEM, shape(leaves, rank, size)),
            (VMEM, shape(leaves, rank, size)),
            (VMEM, shape(leaves + 1, depth, rank, dtype=BF16)),
            (VMEM, shape(reach, halo_rows, size)),
            (VMEM, shape(reach, halo_rows, size)),
        ],
        [pltpu.VMEM((leaves, depth, size), BF16)],
    )(points, right_side, near_mask, skeleton, top_index)

    gathered = lax.all_gather(piece[None], "leaf", axis=0, tiled=True)
    following = passed_along(first, "leaf", -1)
    preceding = passed_along(last, "leaf", 1)
    lists = everyones(jnp.stack([far_dest.reshape(-1), far_leaf.reshape(-1)]), "leaf")
    lists = lists.reshape(devices, 2, leaves * fan_out)

    most = leaves * fan_out + leaves + capacity * devices
    most = -(-most // UNROLL) * UNROLL
    targets, sources, count = kernel_call(
        functools.partial(make_list, "leaf", leaves, fan_out),
        "far_list",
        [SMEM, SMEM],
        [
            (SMEM, shape(most, dtype=jnp.int32)),
            (SMEM, shape(most, dtype=jnp.int32)),
            (SMEM, shape(1, dtype=jnp.int32)),
        ],
    )(lists[:, 0].reshape(-1), lists[:, 1].reshape(-1))

    def near_apply(packed, values, value_next, value_prev):
        return kernel_call(
            functools.partial(near_kernel, packed),
            "near_first" if packed else "near_second",
            [VMEM, VMEM, SMEM, VMEM, VMEM, VMEM, VMEM],
            [(VMEM, shape(leaves, size))],
            [
                pltpu.VMEM((leaves + reach, depth, size), BF16),
                pltpu.VMEM((leaves + 2 * reach, depth, size), BF16),
                pltpu.VMEM((leaves + reach, size, 128), F32),
                pltpu.VMEM((leaves, size, 128), F32),
                pltpu.VMEM((leaves, 8, size), F32),
            ],
        )(points, values, near_mask, following, preceding, value_next, value_prev)[0]

    near = near_apply(True, right_side, right_side[:reach], right_side[:reach])
    sums = pltpu.VMEM((leaves + 1, rank, rank), F32)
    image, head, tail, payload = kernel_call(
        first_kernel,
        "far_first",
        [SMEM, SMEM, SMEM, VMEM, VMEM, VMEM, VMEM, VMEM, VMEM],
        [
            (VMEM, shape(leaves, size)),
            (VMEM, shape(reach, size)),
            (VMEM, shape(reach, size)),
            (VMEM, shape(16, rank)),
        ],
        [sums],
    )(targets, sources, count, gathered, lefts, to_skel, to_top, right_side, near)

    value_next = passed_along(head, "leaf", -1)
    value_prev = passed_along(tail, "leaf", 1)
    everyone = everyones(payload, "leaf").reshape(devices, 16, rank)
    near = near_apply(False, image, value_next, value_prev)
    residual, along, numbers = kernel_call(
        second_kernel,
        "far_second",
        [SMEM, SMEM, SMEM] + [VMEM] * 8,
        [
            (VMEM, shape(leaves, size)),
            (VMEM, shape(leaves, size)),
            (VMEM, shape(8, 128)),
        ],
        [sums],
    )(targets, sources, count, gathered, everyone, lefts, to_skel, to_top, right_side, image, near)

    scalars = everyones(numbers, "leaf").reshape(devices, 8, 128)
    solution_field, final = kernel_call(
        last_kernel,
        "finish",
        [VMEM] * 6,
        [(VMEM, shape(leaves, size)), (VMEM, shape(leaves, size))],
    )(scalars, numbers, right_side, image, residual, along)
    return solution_field, final


def solution(mesh):
    rows = P(("groups", "leaf"), None)
    in_specs = (P(("groups", "leaf"), None, None),) + (rows,) * 6
    return jax.shard_map(
        on_device, mesh=mesh, in_specs=in_specs, out_specs=(rows, rows), check_vma=False
    )
```

time: 1110 us -> 130 us (0.12)
  local copies, waits for them, and re-layouts: 738 us -> 11.6 us
  matrix products: 124 us -> 0 us
  blocking collectives: 123 us -> 9.48 us
  other arithmetic: 56.5 us -> 0.01 us
  Pallas kernels: 0 us -> 40.3 us
  starting transfers between devices: 42.3 us -> 19.4 us
  waiting for transfers between devices: 13.3 us -> 33.2 us
    gather x89 -> x0, local copies, waits for them, and re-layouts: 699 us -> none  [the longest x1 645 us: on_device(): jnp.take_along_axis(points, jnp.broadcast_to(skeleton[:, None, :], (leave...]
    dot_general x152 -> x0, matrix products: 124 us -> none  [the longest x52 56.9 us: kernel_block(): jnp.einsum('...dm,...dn->...mn', first_set, second_set, precision=HIGHEST)]
    all_gather x3 -> x0, blocking collectives: 62.9 us -> none  [the longest x2 39.4 us: top_apply(): piece = lax.all_gather(coarse[None], 'leaf', axis=0, tiled=True)]
    psum x2 -> x0, blocking collectives: 60.6 us -> none  [two_products(): return lax.psum((jnp.sum(vector * vector), jnp.sum(vector * image)), 'leaf')]
    pallas_call x0 -> x7, Pallas kernels: none -> 40.3 us  [the longest x1 10 us: on_device(): kernel_call(first_kernel, 'far_first', [SMEM, SMEM, SMEM, VMEM, VMEM, VME...]
    all_to_all x6 -> x2, starting transfers between devices: 37.1 us -> 9.43 us  [everyones(): lax.all_to_all(jnp.broadcast_to(block[None], (size,) + block.shape), axis...]
    select_n x52 -> x0, other arithmetic: 23.3 us -> none  [the longest x32 11.4 us: near_one_block(): tiles = kernel_block(extended[first_ids], extended[second_ids])]
    reduce_sum x88 -> x0, other arithmetic: 22.7 us -> none  [the longest x35 17.8 us: kernel_block(): second_sq = jnp.sum(second_set * second_set, axis=-2)]
  transfers between devices with their start and end apart: 11 -> 7, of which waited for: 3 -> 4; matrix products, arithmetic and copies ran while one was open for 82% -> 2% of each run, Pallas kernels for 0% -> 13%
where the time goes in v1:
time: 130 us; the launch traced here: 128 us
  Pallas kernels  40.3 us (31%)
  waiting for transfers between devices  33.2 us (26%)
  starting transfers between devices  19.4 us (15%)
  between operations  14.2 us (11%)
  local copies, waits for them, and re-layouts  11.6 us (9%)
  blocking collectives  9.48 us (7%)
    all_gather x1, waiting for transfers between devices, on_device(): gathered = lax.all_gather(piece[None], 'leaf', axis=0, tiled=True)  21.4 us
    pallas_call x1, Pallas kernels, on_device(): kernel_call(first_kernel, 'far_first', [SMEM, SMEM, SMEM, VMEM, VMEM, VME...  10 us
    ppermute x4, starting transfers between devices, passed_along(): lax.ppermute(block, axis, [((i - distance) % size, i) for i in range(size)])  9.88 us
    pallas_call x1, Pallas kernels, on_device(): kernel_call(second_kernel, 'far_second', [SMEM, SMEM, SMEM] + [VMEM] * 8,...  9.87 us
    all_to_all x1, blocking collectives, everyones(): lax.all_to_all(jnp.broadcast_to(block[None], (size,) + block.shape), axis...  9.48 us
    all_to_all x2, starting transfers between devices, everyones(): lax.all_to_all(jnp.broadcast_to(block[None], (size,) + block.shape), axis...  9.43 us
    unnamed x29, local copies, waits for them, and re-layouts  9.22 us
    pallas_call x1, Pallas kernels, on_device(): kernel_call(functools.partial(make_list, 'leaf', leaves, fan_out), 'far_l...  9.06 us
  transfers between devices with their start and end apart: 7, of which 4 were waited for; matrix products, arithmetic and copies ran while one was open for 2% of the time, Pallas kernels for 13%

profile of v1, /device:TPU:0, one launch (start us, length us, event | category | flops | bytes accessed | tf_op | source)
XLA Modules:
  0.0 128.1 jit_solution(12651348405168932575)
XLA Ops:
  7.2 0.8 copy.16.mask
  8.0 1.0 copy-done
  9.0 0.7 copy-done.3
  9.7 0.7 copy-done.7
  10.4 0.7 copy-done.12
  11.0 2.5 %prepare.1 = (f32[592,128]{1,0:T(8,128)}, f32[8,128,256]{2,1,0:T(8,128)S(1)}, f32[8,128,256]{2,1,0:T(8,128)S(1)}, bf16[9,208,128]{2,1,0:T(8,128)(2,1)S(1)}, f32[...) custom-call(f32[8,64,256]{2,1,0:T(8,128)S(1)} %copy-done, f32[8,256]{1,0:T(8,128)S(1)} %copy-done.3, s32[8,2]{1,0:T(8,128)S(1)} %copy.16.mask, ...), custom_call_target="tpu_custom_call" | custom-call | tf_op jit(solution)/shard_map/prepare/pallas_call | solution.py:362
  13.6 5.5 %collective-permute-start = (f32[2,72,256]{2,1,0:T(8,128)}, f32[2,72,256]{2,1,0:T(8,128)S(1)}, u32[]{:S(2)}, u32[]{:S(2)}) collective-permute-start(f32[2,72,256]{2,1,0:T(8,128)} %get-tuple-element.25), channel_id=1, source_target_pairs={{1,0},{2,1},{3,2},{4,3},{5,4},{6,5},{7,6},{8,7},{9,8},{10,9},{11,1... | collective-permute-start | bytes 442376 | tf_op jit(solution)/shard_map/ppermute | solution.py:341
  19.1 0.8 copy.15
  19.9 0.8 copy.14
  20.7 0.1 stack_reshape.6
  20.8 0.6 broadcast_in_dim.8
  21.4 5.8 %all-to-all-start = ((s32[16,2,32]{2,1,0:T(2,128)}), s32[16,2,32]{2,1,0:T(2,128)S(1)}, u32[]{:S(2)}, u32[]{:S(2)}) async-start(s32[16,2,32]{2,1,0:T(2,128)} %broadcast_in_dim.8), calls=%async_computation | async-start | bytes 32768 | tf_op jit(solution)/shard_map/all_to_all | solution.py:346
  27.2 0.7 slice.12.value_next.value_prev
  27.9 6.0 %all-to-all-done = s32[16,2,32]{2,1,0:T(2,128)S(1)} async-done(((s32[16,2,32]{2,1,0:T(2,128)}), s32[16,2,32]{2,1,0:T(2,128)S(1)}, u32[]{:S(2)}, u32[]{:S(2)}) %all-to-all-start) | async-done | bytes 4128 | tf_op jit(solution)/shard_map/all_to_all | solution.py:346
  34.2 9.1 %far_list.1 = (s32[104]{0:T(128)S(1)}, s32[104]{0:T(128)S(1)}, s32[1]{0:T(128)}) custom-call(s32[512]{0:T(512)S(1)} %reshape_squeeze.6.dest, s32[512]{0:T(512)S(1)} %reshape_squeeze.7.leaf), custom_call_target="tpu_custom_call" | custom-call | tf_op jit(solution)/shard_map/far_list/pallas_call | solution.py:385
  43.3 1.2 copy-done.1
  44.5 0.7 copy-done.4
  45.2 4.0 %near_first.1.near = f32[8,256]{1,0:T(8,128)S(1)} custom-call(f32[8,64,256]{2,1,0:T(8,128)S(1)} %copy-done.1, f32[8,256]{1,0:T(8,128)S(1)} %copy-done.4, s32[8,2]{1,0:T(8,128)S(1)} %copy.16.mask, f32[2,72,256]{2,1,0:T(8,128)S(1)} %collective-permute-done.following, f32[2,72,256]{2,1,0:T(8,128)S(1)} %collective-permute-done.1.preceding, ...), custom_call_target="tpu_custom_call" | custom-call | tf_op jit(solution)/shard_map/near_first/pallas_call | solution.py:397
  49.2 21.4 %all-gather.3.cloned.1.call-done = f32[9472,128]{1,0:T(8,128)} async-done(((f32[592,128]{1,0:T(8,128)}), f32[9472,128]{1,0:T(8,128)}) %all-gather.3.cloned.1.call-update) | async-done | bytes 4849680 | tf_op jit(solution)/shard_map/all_gather | solution.py:377
  70.6 0.7 copy-done.5
  71.3 10.0 %far_first.1 = (f32[8,256]{1,0:T(8,128)S(1)}, f32[2,256]{1,0:T(2,128)S(1)}, f32[2,256]{1,0:T(2,128)S(1)}, f32[16,128]{1,0:T(8,128)S(1)}) custom-call(s32[104]{0:T(128)S(1)} %get-tuple-element.18.targets, s32[104]{0:T(128)S(1)} %get-tuple-element.19.sources, s32[1]{0:T(128)} %get-tuple-element.20.count, f32[16,592,128]{2,1,0:T(8,128)} %bitcast.1, ...), custom_call_target="tpu_custom_call" | custom-call | tf_op jit(solution)/shard_map/far_first/pallas_call | solution.py:413
  81.3 0.7 broadcast_in_dim.10
  82.0 3.6 %all-to-all-start.1 = ((f32[16,16,128]{2,1,0:T(8,128)}), f32[16,16,128]{2,1,0:T(8,128)S(1)}, u32[]{:S(2)}, u32[]{:S(2)}) async-start(f32[16,16,128]{2,1,0:T(8,128)} %broadcast_in_dim.10), calls=%async_computation.1 | async-start | bytes 262144 | tf_op jit(solution)/shard_map/all_to_all | solution.py:346
  85.6 4.4 %collective-permute-start.2 = (f32[2,256]{1,0:T(2,128)S(1)}, f32[2,256]{1,0:T(2,128)S(1)}, u32[]{:S(2)}, u32[]{:S(2)}) collective-permute-start(f32[2,256]{1,0:T(2,128)S(1)} %get-tuple-element.29), channel_id=1, source_target_pairs={{1,0},{2,1},{3,2},{4,3},{5,4},{6,5},{7,6},{8,7},{9,8},{10,9},{11,1... | collective-permute-start | bytes 6152 | tf_op jit(solution)/shard_map/ppermute | solution.py:341
  90.0 1.3 %collective-permute-done.2.value_next = f32[2,256]{1,0:T(2,128)S(1)} collective-permute-done((f32[2,256]{1,0:T(2,128)S(1)}, f32[2,256]{1,0:T(2,128)S(1)}, u32[]{:S(2)}, u32[]{:S(2)}) %collective-permute-start.2) | collective-permute-done | bytes 2080 | tf_op jit(solution)/shard_map/ppermute | solution.py:341
  91.3 4.4 %collective-permute-done.3.value_prev = f32[2,256]{1,0:T(2,128)S(1)} collective-permute-done((f32[2,256]{1,0:T(2,128)S(1)}, f32[2,256]{1,0:T(2,128)S(1)}, u32[]{:S(2)}, u32[]{:S(2)}) %collective-permute-start.3) | collective-permute-done | bytes 2080 | tf_op jit(solution)/shard_map/ppermute | solution.py:341
  95.7 4.0 %near_second.1.near = f32[8,256]{1,0:T(8,128)S(1)} custom-call(f32[8,64,256]{2,1,0:T(8,128)S(1)} %copy-done.2, f32[8,256]{1,0:T(8,128)S(1)} %get-tuple-element.28.values.image, s32[8,2]{1,0:T(8,128)S(1)} %copy.16.mask, f32[2,72,256]{2,1,0:T(8,128)S(1)} %collective-permute-done.following, f32[2,72,256]{2,1,0:T(8,128)S(1)} %collective-permute-done.1.preceding, ...), custom_call_target="tpu_custom_call" | custom-call | tf_op jit(solution)/shard_map/near_second/pallas_call | solution.py:397
  99.7 0.6 copy-done.9
  100.4 0.6 copy-done.11
  101.0 9.9 %far_second.1 = (f32[8,256]{1,0:T(8,128)S(1)}, f32[8,256]{1,0:T(8,128)S(1)}, f32[8,128]{1,0:T(8,128)S(1)}) custom-call(s32[104]{0:T(128)S(1)} %copy-done.9, s32[104]{0:T(128)S(1)} %copy-done.11, s32[1]{0:T(128)} %get-tuple-element.20.count, f32[16,592,128]{2,1,0:T(8,128)} %bitcast.2, f32[16,16,128]{2,1,0:T(8,128)S(1)} %all-to-all-done.1.everyone, ...), custom_call_target="tpu_custom_call" | custom-call | tf_op jit(solution)/shard_map/far_second/pallas_call | solution.py:430
  110.9 9.5 %all_to_all.15.everyone = f32[16,8,128]{2,1,0:T(8,128)S(1)} all-to-all(f32[16,8,128]{2,1,0:T(8,128)S(1)} %broadcast_in_dim.11), channel_id=1, replica_groups=mesh['groups'=2,'leaf'=16] {'leaf'}, dimensions={0} | all-to-all | bytes 131072 | tf_op jit(solution)/shard_map/all_to_all | solution.py:346
  120.4 0.9 finish.1
  (30 shorter events, 0.4 us)
Async XLA Ops:
  7.2 63.4 %all-gather.3.cloned.1.call-start = ((), (), s32[]{:S(2)}) async-start(), calls=%async_computation.3 | async-start | bytes 5152768 | tf_op jit(solution)/shard_map/all_gather | solution.py:377
  8.0 1.0 copy-start
  9.0 0.7 copy-start.3
  9.7 0.7 copy-start.7
  10.4 0.7 copy-start.12
  11.0 84.7 %copy-start.2 = (f32[8,64,256]{2,1,0:T(8,128)S(1)}, f32[8,64,256]{2,1,0:T(8,128)}, u32[]{:S(2)}) copy-start(f32[8,64,256]{2,1,0:T(8,128)} %points.5) | copy-start | bytes 1572868
  13.6 86.1 %copy-start.6 = (f32[8,256]{1,0:T(8,128)S(1)}, f32[8,256]{1,0:T(8,128)}, u32[]{:S(2)}) copy-start(f32[8,256]{1,0:T(8,128)} %values.9) | copy-start | bytes 24580
  13.6 29.6 %collective-permute-start = (f32[2,72,256]{2,1,0:T(8,128)}, f32[2,72,256]{2,1,0:T(8,128)S(1)}, u32[]{:S(2)}, u32[]{:S(2)}) collective-permute-start(f32[2,72,256]{2,1,0:T(8,128)} %get-tuple-element.25), channel_id=1, source_target_pairs={{1,0},{2,1},{3,2},{4,3},{5,4},{6,5},{7,6},{8,7},{9,8},{10,9},{11,1... | collective-permute-start | bytes 442376 | tf_op jit(solution)/shard_map/ppermute | solution.py:341
  19.1 24.2 %collective-permute-start.1 = (f32[2,72,256]{2,1,0:T(8,128)}, f32[2,72,256]{2,1,0:T(8,128)S(1)}, u32[]{:S(2)}, u32[]{:S(2)}) collective-permute-start(f32[2,72,256]{2,1,0:T(8,128)} %get-tuple-element.26), channel_id=1, source_target_pairs={{15,0},{0,1},{1,2},{2,3},{3,4},{4,5},{5,6},{6,7},{7,8},{8,9},{9,10... | collective-permute-start | bytes 442376 | tf_op jit(solution)/shard_map/ppermute | solution.py:341
  21.4 12.6 %all-to-all-start = ((s32[16,2,32]{2,1,0:T(2,128)}), s32[16,2,32]{2,1,0:T(2,128)S(1)}, u32[]{:S(2)}, u32[]{:S(2)}) async-start(s32[16,2,32]{2,1,0:T(2,128)} %broadcast_in_dim.8), calls=%async_computation | async-start | bytes 32768 | tf_op jit(solution)/shard_map/all_to_all | solution.py:346
  43.2 38.8 %copy-start.8 = (s32[104]{0:T(128)}, s32[104]{0:T(128)S(1)}, u32[]{:S(2)}) copy-start(s32[104]{0:T(128)S(1)} %get-tuple-element.18.targets) | copy-start | bytes 1252
  43.2 38.8 %copy-start.10 = (s32[104]{0:T(128)}, s32[104]{0:T(128)S(1)}, u32[]{:S(2)}) copy-start(s32[104]{0:T(128)S(1)} %get-tuple-element.19.sources) | copy-start | bytes 1252
  43.3 1.2 copy-start.1
  44.5 0.7 copy-start.4
  70.6 0.7 copy-start.5
  82.0 17.7 %all-to-all-start.1 = ((f32[16,16,128]{2,1,0:T(8,128)}), f32[16,16,128]{2,1,0:T(8,128)S(1)}, u32[]{:S(2)}, u32[]{:S(2)}) async-start(f32[16,16,128]{2,1,0:T(8,128)} %broadcast_in_dim.10), calls=%async_computation.1 | async-start | bytes 262144 | tf_op jit(solution)/shard_map/all_to_all | solution.py:346
  85.6 5.7 %collective-permute-start.2 = (f32[2,256]{1,0:T(2,128)S(1)}, f32[2,256]{1,0:T(2,128)S(1)}, u32[]{:S(2)}, u32[]{:S(2)}) collective-permute-start(f32[2,256]{1,0:T(2,128)S(1)} %get-tuple-element.29), channel_id=1, source_target_pairs={{1,0},{2,1},{3,2},{4,3},{5,4},{6,5},{7,6},{8,7},{9,8},{10,9},{11,1... | collective-permute-start | bytes 6152 | tf_op jit(solution)/shard_map/ppermute | solution.py:341
  90.0 5.7 %collective-permute-start.3 = (f32[2,256]{1,0:T(2,128)S(1)}, f32[2,256]{1,0:T(2,128)S(1)}, u32[]{:S(2)}, u32[]{:S(2)}) collective-permute-start(f32[2,256]{1,0:T(2,128)S(1)} %get-tuple-element.30), channel_id=1, source_target_pairs={{15,0},{0,1},{1,2},{2,3},{3,4},{4,5},{5,6},{6,7},{7,8},{8,9},{9,10... | collective-permute-start | bytes 6152 | tf_op jit(solution)/shard_map/ppermute | solution.py:341
  99.7 0.7 copy-start.9
  100.4 0.6 copy-start.11
Sparse Core Ops, SparseCore 0:
  13.7 56.8 all-gather.2

commit v2 on v1

v2 whole, which is shorter than its diff:
```python
import functools
import math

import jax
import jax.numpy as jnp
from jax import lax
from jax.experimental import pallas as pl
from jax.experimental.pallas import tpu as pltpu
from jax.sharding import PartitionSpec as P

F32 = jnp.float32
BF16 = jnp.bfloat16
VMEM_LIMIT = 20 * 1024 * 1024
UNROLL = 4
GRID_DEVICES = 16
ORDER = ((0, 0), (0, 1), (1, 0), (3, 0), (1, 1), (3, 1), (2, 0), (2, 1))


def contract_first(left, right):
    return lax.dot_general(left, right, (((0,), (0,)), ((), ())), preferred_element_type=F32)


def halves(x):
    high = x.astype(BF16)
    return high, (x - high.astype(F32)).astype(BF16)


def thirds(x):
    high = x.astype(BF16)
    rest = x - high.astype(F32)
    middle = rest.astype(BF16)
    return high, middle, (rest - middle.astype(F32)).astype(BF16)


def norm_rows(x, factor, first):
    norm = jnp.sum(x * x, axis=0, keepdims=True) * factor
    high, middle, low = [piece.astype(F32) for piece in thirds(norm)]
    row = lax.broadcasted_iota(jnp.int32, (16, x.shape[1]), 0)
    rows = jnp.where(row < 6, 1.0, 0.0)
    for place, piece in ((first, high), (first + 1, middle), (first + 2, low)):
        rows = jnp.where(row == place, piece, rows)
    return rows.astype(BF16)


def unit(features):
    return 2.0 / features * math.log2(math.e)


def right_form(x):
    high, low = halves(x)
    return jnp.concatenate([high, high, low, norm_rows(x, -unit(x.shape[0]), 0)], axis=0)


def left_form(x):
    high, low = halves(x * (2.0 * unit(x.shape[0])))
    return jnp.concatenate([high, low, high, norm_rows(x, -unit(x.shape[0]), 3)], axis=0)


def tile_of(left, right):
    return jnp.exp2(contract_first(left, right))


def folded(tile, row):
    total = tile[:, :128] * row[:, :128]
    for start in range(128, tile.shape[1], 128):
        total = total + tile[:, start:start + 128] * row[:, start:start + 128]
    return total


def as_row(matrix):
    return jnp.sum(matrix.T, axis=0, keepdims=True)


def down(row):
    return jnp.broadcast_to(row, (128, row.shape[1])).T


def wide(column_matrix, columns):
    return jnp.concatenate([column_matrix] * (columns // 128), axis=1)


def owner_of(place, me, devices):
    if devices != GRID_DEVICES:
        return place
    turn, across = ORDER[place // 2]
    return (((me >> 2) - turn + 4) & 3) * 4 + ((me & 3) ^ (2 * across + place % 2))


def prepare_kernel(devices, capacity, *refs):
    (points_in, values_in, mask_in, skeleton_in, top_in, dest_in, leaf_in) = refs[:7]
    piece, again, to_skel, to_top, lefts, first, last = refs[7:14]
    points, values, mask, skeleton, top, dest, leaf, rights, sems = refs[14:]
    copies = []
    for n, (source, target) in enumerate(zip(refs[:7], (points, values, mask, skeleton, top, dest, leaf))):
        copies.append(pltpu.make_async_copy(source, target, sems.at[n]))
        copies[-1].start()
    for copy in copies:
        copy.wait()
    leaves, features, size = points.shape
    reach = first.shape[0]
    rank = skeleton.shape[1]
    fan_out = dest.shape[0]
    pad = first.shape[1] - features - 1 - reach
    top_total = jnp.zeros((3 * features, rank), F32)
    spot = lax.broadcasted_iota(jnp.int32, (size, rank), 0)
    for l in range(leaves):
        x = points[l]
        chosen = jnp.concatenate(
            [spot == skeleton[l:l + 1, :], spot == top[...] - l * size], axis=1
        )
        picked = jnp.dot(
            jnp.concatenate(thirds(x), axis=0),
            jnp.where(chosen, 1.0, 0.0).astype(BF16),
            preferred_element_type=F32,
        )
        skel = picked[:, :rank]
        skel = skel[:features] + skel[features:2 * features] + skel[2 * features:]
        piece[l * features:(l + 1) * features, :] = skel
        lefts[l] = left_form(skel)
        rights[l] = right_form(x)
        top_total = top_total + picked[:, rank:]
    chosen_top = top_total[:features] + top_total[features:2 * features] + top_total[2 * features:]
    piece[leaves * features:(leaves + 1) * features, :] = chosen_top
    lefts[leaves] = left_form(chosen_top)
    coarse = jnp.zeros((rank, 128), F32)
    base = (leaves + 1) * features
    for l in range(leaves):
        both = tile_of(jnp.concatenate([lefts[l], lefts[leaves]], axis=1), rights[l])
        to_skel[l] = both[:rank]
        to_top[l] = both[rank:]
        row = values[l:l + 1, :]
        piece[base + l:base + l + 1, :] = as_row(folded(both[:rank], row))
        coarse = coarse + folded(both[rank:], row)
    lane = lax.broadcasted_iota(jnp.int32, (1, 128), 1)
    codes = jnp.full((1, 128), -1.0, F32)
    seen = jnp.zeros((1, 128), jnp.int32)
    for l in range(leaves):
        for f in range(fan_out):
            here = lax.div(lane, jnp.int32(capacity)) == dest[f:f + 1, l:l + 1]
            code = (leaf[f:f + 1, l:l + 1] * leaves + l).astype(F32)
            codes = jnp.where(here & (lax.rem(lane, jnp.int32(capacity)) == seen), code, codes)
            seen = seen + here.astype(jnp.int32)
    piece[base + leaves:base + leaves + 8, :] = jnp.concatenate(
        [as_row(coarse), codes, jnp.zeros((6, 128), F32)], axis=0
    )
    again[...] = piece[...]
    for r in range(reach):
        first[r, :features, :] = points[r]
        last[r, :features, :] = points[leaves - reach + r]
        first[r, features:, :] = jnp.broadcast_to(values[r:r + 1, :], (first.shape[1] - features, size))
        own = leaves - reach + r
        rows = [values[own:own + 1, :]]
        rows += [jnp.broadcast_to(mask[s:s + 1, own:own + 1].astype(F32), (1, size)) for s in range(reach)]
        last[r, features:, :] = jnp.concatenate(rows + [jnp.zeros((pad, size), F32)], axis=0)


def edges_of(leaves, reach):
    pairs = [(a, r) for a in range(leaves + reach) for r in range(reach)]
    before = [(a, r) for a, r in pairs if a < reach <= a + 1 + r]
    after = [(a, r) for a, r in pairs if a >= reach and a + 1 + r >= leaves + reach]
    return before, after


def backward(tile, column):
    size = tile.shape[1]
    return jnp.sum((tile * wide(column, size)).reshape(-1, 8, size), axis=0)


def near_kernel(halo, points, values, mask, *refs):
    leaves, features, size = points.shape
    if halo:
        following, preceding, _, out, edges, _, lefts, rights, downs, across, along = refs
    else:
        out, lefts, rights, downs, across, along = refs
    reach = mask.shape[0]
    before, after = edges_of(leaves, reach)

    def block(e):
        if e < reach:
            return preceding[e, :features, :]
        if e < reach + leaves:
            return points[e - reach]
        return following[e - reach - leaves, :features, :]

    def row_of(e):
        if e < reach:
            return preceding[e, features:features + 1, :]
        if e < reach + leaves:
            return values[e - reach:e - reach + 1, :]
        return following[e - reach - leaves, features:features + 1, :]

    for e in range(leaves + 2 * reach):
        own = reach <= e < leaves + reach
        if own or halo:
            x = block(e)
            if e < leaves + reach:
                lefts[e] = left_form(x)
                downs[e] = down(row_of(e))
            if e >= reach:
                rights[e] = right_form(x)
    for l in range(leaves):
        e = l + reach
        along[l] = backward(tile_of(lefts[e], rights[e]), downs[e])
        across[l] = jnp.zeros((size, 128), F32)
    for a in range(leaves + reach):
        for r in range(reach):
            b = a + 1 + r
            if a >= reach and b < leaves + reach:
                @pl.when(mask[r, a - reach] != 0)
                def _(a=a, b=b):
                    tile = tile_of(lefts[a], rights[b])
                    across[a - reach] += folded(tile, row_of(b))
                    along[b - reach] += backward(tile, downs[a])
    if halo:
        for n, (a, r) in enumerate(before):
            b = a + 1 + r
            tile = tile_of(lefts[a], rights[b]) * preceding[a, features + 1 + r:features + 2 + r, :]
            edges[n] = tile
            along[b - reach] += backward(tile, downs[a])
        for n, (a, r) in enumerate(after):
            b = a + 1 + r
            place = len(before) + n

            @pl.when(mask[r, a - reach] == 0)
            def _(place=place):
                edges[place] = jnp.zeros((size, size), F32)

            @pl.when(mask[r, a - reach] != 0)
            def _(a=a, b=b, place=place):
                tile = tile_of(lefts[a], rights[b])
                edges[place] = tile
                across[a - reach] += folded(tile, row_of(b))

    for l in range(leaves):
        out[l:l + 1, :] = as_row(across[l]) + jnp.sum(along[l], axis=0, keepdims=True)


def far_group(axis, devices, capacity, places, own_piece, pieces, lefts, lists, tiles, tops, sums, scratch):
    targets, vectors, count = lists
    sources, rows, codes, sems = scratch
    leaves = lefts.shape[0] - 1
    features = (pieces[0].shape[0] - 16) // (leaves + 1)
    base = (leaves + 1) * features
    me = lax.axis_index(axis)
    copies = [
        pltpu.make_async_copy(ref.at[base + 8:base + 16, :], codes.at[n], sems.at[n])
        for n, ref in enumerate([own_piece] + list(pieces))
    ]
    for copy in copies:
        copy.start()
    for n, piece in enumerate(pieces):
        tile = tile_of(lefts[leaves], right_form(piece[leaves * features:(leaves + 1) * features, :]))
        tops[n] = tile
        sums[leaves + 1] += tile * piece[base + leaves:base + leaves + 1, :]
    for copy in copies:
        copy.wait()
    filled = 0
    for n, (place, piece) in enumerate(zip(places, pieces)):
        device = owner_of(place, me, devices)
        found = []
        if place == 0 and devices == GRID_DEVICES:
            found += [(l, l, None) for l in range(leaves)]
        for k in range(capacity):
            code = codes[0, 1, device * capacity + k].astype(jnp.int32)
            safe = jnp.maximum(code, 0)
            found.append((lax.rem(safe, leaves), lax.div(safe, leaves), code >= 0))
            code = codes[n + 1, 1, me * capacity + k].astype(jnp.int32)
            safe = jnp.maximum(code, 0)
            found.append((lax.div(safe, leaves), lax.rem(safe, leaves), code >= 0))
        if devices != GRID_DEVICES:
            found += [(l, l, device == me) for l in range(leaves)]
        for target, leaf, used in found:
            start = leaf * features
            if not isinstance(leaf, int):
                start = pl.multiple_of(start, features)
            sources[filled] = piece[pl.ds(start, features), :]
            rows[pl.ds(filled, 1), :] = piece[pl.ds(base + leaf, 1), :]
            targets[filled] = target
            vectors[filled] = device * leaves + leaf
            filled = filled + (1 if used is None else used.astype(jnp.int32))
    count[0] = filled
    for k in range(UNROLL):
        targets[filled + k] = leaves
        vectors[filled + k] = 0
        sources[filled + k] = pieces[0][:features, :]
        rows[pl.ds(filled + k, 1), :] = pieces[0][:1, :]

    def step(g, carry):
        found = []
        for k in range(UNROLL):
            n = g * UNROLL + k
            tile = tile_of(lefts[targets[n]], right_form(sources[n]))
            tiles[n] = tile
            found.append((n, tile * rows[pl.ds(n, 1), :]))
        for n, product in found:
            sums[targets[n]] += product
        return carry

    lax.fori_loop(0, (filled + UNROLL - 1) // UNROLL, step, 0)


def far_rows(sums, to_skel, to_top):
    leaves = to_skel.shape[0]
    mixed = jnp.sum(sums[leaves + 1], axis=1, keepdims=True)
    far, top = [], []
    for l in range(leaves):
        far.append(jnp.sum(to_skel[l] * jnp.sum(sums[l], axis=1, keepdims=True), axis=0, keepdims=True))
        top.append(jnp.sum(to_top[l] * mixed, axis=0, keepdims=True))
    return jnp.concatenate(far, axis=0), jnp.concatenate(top, axis=0)


def total_of(x):
    return jnp.sum(jnp.sum(x, axis=1, keepdims=True), axis=0, keepdims=True)


def in_lanes(*numbers):
    lane = lax.broadcasted_iota(jnp.int32, (1, 128), 1)
    row = jnp.zeros((1, 128), F32)
    for place, number in enumerate(numbers):
        row = jnp.where(lane == place, number, row)
    return row


def early_kernel(axis, devices, capacity, places, *refs):
    n = len(places)
    own_piece, pieces, lefts = refs[0], refs[1:n + 1], refs[n + 1]
    start = None
    if places[0] != 0:
        start, refs = refs[n + 2], refs[:n + 2] + refs[n + 3:]
    targets, vectors, count, tiles, tops, sums = refs[n + 2:n + 8]
    sums[...] = jnp.zeros_like(sums) if start is None else start[...]
    far_group(
        axis, devices, capacity, places, own_piece, pieces, lefts,
        (targets, vectors, count), tiles, tops, sums, refs[n + 8:],
    )


def first_kernel(reach, axis, devices, capacity, places, *refs):
    n = len(places)
    own_piece, pieces, lefts = refs[0], refs[1:n + 1], refs[n + 1]
    so_far, to_skel, to_top, values, near = refs[n + 2:n + 7]
    targets, vectors, count, tiles, tops, image, payload = refs[n + 7:n + 14]
    sums = refs[n + 14]
    sums[...] = so_far[...]
    far_group(
        axis, devices, capacity, places, own_piece, pieces, lefts,
        (targets, vectors, count), tiles, tops, sums, refs[n + 15:],
    )
    leaves, rank, size = to_skel.shape
    far, top = far_rows(sums, to_skel, to_top)
    start = values[...]
    result = start + 0.25 * near[...] + 0.125 * far + 0.25 * top
    image[...] = result
    coarse = jnp.zeros((rank, 128), F32)
    rows = []
    for l in range(leaves):
        row = result[l:l + 1, :]
        rows.append(as_row(folded(to_skel[l], row)))
        coarse = coarse + folded(to_top[l], row)
    rows.append(as_row(coarse))
    rows.append(in_lanes(total_of(start * start), total_of(start * result)))
    rows.append(jnp.zeros((16 - leaves - 2, 128), F32))
    for l in list(range(reach)) + list(range(leaves - reach, leaves)):
        rows += [result[l:l + 1, part:part + 128] for part in range(0, size, 128)]
    payload[...] = jnp.concatenate(rows, axis=0)


def beside_of(me, devices):
    return jnp.where(me == 0, devices - 1, me - 1), jnp.where(me == devices - 1, 0, me + 1)


def second_kernel(reach, axis, devices, groups, *refs):
    lists, refs = refs[:3 * len(groups)], refs[3 * len(groups):]
    tiles, refs = refs[:len(groups)], refs[len(groups):]
    tops, refs = refs[:len(groups)], refs[len(groups):]
    received, refs = refs[:1 if devices != GRID_DEVICES else 4], refs[1 if devices != GRID_DEVICES else 4:]
    to_skel, to_top, values, image, near, edges, residual, along, numbers, everyone, sums, across, beside = refs
    leaves, rank, size = to_skel.shape
    me = lax.axis_index(axis)
    if devices != GRID_DEVICES:
        everyone[...] = received[0][...]
    else:
        for other, blocks in enumerate(received):
            for turn in range(4):
                source = (((me >> 2) - turn + 4) & 3) * 4 + ((me & 3) ^ other)
                everyone[source] = blocks[turn]
    sums[...] = jnp.zeros_like(sums)
    for g, places in enumerate(groups):
        targets, vectors, count = lists[3 * g:3 * g + 3]

        def step(n, carry, g=g, targets=targets, vectors=vectors):
            products = []
            for k in range(UNROLL):
                vector = vectors[n * UNROLL + k]
                products.append(tiles[g][n * UNROLL + k] * everyone[lax.div(vector, leaves), pl.ds(lax.rem(vector, leaves), 1), :])
            for k in range(UNROLL):
                sums[targets[n * UNROLL + k]] += products[k]
            return carry

        lax.fori_loop(0, (count[0] + UNROLL - 1) // UNROLL, step, 0)
        for n, place in enumerate(places):
            device = owner_of(place, me, devices)
            sums[leaves + 1] += tops[g][n] * everyone[device, leaves:leaves + 1, :]
    far, top = far_rows(sums, to_skel, to_top)

    before, after = edges_of(leaves, reach)
    across[...] = jnp.zeros_like(across)
    beside[...] = jnp.zeros_like(beside)

    def edge_row(device, place):
        first = 16 + place * (size // 128)
        return jnp.concatenate([everyone[device, n:n + 1, :] for n in range(first, first + size // 128)], axis=1)

    behind, ahead = beside_of(me, devices)
    for n, (a, r) in enumerate(before):
        beside[a + 1 + r - reach] += backward(edges[n], down(edge_row(behind, reach + a)))
    for n, (a, r) in enumerate(after):
        row = edge_row(ahead, a + 1 + r - reach - leaves)
        across[a - leaves] += folded(edges[len(before) + n], row)
    extra = [jnp.sum(beside[r], axis=0, keepdims=True) for r in range(reach)]
    extra += [jnp.zeros((leaves - 2 * reach, size), F32)]
    extra += [as_row(across[r]) for r in range(reach)]
    start, first = values[...], image[...]
    near_all = near[...] + jnp.concatenate(extra, axis=0)
    second = first + 0.25 * near_all + 0.125 * far + 0.25 * top
    scalars = jnp.sum(everyone[:, leaves + 1, :], axis=0, keepdims=True)
    norm, product = scalars[:, 0:1], scalars[:, 1:2]
    alpha = norm / product
    left = start - alpha * first
    image_left = first - alpha * second
    residual[...] = left
    along[...] = image_left
    row = in_lanes(total_of(left * left), total_of(left * image_left), norm, alpha)
    numbers[...] = jnp.broadcast_to(row, numbers.shape)


def last_kernel(everyone, values, image, residual, along, solution_field, final):
    scalars = jnp.sum(everyone[:, 0, :], axis=0, keepdims=True)
    norm_next, product = scalars[:, 0:1], scalars[:, 1:2]
    norm, alpha = everyone[0, 0:1, 2:3], everyone[0, 0:1, 3:4]
    ratio = norm_next / norm
    step = norm_next / (product - ratio * norm_next / alpha)
    start, left = values[...], residual[...]
    solution_field[...] = alpha * start + step * (left + ratio * start)
    final[...] = left - step * (along[...] + ratio * image[...])


def shape(*dims, dtype=F32):
    return jax.ShapeDtypeStruct(dims, dtype)


SMEM = pl.BlockSpec(memory_space=pltpu.SMEM)
VMEM = pl.BlockSpec(memory_space=pltpu.VMEM)
ANY = pl.BlockSpec(memory_space=pl.ANY)
HBM = pl.BlockSpec(memory_space=pltpu.HBM)


def kernel_call(body, name, inputs, outputs, scratch=(), aliases={}, limit=VMEM_LIMIT, microseconds=1):
    out_specs, out_shapes = zip(*outputs)
    return pl.pallas_call(
        body,
        in_specs=list(inputs),
        out_specs=list(out_specs),
        out_shape=list(out_shapes),
        scratch_shapes=list(scratch),
        input_output_aliases=aliases,
        compiler_params=pltpu.CompilerParams(vmem_limit_bytes=limit),
        cost_estimate=pl.CostEstimate(
            flops=microseconds * 1_000_000_000, bytes_accessed=microseconds * 3_000_000, transcendentals=0
        ),
        name=name,
    )


def passed_along(block, axis, distance):
    size = lax.axis_size(axis)
    return lax.ppermute(block, axis, [((i - distance) % size, i) for i in range(size)])


def swapped(block, axis, bit):
    return lax.ppermute(block, axis, [(i, i ^ bit) for i in range(lax.axis_size(axis))])


def exchanged(blocks, axis):
    return lax.all_to_all(blocks, axis, split_axis=0, concat_axis=0, tiled=True)


def gathered_blocks(block, axis):
    devices = lax.axis_size(axis)
    if devices != GRID_DEVICES:
        return [exchanged(jnp.broadcast_to(block[None], (devices,) + block.shape), axis)]
    turned = jnp.stack([block] + [passed_along(block, axis, 4 * turn) for turn in (1, 2, 3)])
    return [turned] + [swapped(turned, axis, other) for other in (1, 2, 3)]


def all_pieces(piece, again, axis):
    devices = lax.axis_size(axis)
    if devices != GRID_DEVICES:
        together = lax.all_gather(piece[None], axis, axis=0, tiled=True)
        return [together[n] for n in range(devices)]
    turned = {0: piece}
    for turn in (1, 3, 2):
        turned[turn] = passed_along(again if turn == 2 else piece, axis, 4 * turn)
    pieces = []
    for turn, across in ORDER:
        mine = swapped(turned[turn], axis, 2) if across else turned[turn]
        pieces += [mine, swapped(mine, axis, 1)]
    return pieces


def on_device(points, right_side, near_mask, far_dest, far_leaf, skeleton, top_index):
    leaves, features, size = points.shape
    reach = near_mask.shape[1]
    fan_out = far_dest.shape[1]
    rank = skeleton.shape[1]
    devices = lax.axis_size("leaf")
    capacity = max(2, (2 * leaves * fan_out + devices - 1) // devices)
    depth = 3 * features + 16
    piece_rows = (leaves + 1) * features + 16
    halo_rows = features + 8
    integers = jnp.int32
    payload_rows = 16 + 2 * reach * size // rank

    piece, again, to_skel, to_top, lefts, first, last = kernel_call(
        functools.partial(prepare_kernel, devices, capacity),
        "prepare",
        [HBM] * 7,
        [
            (VMEM, shape(piece_rows, rank)),
            (VMEM, shape(piece_rows, rank)),
            (VMEM, shape(leaves, rank, size)),
            (VMEM, shape(leaves, rank, size)),
            (VMEM, shape(leaves + 1, depth, rank, dtype=BF16)),
            (VMEM, shape(reach, halo_rows, size)),
            (VMEM, shape(reach, halo_rows, size)),
        ],
        [
            pltpu.VMEM(points.shape, F32),
            pltpu.VMEM(right_side.shape, F32),
            pltpu.VMEM(near_mask.T.shape, integers),
            pltpu.VMEM(skeleton.shape, integers),
            pltpu.VMEM(top_index.shape, integers),
            pltpu.VMEM(far_dest.T.shape, integers),
            pltpu.VMEM(far_leaf.T.shape, integers),
            pltpu.VMEM((leaves, depth, size), BF16),
            pltpu.SemaphoreType.DMA((7,)),
        ],
        limit=60 * 1024 * 1024,
        microseconds=2,
    )(points, right_side, near_mask.T, skeleton, top_index, far_dest.T, far_leaf.T)

    following = passed_along(first, "leaf", -1)
    preceding = passed_along(last, "leaf", 1)
    def near_apply(halo, values, *others):
        before, after = edges_of(leaves, reach)
        outputs = [(VMEM, shape(leaves, size))]
        if halo:
            outputs.append((VMEM, shape(len(before) + len(after), size, size)))
            outputs.append((ANY, shape(piece_rows, rank)))
        return kernel_call(
            functools.partial(near_kernel, halo),
            "near_first" if halo else "near_second",
            [VMEM, VMEM, SMEM] + [VMEM, VMEM, ANY][:len(others)],
            outputs,
            [
                pltpu.VMEM((leaves + reach, depth, size), BF16),
                pltpu.VMEM((leaves + 2 * reach, depth, size), BF16),
                pltpu.VMEM((leaves + reach, size, 128), F32),
                pltpu.VMEM((leaves, size, 128), F32),
                pltpu.VMEM((leaves, 8, size), F32),
            ],
            {5: 2} if halo else {},
            microseconds=5,
        )(points, values, near_mask.T, *others)

    near, edges, again = near_apply(True, right_side, following, preceding, again)
    pieces = all_pieces(piece, again, "leaf")
    cuts = (0, devices // 2, devices * 7 // 8, devices)
    groups = [tuple(range(start, end)) for start, end in zip(cuts, cuts[1:])]
    sums = shape(leaves + 2, rank, rank)

    def group_call(body, name, places, inputs, outputs, scratch):
        most = -(-(2 * capacity * len(places) + leaves + UNROLL) // UNROLL) * UNROLL
        return kernel_call(
            functools.partial(body, "leaf", devices, capacity, places),
            name,
            [ANY] + [VMEM] * (len(places) + 1 + len(inputs)),
            [
                (SMEM, shape(most, dtype=integers)),
                (SMEM, shape(most, dtype=integers)),
                (SMEM, shape(1, dtype=integers)),
                (VMEM, shape(most, rank, rank)),
                (VMEM, shape(len(places), rank, rank)),
            ] + outputs,
            scratch + [
                pltpu.VMEM((most, features, rank), F32),
                pltpu.VMEM((most, rank), F32),
                pltpu.SMEM((len(places) + 1, 8, 128), F32),
                pltpu.SemaphoreType.DMA((len(places) + 1,)),
            ],
            microseconds=1 + len(places),
        )(piece, *[pieces[place] for place in places], lefts, *inputs)

    early = group_call(early_kernel, "far_early", groups[0], [], [(VMEM, sums)], [])
    middle = group_call(early_kernel, "far_middle", groups[1], [early[5]], [(VMEM, sums)], [])
    late = group_call(
        functools.partial(first_kernel, reach),
        "far_late",
        groups[2],
        [middle[5], to_skel, to_top, right_side, near],
        [(VMEM, shape(leaves, size)), (VMEM, shape(payload_rows, rank))],
        [pltpu.VMEM(sums.shape, F32)],
    )
    image, payload = late[5:]

    everyone = gathered_blocks(payload, "leaf")
    near_second = near_apply(False, image)[0]
    residual, along, numbers = kernel_call(
        functools.partial(second_kernel, reach, "leaf", devices, groups),
        "far_second",
        [SMEM] * 9 + [VMEM] * (12 + len(everyone)),
        [
            (VMEM, shape(leaves, size)),
            (VMEM, shape(leaves, size)),
            (VMEM, shape(devices, 1, 128)),
        ],
        [
            pltpu.VMEM((devices, payload_rows, rank), F32),
            pltpu.VMEM(sums.shape, F32),
            pltpu.VMEM((reach, size, 128), F32),
            pltpu.VMEM((reach, 8, size), F32),
        ],
    )(
        *early[:3], *middle[:3], *late[:3], early[3], middle[3], late[3], early[4], middle[4], late[4],
        *everyone, to_skel, to_top, right_side, image, near_second, edges,
    )

    solution_field, final = kernel_call(
        last_kernel,
        "finish",
        [VMEM] * 5,
        [(VMEM, shape(leaves, size)), (VMEM, shape(leaves, size))],
    )(exchanged(numbers, "leaf"), right_side, image, residual, along)
    return solution_field, final


def solution(mesh):
    rows = P(("groups", "leaf"), None)
    in_specs = (P(("groups", "leaf"), None, None),) + (rows,) * 6
    return jax.shard_map(
        on_device, mesh=mesh, in_specs=in_specs, out_specs=(rows, rows), check_vma=False
    )
```

time: 130 us -> 91.7 us (0.71); the launches traced: 128 us -> 92.3 us
  between operations: 14.2 us -> 0.84 us
  waiting for transfers between devices: 33.2 us -> 21.9 us
  Pallas kernels: 40.3 us -> 29 us
  local copies, waits for them, and re-layouts: 11.6 us -> 0.99 us
  starting transfers between devices: 19.4 us -> 27 us
  blocking collectives: 9.48 us -> 12.5 us
    all_gather x1 -> x0, waiting for transfers between devices: 21.4 us -> none  [on_device(): gathered = lax.all_gather(piece[None], 'leaf', axis=0, tiled=True)]
    ppermute x4 -> x8, waiting for transfers between devices: 5.71 us -> 18.7 us  [passed_along(): lax.ppermute(block, axis, [((i - distance) % size, i) for i in range(size)])]
    pallas_call x7 -> x8, Pallas kernels: 40.3 us -> 29 us  [the longest x3 12.3 us: group_call(): kernel_call(functools.partial(body, 'leaf', devices, capacity, places), n...]
    ppermute x4 -> x8, starting transfers between devices: 9.88 us -> 19.7 us  [passed_along(): lax.ppermute(block, axis, [((i - distance) % size, i) for i in range(size)])]
    all_to_all x2 -> x0, starting transfers between devices: 9.43 us -> none  [everyones(): lax.all_to_all(jnp.broadcast_to(block[None], (size,) + block.shape), axis...]
    unnamed x29 -> x16, local copies, waits for them, and re-layouts: 9.22 us -> 0.99 us
    ppermute x0 -> x15, starting transfers between devices: none -> 7.32 us  [swapped(): lax.ppermute(block, axis, [(i, i ^ bit) for i in range(lax.axis_size(axis...]
    all_to_all x2 -> x0, waiting for transfers between devices: 6.03 us -> none  [everyones(): lax.all_to_all(jnp.broadcast_to(block[None], (size,) + block.shape), axis...]
  transfers between devices with their start and end apart: 7 -> 23, of which waited for: 4 -> 8; matrix products, arithmetic and copies ran while one was open for 2% -> 0% of each run, Pallas kernels for 13% -> 19%
where the time goes in v2:
time: 91.7 us; the launch traced here: 92.3 us
  Pallas kernels  29 us (32%)
  starting transfers between devices  27 us (29%)
  waiting for transfers between devices  21.9 us (24%)
  blocking collectives  12.5 us (14%)
  local copies, waits for them, and re-layouts  0.99 us (1%)
    ppermute x8, starting transfers between devices, passed_along(): lax.ppermute(block, axis, [((i - distance) % size, i) for i in range(size)])  19.7 us
    ppermute x8, waiting for transfers between devices, passed_along(): lax.ppermute(block, axis, [((i - distance) % size, i) for i in range(size)])  18.7 us
    all_to_all x1, blocking collectives, exchanged(): return lax.all_to_all(blocks, axis, split_axis=0, concat_axis=0, tiled=True)  12.5 us
    pallas_call x3, Pallas kernels, group_call(): kernel_call(functools.partial(body, 'leaf', devices, capacity, places), n...  12.3 us
    pallas_call x2, Pallas kernels, near_apply(): kernel_call(functools.partial(near_kernel, halo), 'near_first' if halo el...  7.68 us
    ppermute x15, starting transfers between devices, swapped(): lax.ppermute(block, axis, [(i, i ^ bit) for i in range(lax.axis_size(axis...  7.32 us
    pallas_call x1, Pallas kernels, on_device(): kernel_call(functools.partial(second_kernel, reach, 'leaf', devices, grou...  4.13 us
    pallas_call x1, Pallas kernels, on_device(): kernel_call(functools.partial(prepare_kernel, devices, capacity), 'prepar...  4.03 us
  transfers between devices with their start and end apart: 23, of which 8 were waited for; matrix products, arithmetic and copies ran while one was open for 0% of the time, Pallas kernels for 19%

profile of v2, /device:TPU:0, one launch (start us, length us, event | category | flops | bytes accessed | tf_op | source)
XLA Modules:
  0.0 92.3 jit_solution(6561186559668436580)
XLA Ops:
  0.7 4.0 %prepare.1 = (f32[592,128]{1,0:T(8,128)}, f32[592,128]{1,0:T(8,128)}, f32[8,128,256]{2,1,0:T(8,128)}, f32[8,128,256]{2,1,0:T(8,128)}, bf16[9,208,128]{2,1,0:T(8,...) custom-call(f32[8,64,256]{2,1,0:T(8,128)} %points.3, f32[8,256]{1,0:T(8,128)} %values.3, s32[2,8]{1,0:T(2,128)} %bitcast.8, ...), custom_call_target="tpu_custom_call" | custom-call | flops 2000000000 | bytes 6000000 | tf_op jit(solution)/shard_map/prepare/pallas_call | solution.py:524
  4.7 5.5 %collective-permute-start.11 = (f32[2,72,256]{2,1,0:T(8,128)}, f32[2,72,256]{2,1,0:T(8,128)S(1)}, u32[]{:S(2)}, u32[]{:S(2)}) collective-permute-start(f32[2,72,256]{2,1,0:T(8,128)} %get-tuple-element.39), channel_id=1, source_target_pairs={{1,0},{2,1},{3,2},{4,3},{5,4},{6,5},{7,6},{8,7},{9,8},{10,9},{11,1... | collective-permute-start | bytes 442376 | tf_op jit(solution)/shard_map/ppermute | solution.py:477
  10.2 3.8 %collective-permute-start.5 = (f32[592,128]{1,0:T(8,128)}, f32[592,128]{1,0:T(8,128)S(1)}, u32[]{:S(2)}, u32[]{:S(2)}) collective-permute-start(f32[592,128]{1,0:T(8,128)} %get-tuple-element.34.refs_0_.refs_1_), channel_id=1, source_target_pairs={{4,0},{5,1},{6,2},{7,3},{8,4},{9,5},{10,6},{11,7},{12,8},{13,9},{1... | collective-permute-start | bytes 909320 | tf_op jit(solution)/shard_map/ppermute | solution.py:477
  14.0 0.8 collective-permute-done.11.refs_0_
  14.8 0.2 collective-permute-start
  15.0 4.3 %collective-permute-done.12.refs_1_ = f32[2,72,256]{2,1,0:T(8,128)S(1)} collective-permute-done((f32[2,72,256]{2,1,0:T(8,128)}, f32[2,72,256]{2,1,0:T(8,128)S(1)}, u32[]{:S(2)}, u32[]{:S(2)}) %collective-permute-start.12) | collective-permute-done | bytes 147488 | tf_op jit(solution)/shard_map/ppermute | solution.py:477
  19.3 1.0 %copy-done.5 = f32[592,128]{1,0:T(8,128)S(1)} copy-done((f32[592,128]{1,0:T(8,128)S(1)}, f32[592,128]{1,0:T(8,128)}, u32[]{:S(2)}) %copy-start.5) | copy-done | bytes 303128
  20.3 4.2 %near_first.1 = (f32[8,256]{1,0:T(8,128)S(1)}, f32[6,256,256]{2,1,0:T(8,128)S(1)}, f32[592,128]{1,0:T(8,128)S(1)}) custom-call(f32[8,64,256]{2,1,0:T(8,128)S(1)} %copy-done.3, f32[8,256]{1,0:T(8,128)S(1)} %copy-done.2, s32[2,8]{1,0:T(2,128)S(1)} %bitcast.9, f32[2,72,256]{2,1,0:T(8,128)S(1)} %collective-permute-done.11.refs_0_, ...), custom_call_target="tpu_custom_call", output_to_operand_aliasing={{2}: (5, {})} | custom-call | flops 5000000000 | bytes 15000000 | tf_op jit(solution)/shard_map/near_first/pallas_call | solution.py:560
  24.5 0.1 collective-permute-start.13
  24.6 0.1 collective-permute-start.4
  24.7 3.0 %collective-permute-done.5.refs_7_ = f32[592,128]{1,0:T(8,128)S(1)} collective-permute-done((f32[592,128]{1,0:T(8,128)}, f32[592,128]{1,0:T(8,128)S(1)}, u32[]{:S(2)}, u32[]{:S(2)}) %collective-permute-start.5) | collective-permute-done | bytes 303136 | tf_op jit(solution)/shard_map/ppermute | solution.py:477
  27.7 0.3 collective-permute-start.9
  28.0 1.8 %collective-permute-start.7 = (f32[592,128]{1,0:T(8,128)S(1)}, f32[592,128]{1,0:T(8,128)S(1)}, u32[]{:S(2)}, u32[]{:S(2)}) collective-permute-start(f32[592,128]{1,0:T(8,128)S(1)} %collective-permute-done.3.refs_5_), channel_id=1, source_target_pairs={{0,2},{1,3},{2,0},{3,1},{4,6},{5,7},{6,4},{7,5},{8,10},{9,11},{10,... | collective-permute-start | bytes 909320 | tf_op jit(solution)/shard_map/ppermute | solution.py:481
  29.8 9.2 %collective-permute-done.13.refs_5_ = f32[592,128]{1,0:T(8,128)S(1)} collective-permute-done((f32[592,128]{1,0:T(8,128)S(1)}, f32[592,128]{1,0:T(8,128)S(1)}, u32[]{:S(2)}, u32[]{:S(2)}) %collective-permute-start.13) | collective-permute-done | bytes 303136 | tf_op jit(solution)/shard_map/ppermute | solution.py:477
  39.0 0.5 collective-permute-start.14
  39.5 2.3 %collective-permute-start.15 = (f32[592,128]{1,0:T(8,128)S(1)}, f32[592,128]{1,0:T(8,128)S(1)}, u32[]{:S(2)}, u32[]{:S(2)}) collective-permute-start(f32[592,128]{1,0:T(8,128)S(1)} %collective-permute-done.13.refs_5_), channel_id=1, source_target_pairs={{0,2},{1,3},{2,0},{3,1},{4,6},{5,7},{6,4},{7,5},{8,10},{9,11},{10,... | collective-permute-start | bytes 909320 | tf_op jit(solution)/shard_map/ppermute | solution.py:481
  41.8 2.4 %collective-permute-done.7.refs_1_ = f32[592,128]{1,0:T(8,128)S(1)} collective-permute-done((f32[592,128]{1,0:T(8,128)S(1)}, f32[592,128]{1,0:T(8,128)S(1)}, u32[]{:S(2)}, u32[]{:S(2)}) %collective-permute-start.7) | collective-permute-done | bytes 303136 | tf_op jit(solution)/shard_map/ppermute | solution.py:481
  44.2 5.5 %far_early.1 = (s32[76]{0:T(128)S(1)}, s32[76]{0:T(128)S(1)}, s32[1]{0:T(128)}, f32[76,128,128]{2,1,0:T(8,128)S(1)}, f32[8,128,128]{2,1,0:T(8,128)S(1)}, /*index=5*/f32[10,128,128]{2,1,0:T(8,128)S(1)}) custom-call(f32[592,128]{1,0:T(8,128)S(1)} %copy-done.4, f32[592,128]{1,0:T(8,128)S(1)} %copy-done.4, f32[592,128]{1,0:T(8,128)S(1)} %collective-permute-done.refs_2_, ...), custom_call_target="tpu_custom_call" | custom-call | flops 8999999488 | bytes 27000000 | tf_op jit(solution)/shard_map/far_early/pallas_call | solution.py:584
  49.8 0.6 collective-permute-done.15.refs_1_
  50.4 4.0 %far_middle.1 = (s32[60]{0:T(128)S(1)}, s32[60]{0:T(128)S(1)}, s32[1]{0:T(128)}, f32[60,128,128]{2,1,0:T(8,128)S(1)}, f32[6,128,128]{2,1,0:T(8,128)S(1)}, /*index=5*/f32[10,128,128]{2,1,0:T(8,128)S(1)}) custom-call(f32[592,128]{1,0:T(8,128)S(1)} %copy-done.4, f32[592,128]{1,0:T(8,128)S(1)} %collective-permute-done.7.refs_1_, ...), custom_call_target="tpu_custom_call" | custom-call | flops 7000000000 | bytes 21000000 | tf_op jit(solution)/shard_map/far_middle/pallas_call | solution.py:584
  54.4 2.8 %far_late.1 = (s32[28]{0:T(128)S(1)}, s32[28]{0:T(128)S(1)}, s32[1]{0:T(128)}, f32[28,128,128]{2,1,0:T(8,128)S(1)}, f32[2,128,128]{2,1,0:T(8,128)S(1)}, /*index=5*/f32[8,256]{1,0:T(8,128)S(1)}, f32[24,128]{1,0:T(8,128)S(1)}) custom-call(f32[592,128]{1,0:T(8,128)S(1)} %copy-done.4, f32[592,128]{1,0:T(8,128)S(1)} %collective-permute-done.15.refs_1_, ...), custom_call_target="tpu_custom_call" | custom-call | flops 3000000000 | bytes 9000000 | tf_op jit(solution)/shard_map/far_late/pallas_call | solution.py:584
  57.2 0.6 collective-permute-start.17
  57.8 6.8 %collective-permute-start.18 = (f32[24,128]{1,0:T(8,128)S(1)}, f32[24,128]{1,0:T(8,128)S(1)}, u32[]{:S(2)}, u32[]{:S(2)}) collective-permute-start(f32[24,128]{1,0:T(8,128)S(1)} %get-tuple-element.60), channel_id=1, source_target_pairs={{8,0},{9,1},{10,2},{11,3},{12,4},{13,5},{14,6},{15,7},{0,8},{1,9},... | collective-permute-start | bytes 36872 | tf_op jit(solution)/shard_map/ppermute | solution.py:477
  64.6 2.8 %collective-permute-start.19 = (f32[24,128]{1,0:T(8,128)S(1)}, f32[24,128]{1,0:T(8,128)S(1)}, u32[]{:S(2)}, u32[]{:S(2)}) collective-permute-start(f32[24,128]{1,0:T(8,128)S(1)} %get-tuple-element.60), channel_id=1, source_target_pairs={{4,0},{5,1},{6,2},{7,3},{8,4},{9,5},{10,6},{11,7},{12,8},{13,9},{1... | collective-permute-start | bytes 36872 | tf_op jit(solution)/shard_map/ppermute | solution.py:477
  67.5 1.4 %collective-permute-done.19 = f32[24,128]{1,0:T(8,128)S(1)} collective-permute-done((f32[24,128]{1,0:T(8,128)S(1)}, f32[24,128]{1,0:T(8,128)S(1)}, u32[]{:S(2)}, u32[]{:S(2)}) %collective-permute-start.19) | collective-permute-done | bytes 12320 | tf_op jit(solution)/shard_map/ppermute | solution.py:477
  68.9 2.1 %collective-permute-start.21 = (f32[4,24,128]{2,1,0:T(8,128)S(1)}, f32[4,24,128]{2,1,0:T(8,128)S(1)}, u32[]{:S(2)}, u32[]{:S(2)}) collective-permute-start(f32[4,24,128]{2,1,0:T(8,128)S(1)} %pad_maximum_fusion.refs_15_), channel_id=1, source_target_pairs={{0,2},{1,3},{2,0},{3,1},{4,6},{5,7},{6,4},{7,5},{8,10},{9,11},{10,... | collective-permute-start | bytes 147464 | tf_op jit(solution)/shard_map/ppermute | solution.py:481
  71.0 0.1 collective-permute-start.22
  71.1 3.5 %near_second.1.refs_23_ = f32[8,256]{1,0:T(8,128)S(1)} custom-call(f32[8,64,256]{2,1,0:T(8,128)S(1)} %copy-done.3, f32[8,256]{1,0:T(8,128)S(1)} %get-tuple-element.61.values.refs_22_.image, s32[2,8]{1,0:T(2,128)S(1)} %bitcast.10), custom_call_target="tpu_custom_call" | custom-call | flops 5000000000 | bytes 15000000 | tf_op jit(solution)/shard_map/near_second/pallas_call | solution.py:560
  74.6 0.2 collective-permute-done.22.refs_18_
  74.8 4.1 %far_second.1 = (f32[8,256]{1,0:T(8,128)S(1)}, f32[8,256]{1,0:T(8,128)S(1)}, f32[16,1,128]{2,1,0:T(1,128)S(1)}) custom-call(s32[76]{0:T(128)S(1)} %get-tuple-element.36.refs_0_, s32[76]{0:T(128)S(1)} %get-tuple-element.37.refs_1_, s32[1]{0:T(128)} %get-tuple-element.38.refs_2_, s32[60]{0:T(128)S(1)} %get-tuple-element.44.refs_3_, ...), custom_call_target="tpu_custom_call" | custom-call | flops 1000000000 | bytes 3000000 | tf_op jit(solution)/shard_map/far_second/pallas_call | solution.py:618
  78.9 12.5 %all_to_all.5.everyone = f32[16,1,128]{2,1,0:T(1,128)S(1)} all-to-all(f32[16,1,128]{2,1,0:T(1,128)S(1)} %get-tuple-element.63), channel_id=1, replica_groups=mesh['groups'=2,'leaf'=16] {'leaf'}, dimensions={0} | all-to-all | bytes 16384 | tf_op jit(solution)/shard_map/all_to_all | solution.py:485
  91.4 0.9 finish.1
  (40 shorter events, 0.1 us)
Async XLA Ops:
  0.6 18.7 %copy-start.6 = (s32[8,2]{0,1:T(2,128)S(1)}, s32[8,2]{0,1:T(2,128)}, u32[]{:S(2)}) copy-start(s32[8,2]{0,1:T(2,128)} %param.9) | copy-start | bytes 196
  0.6 18.7 %copy-start.3 = (f32[8,64,256]{2,1,0:T(8,128)S(1)}, f32[8,64,256]{2,1,0:T(8,128)}, u32[]{:S(2)}) copy-start(f32[8,64,256]{2,1,0:T(8,128)} %points.3) | copy-start | bytes 1572868
  0.7 18.7 %copy-start.2 = (f32[8,256]{1,0:T(8,128)S(1)}, f32[8,256]{1,0:T(8,128)}, u32[]{:S(2)}) copy-start(f32[8,256]{1,0:T(8,128)} %values.3) | copy-start | bytes 24580
  4.7 10.1 %collective-permute-start.11 = (f32[2,72,256]{2,1,0:T(8,128)}, f32[2,72,256]{2,1,0:T(8,128)S(1)}, u32[]{:S(2)}, u32[]{:S(2)}) collective-permute-start(f32[2,72,256]{2,1,0:T(8,128)} %get-tuple-element.39), channel_id=1, source_target_pairs={{1,0},{2,1},{3,2},{4,3},{5,4},{6,5},{7,6},{8,7},{9,8},{10,9},{11,1... | collective-permute-start | bytes 442376 | tf_op jit(solution)/shard_map/ppermute | solution.py:477
  10.2 9.1 %collective-permute-start.12 = (f32[2,72,256]{2,1,0:T(8,128)}, f32[2,72,256]{2,1,0:T(8,128)S(1)}, u32[]{:S(2)}, u32[]{:S(2)}) collective-permute-start(f32[2,72,256]{2,1,0:T(8,128)} %get-tuple-element.40), channel_id=1, source_target_pairs={{15,0},{0,1},{1,2},{2,3},{3,4},{4,5},{5,6},{6,7},{7,8},{8,9},{9,10... | collective-permute-start | bytes 442376 | tf_op jit(solution)/shard_map/ppermute | solution.py:477
  10.2 14.4 %collective-permute-start.3 = (f32[592,128]{1,0:T(8,128)}, f32[592,128]{1,0:T(8,128)S(1)}, u32[]{:S(2)}, u32[]{:S(2)}) collective-permute-start(f32[592,128]{1,0:T(8,128)} %get-tuple-element.34.refs_0_.refs_1_), channel_id=1, source_target_pairs={{12,0},{13,1},{14,2},{15,3},{0,4},{1,5},{2,6},{3,7},{4,8},{5,9},{6... | collective-permute-start | bytes 909320 | tf_op jit(solution)/shard_map/ppermute | solution.py:477
  10.2 17.5 %collective-permute-start.5 = (f32[592,128]{1,0:T(8,128)}, f32[592,128]{1,0:T(8,128)S(1)}, u32[]{:S(2)}, u32[]{:S(2)}) collective-permute-start(f32[592,128]{1,0:T(8,128)} %get-tuple-element.34.refs_0_.refs_1_), channel_id=1, source_target_pairs={{4,0},{5,1},{6,2},{7,3},{8,4},{9,5},{10,6},{11,7},{12,8},{13,9},{1... | collective-permute-start | bytes 909320 | tf_op jit(solution)/shard_map/ppermute | solution.py:477
  14.0 13.7 %collective-permute-start.1 = (f32[592,128]{1,0:T(8,128)}, f32[592,128]{1,0:T(8,128)S(1)}, u32[]{:S(2)}, u32[]{:S(2)}) collective-permute-start(f32[592,128]{1,0:T(8,128)} %get-tuple-element.34.refs_0_.refs_1_), channel_id=1, source_target_pairs={{0,2},{1,3},{2,0},{3,1},{4,6},{5,7},{6,4},{7,5},{8,10},{9,11},{10,... | collective-permute-start | bytes 909320 | tf_op jit(solution)/shard_map/ppermute | solution.py:481
  14.8 13.2 %collective-permute-start = (f32[592,128]{1,0:T(8,128)}, f32[592,128]{1,0:T(8,128)S(1)}, u32[]{:S(2)}, u32[]{:S(2)}) collective-permute-start(f32[592,128]{1,0:T(8,128)} %get-tuple-element.34.refs_0_.refs_1_), channel_id=1, source_target_pairs={{0,1},{1,0},{2,3},{3,2},{4,5},{5,4},{6,7},{7,6},{8,9},{9,8},{10,11... | collective-permute-start | bytes 909320 | tf_op jit(solution)/shard_map/ppermute | solution.py:481
  19.3 1.0 %copy-start.5 = (f32[592,128]{1,0:T(8,128)S(1)}, f32[592,128]{1,0:T(8,128)}, u32[]{:S(2)}) copy-start(f32[592,128]{1,0:T(8,128)} %get-tuple-element.41.refs_2_) | copy-start | bytes 909316
  20.3 23.9 %copy-start.4 = (f32[592,128]{1,0:T(8,128)S(1)}, f32[592,128]{1,0:T(8,128)}, u32[]{:S(2)}) copy-start(f32[592,128]{1,0:T(8,128)} %get-tuple-element.34.refs_0_.refs_1_) | copy-start | bytes 909316
  20.3 23.9 %copy-start.7 = (bf16[9,208,128]{2,1,0:T(8,128)(2,1)S(1)}, bf16[9,208,128]{2,1,0:T(8,128)(2,1)}, u32[]{:S(2)}) copy-start(bf16[9,208,128]{2,1,0:T(8,128)(2,1)} %get-tuple-element.35.refs_9_.refs_7_.refs_3_) | copy-start | bytes 1437700
  24.5 14.5 %collective-permute-start.13 = (f32[592,128]{1,0:T(8,128)S(1)}, f32[592,128]{1,0:T(8,128)S(1)}, u32[]{:S(2)}, u32[]{:S(2)}) collective-permute-start(f32[592,128]{1,0:T(8,128)S(1)} %get-tuple-element.42), channel_id=1, source_target_pairs={{8,0},{9,1},{10,2},{11,3},{12,4},{13,5},{14,6},{15,7},{0,8},{1,9},... | collective-permute-start | bytes 909320 | tf_op jit(solution)/shard_map/ppermute | solution.py:477
  24.6 14.4 %collective-permute-start.4 = (f32[592,128]{1,0:T(8,128)S(1)}, f32[592,128]{1,0:T(8,128)S(1)}, u32[]{:S(2)}, u32[]{:S(2)}) collective-permute-start(f32[592,128]{1,0:T(8,128)S(1)} %collective-permute-done.3.refs_5_), channel_id=1, source_target_pairs={{0,1},{1,0},{2,3},{3,2},{4,5},{5,4},{6,7},{7,6},{8,9},{9,8},{10,11... | collective-permute-start | bytes 909320 | tf_op jit(solution)/shard_map/ppermute | solution.py:481
  27.7 11.8 %collective-permute-start.6 = (f32[592,128]{1,0:T(8,128)S(1)}, f32[592,128]{1,0:T(8,128)S(1)}, u32[]{:S(2)}, u32[]{:S(2)}) collective-permute-start(f32[592,128]{1,0:T(8,128)S(1)} %collective-permute-done.5.refs_7_), channel_id=1, source_target_pairs={{0,1},{1,0},{2,3},{3,2},{4,5},{5,4},{6,7},{7,6},{8,9},{9,8},{10,11... | collective-permute-start | bytes 909320 | tf_op jit(solution)/shard_map/ppermute | solution.py:481
  27.7 14.1 %collective-permute-start.9 = (f32[592,128]{1,0:T(8,128)S(1)}, f32[592,128]{1,0:T(8,128)S(1)}, u32[]{:S(2)}, u32[]{:S(2)}) collective-permute-start(f32[592,128]{1,0:T(8,128)S(1)} %collective-permute-done.5.refs_7_), channel_id=1, source_target_pairs={{0,2},{1,3},{2,0},{3,1},{4,6},{5,7},{6,4},{7,5},{8,10},{9,11},{10,... | collective-permute-start | bytes 909320 | tf_op jit(solution)/shard_map/ppermute | solution.py:481
  28.0 16.2 %collective-permute-start.7 = (f32[592,128]{1,0:T(8,128)S(1)}, f32[592,128]{1,0:T(8,128)S(1)}, u32[]{:S(2)}, u32[]{:S(2)}) collective-permute-start(f32[592,128]{1,0:T(8,128)S(1)} %collective-permute-done.3.refs_5_), channel_id=1, source_target_pairs={{0,2},{1,3},{2,0},{3,1},{4,6},{5,7},{6,4},{7,5},{8,10},{9,11},{10,... | collective-permute-start | bytes 909320 | tf_op jit(solution)/shard_map/ppermute | solution.py:481
  39.0 5.2 %collective-permute-start.2 = (f32[592,128]{1,0:T(8,128)S(1)}, f32[592,128]{1,0:T(8,128)S(1)}, u32[]{:S(2)}, u32[]{:S(2)}) collective-permute-start(f32[592,128]{1,0:T(8,128)S(1)} %collective-permute-done.1.refs_3_), channel_id=1, source_target_pairs={{0,1},{1,0},{2,3},{3,2},{4,5},{5,4},{6,7},{7,6},{8,9},{9,8},{10,11... | collective-permute-start | bytes 909320 | tf_op jit(solution)/shard_map/ppermute | solution.py:481
  39.0 11.3 %collective-permute-start.14 = (f32[592,128]{1,0:T(8,128)S(1)}, f32[592,128]{1,0:T(8,128)S(1)}, u32[]{:S(2)}, u32[]{:S(2)}) collective-permute-start(f32[592,128]{1,0:T(8,128)S(1)} %collective-permute-done.13.refs_5_), channel_id=1, source_target_pairs={{0,1},{1,0},{2,3},{3,2},{4,5},{5,4},{6,7},{7,6},{8,9},{9,8},{10,11... | collective-permute-start | bytes 909320 | tf_op jit(solution)/shard_map/ppermute | solution.py:481
  39.5 10.8 %collective-permute-start.15 = (f32[592,128]{1,0:T(8,128)S(1)}, f32[592,128]{1,0:T(8,128)S(1)}, u32[]{:S(2)}, u32[]{:S(2)}) collective-permute-start(f32[592,128]{1,0:T(8,128)S(1)} %collective-permute-done.13.refs_5_), channel_id=1, source_target_pairs={{0,2},{1,3},{2,0},{3,1},{4,6},{5,7},{6,4},{7,5},{8,10},{9,11},{10,... | collective-permute-start | bytes 909320 | tf_op jit(solution)/shard_map/ppermute | solution.py:481
  41.8 8.5 %collective-permute-start.10 = (f32[592,128]{1,0:T(8,128)S(1)}, f32[592,128]{1,0:T(8,128)S(1)}, u32[]{:S(2)}, u32[]{:S(2)}) collective-permute-start(f32[592,128]{1,0:T(8,128)S(1)} %collective-permute-done.9.refs_3_), channel_id=1, source_target_pairs={{0,1},{1,0},{2,3},{3,2},{4,5},{5,4},{6,7},{7,6},{8,9},{9,8},{10,11... | collective-permute-start | bytes 909320 | tf_op jit(solution)/shard_map/ppermute | solution.py:481
  44.2 6.1 %collective-permute-start.8 = (f32[592,128]{1,0:T(8,128)S(1)}, f32[592,128]{1,0:T(8,128)S(1)}, u32[]{:S(2)}, u32[]{:S(2)}) collective-permute-start(f32[592,128]{1,0:T(8,128)S(1)} %collective-permute-done.7.refs_1_), channel_id=1, source_target_pairs={{0,1},{1,0},{2,3},{3,2},{4,5},{5,4},{6,7},{7,6},{8,9},{9,8},{10,11... | collective-permute-start | bytes 909320 | tf_op jit(solution)/shard_map/ppermute | solution.py:481
  50.3 4.0 %collective-permute-start.16 = (f32[592,128]{1,0:T(8,128)S(1)}, f32[592,128]{1,0:T(8,128)S(1)}, u32[]{:S(2)}, u32[]{:S(2)}) collective-permute-start(f32[592,128]{1,0:T(8,128)S(1)} %collective-permute-done.15.refs_1_), channel_id=1, source_target_pairs={{0,1},{1,0},{2,3},{3,2},{4,5},{5,4},{6,7},{7,6},{8,9},{9,8},{10,11... | collective-permute-start | bytes 909320 | tf_op jit(solution)/shard_map/ppermute | solution.py:481
  50.3 4.0 %copy-start = (f32[8,128,256]{2,1,0:T(8,128)S(1)}, f32[8,128,256]{2,1,0:T(8,128)}, u32[]{:S(2)}) copy-start(f32[8,128,256]{2,1,0:T(8,128)} %get-tuple-element.48.refs_5_.refs_19_) | copy-start | bytes 3145732
  50.3 4.0 %copy-start.1 = (f32[8,128,256]{2,1,0:T(8,128)S(1)}, f32[8,128,256]{2,1,0:T(8,128)}, u32[]{:S(2)}) copy-start(f32[8,128,256]{2,1,0:T(8,128)} %get-tuple-element.49.refs_6_.refs_20_) | copy-start | bytes 3145732
  57.2 10.3 %collective-permute-start.17 = (f32[24,128]{1,0:T(8,128)S(1)}, f32[24,128]{1,0:T(8,128)S(1)}, u32[]{:S(2)}, u32[]{:S(2)}) collective-permute-start(f32[24,128]{1,0:T(8,128)S(1)} %get-tuple-element.60), channel_id=1, source_target_pairs={{12,0},{13,1},{14,2},{15,3},{0,4},{1,5},{2,6},{3,7},{4,8},{5,9},{6... | collective-permute-start | bytes 36872 | tf_op jit(solution)/shard_map/ppermute | solution.py:477
  57.8 9.7 %collective-permute-start.18 = (f32[24,128]{1,0:T(8,128)S(1)}, f32[24,128]{1,0:T(8,128)S(1)}, u32[]{:S(2)}, u32[]{:S(2)}) collective-permute-start(f32[24,128]{1,0:T(8,128)S(1)} %get-tuple-element.60), channel_id=1, source_target_pairs={{8,0},{9,1},{10,2},{11,3},{12,4},{13,5},{14,6},{15,7},{0,8},{1,9},... | collective-permute-start | bytes 36872 | tf_op jit(solution)/shard_map/ppermute | solution.py:477
  64.6 4.3 %collective-permute-start.19 = (f32[24,128]{1,0:T(8,128)S(1)}, f32[24,128]{1,0:T(8,128)S(1)}, u32[]{:S(2)}, u32[]{:S(2)}) collective-permute-start(f32[24,128]{1,0:T(8,128)S(1)} %get-tuple-element.60), channel_id=1, source_target_pairs={{4,0},{5,1},{6,2},{7,3},{8,4},{9,5},{10,6},{11,7},{12,8},{13,9},{1... | collective-permute-start | bytes 36872 | tf_op jit(solution)/shard_map/ppermute | solution.py:477
  68.9 5.7 %collective-permute-start.20 = (f32[4,24,128]{2,1,0:T(8,128)S(1)}, f32[4,24,128]{2,1,0:T(8,128)S(1)}, u32[]{:S(2)}, u32[]{:S(2)}) collective-permute-start(f32[4,24,128]{2,1,0:T(8,128)S(1)} %pad_maximum_fusion.refs_15_), channel_id=1, source_target_pairs={{0,1},{1,0},{2,3},{3,2},{4,5},{5,4},{6,7},{7,6},{8,9},{9,8},{10,11... | collective-permute-start | bytes 147464 | tf_op jit(solution)/shard_map/ppermute | solution.py:481
  68.9 5.7 %collective-permute-start.21 = (f32[4,24,128]{2,1,0:T(8,128)S(1)}, f32[4,24,128]{2,1,0:T(8,128)S(1)}, u32[]{:S(2)}, u32[]{:S(2)}) collective-permute-start(f32[4,24,128]{2,1,0:T(8,128)S(1)} %pad_maximum_fusion.refs_15_), channel_id=1, source_target_pairs={{0,2},{1,3},{2,0},{3,1},{4,6},{5,7},{6,4},{7,5},{8,10},{9,11},{10,... | collective-permute-start | bytes 147464 | tf_op jit(solution)/shard_map/ppermute | solution.py:481
  71.0 3.8 %collective-permute-start.22 = (f32[4,24,128]{2,1,0:T(8,128)S(1)}, f32[4,24,128]{2,1,0:T(8,128)S(1)}, u32[]{:S(2)}, u32[]{:S(2)}) collective-permute-start(f32[4,24,128]{2,1,0:T(8,128)S(1)} %pad_maximum_fusion.refs_15_), channel_id=1, source_target_pairs={{0,3},{1,2},{2,1},{3,0},{4,7},{5,6},{6,5},{7,4},{8,11},{9,10},{10,... | collective-permute-start | bytes 147464 | tf_op jit(solution)/shard_map/ppermute | solution.py:481

commit v3 on v2

--- a/solution.py
+++ b/solution.py
@@ -13,7 +13,8 @@
 VMEM_LIMIT = 20 * 1024 * 1024
 UNROLL = 4
 GRID_DEVICES = 16
-ORDER = ((0, 0), (0, 1), (1, 0), (3, 0), (1, 1), (3, 1), (2, 0), (2, 1))
+ORDER = ((0, 0), (0, 1), (1, 0), (1, 1), (2, 0), (2, 1), (3, 0), (3, 1))
+CUTS = (0, 6, 10, 14, 16)
 
 
 def contract_first(left, right):
@@ -88,8 +89,8 @@
 
 def prepare_kernel(devices, capacity, *refs):
     (points_in, values_in, mask_in, skeleton_in, top_in, dest_in, leaf_in) = refs[:7]
-    piece, again, to_skel, to_top, lefts, first, last = refs[7:14]
-    points, values, mask, skeleton, top, dest, leaf, rights, sems = refs[14:]
+    piece, to_skel, to_top, lefts, first, last = refs[7:13]
+    points, values, mask, skeleton, top, dest, leaf, rights, sems = refs[13:]
     copies = []
     for n, (source, target) in enumerate(zip(refs[:7], (points, values, mask, skeleton, top, dest, leaf))):
         copies.append(pltpu.make_async_copy(source, target, sems.at[n]))
@@ -143,7 +144,6 @@
     piece[base + leaves:base + leaves + 8, :] = jnp.concatenate(
         [as_row(coarse), codes, jnp.zeros((6, 128), F32)], axis=0
     )
-    again[...] = piece[...]
     for r in range(reach):
         first[r, :features, :] = points[r]
         last[r, :features, :] = points[leaves - reach + r]
@@ -169,7 +169,7 @@
 def near_kernel(halo, points, values, mask, *refs):
     leaves, features, size = points.shape
     if halo:
-        following, preceding, _, out, edges, _, lefts, rights, downs, across, along = refs
+        following, preceding, out, edges, lefts, rights, downs, across, along = refs
     else:
         out, lefts, rights, downs, across, along = refs
     reach = mask.shape[0]
@@ -466,7 +466,7 @@
         input_output_aliases=aliases,
         compiler_params=pltpu.CompilerParams(vmem_limit_bytes=limit),
         cost_estimate=pl.CostEstimate(
-            flops=microseconds * 1_000_000_000, bytes_accessed=microseconds * 3_000_000, transcendentals=0
+            flops=int(microseconds * 1_000_000_000), bytes_accessed=int(microseconds * 3_000_000), transcendentals=0
         ),
         name=name,
     )
@@ -491,21 +491,6 @@
         return [exchanged(jnp.broadcast_to(block[None], (devices,) + block.shape), axis)]
     turned = jnp.stack([block] + [passed_along(block, axis, 4 * turn) for turn in (1, 2, 3)])
     return [turned] + [swapped(turned, axis, other) for other in (1, 2, 3)]
-
-
-def all_pieces(piece, again, axis):
-    devices = lax.axis_size(axis)
-    if devices != GRID_DEVICES:
-        together = lax.all_gather(piece[None], axis, axis=0, tiled=True)
-        return [together[n] for n in range(devices)]
-    turned = {0: piece}
-    for turn in (1, 3, 2):
-        turned[turn] = passed_along(again if turn == 2 else piece, axis, 4 * turn)
-    pieces = []
-    for turn, across in ORDER:
-        mine = swapped(turned[turn], axis, 2) if across else turned[turn]
-        pieces += [mine, swapped(mine, axis, 1)]
-    return pieces
 
 
 def on_device(points, right_side, near_mask, far_dest, far_leaf, skeleton, top_index):
@@ -521,12 +506,11 @@
     integers = jnp.int32
     payload_rows = 16 + 2 * reach * size // rank
 
-    piece, again, to_skel, to_top, lefts, first, last = kernel_call(
+    piece, to_skel, to_top, lefts, first, last = kernel_call(
         functools.partial(prepare_kernel, devices, capacity),
         "prepare",
         [HBM] * 7,
         [
-            (VMEM, shape(piece_rows, rank)),
             (VMEM, shape(piece_rows, rank)),
             (VMEM, shape(leaves, rank, size)),
             (VMEM, shape(leaves, rank, size)),
@@ -556,11 +540,10 @@
         outputs = [(VMEM, shape(leaves, size))]
         if halo:
             outputs.append((VMEM, shape(len(before) + len(after), size, size)))
-            outputs.append((ANY, shape(piece_rows, rank)))
         return kernel_call(
             functools.partial(near_kernel, halo),
             "near_first" if halo else "near_second",
-            [VMEM, VMEM, SMEM] + [VMEM, VMEM, ANY][:len(others)],
+            [VMEM, VMEM, SMEM] + [VMEM] * len(others),
             outputs,
             [
                 pltpu.VMEM((leaves + reach, depth, size), BF16),
@@ -569,14 +552,17 @@
                 pltpu.VMEM((leaves, size, 128), F32),
                 pltpu.VMEM((leaves, 8, size), F32),
             ],
-            {5: 2} if halo else {},
-            microseconds=5,
+            microseconds=3 if halo else 4,
         )(points, values, near_mask.T, *others)
 
-    near, edges, again = near_apply(True, right_side, following, preceding, again)
-    pieces = all_pieces(piece, again, "leaf")
-    cuts = (0, devices // 2, devices * 7 // 8, devices)
+    near, edges = near_apply(True, right_side, following, preceding)
+    cuts = [devices * cut // GRID_DEVICES for cut in CUTS]
     groups = [tuple(range(start, end)) for start, end in zip(cuts, cuts[1:])]
+    if devices == GRID_DEVICES:
+        pieces = {}
+    else:
+        together = lax.all_gather(piece[None], "leaf", axis=0, tiled=True)
+        pieces = {place: together[place] for place in range(devices)}
     sums = shape(leaves + 2, rank, rank)
 
     def group_call(body, name, places, inputs, outputs, scratch):
@@ -598,19 +584,52 @@
                 pltpu.SMEM((len(places) + 1, 8, 128), F32),
                 pltpu.SemaphoreType.DMA((len(places) + 1,)),
             ],
-            microseconds=1 + len(places),
+            microseconds={0: 7, 6: 5, 10: 3}.get(places[0], 3),
         )(piece, *[pieces[place] for place in places], lefts, *inputs)
 
-    early = group_call(early_kernel, "far_early", groups[0], [], [(VMEM, sums)], [])
-    middle = group_call(early_kernel, "far_middle", groups[1], [early[5]], [(VMEM, sums)], [])
+    def hold(value, *others):
+        return lax.optimization_barrier((value, *others))[0]
+
+    def put(slot, value):
+        pieces[2 * slot] = value
+        pieces[2 * slot + 1] = swapped(value, "leaf", 1)
+
+    passes = []
+
+    def tiles_of_group():
+        number = len(passes)
+        start = [passes[-1][5]] if passes else []
+        passes.append(
+            group_call(early_kernel, "far_tiles_%d" % number, groups[number], start, [(VMEM, sums)], [])
+        )
+        return passes[-1][5]
+
+    if devices == GRID_DEVICES:
+        put(0, piece)
+        put(1, swapped(piece, "leaf", 2))
+        turned = passed_along(piece, "leaf", 4)
+        put(2, turned)
+        across = swapped(turned, "leaf", 2)
+        turned = hold(passed_along(turned, "leaf", 4), tiles_of_group())
+        put(3, across)
+        put(4, turned)
+        across = swapped(turned, "leaf", 2)
+        turned = hold(passed_along(turned, "leaf", 4), tiles_of_group())
+        put(5, across)
+        put(6, turned)
+        put(7, hold(swapped(turned, "leaf", 2), tiles_of_group(), near))
+    else:
+        for _ in groups[:-1]:
+            tiles_of_group()
     late = group_call(
         functools.partial(first_kernel, reach),
-        "far_late",
-        groups[2],
-        [middle[5], to_skel, to_top, right_side, near],
+        "far_last",
+        groups[3],
+        [passes[-1][5], to_skel, to_top, right_side, near],
         [(VMEM, shape(leaves, size)), (VMEM, shape(payload_rows, rank))],
         [pltpu.VMEM(sums.shape, F32)],
     )
+    passes.append(late)
     image, payload = late[5:]
 
     everyone = gathered_blocks(payload, "leaf")
@@ -618,7 +637,7 @@
     residual, along, numbers = kernel_call(
         functools.partial(second_kernel, reach, "leaf", devices, groups),
         "far_second",
-        [SMEM] * 9 + [VMEM] * (12 + len(everyone)),
+        [SMEM] * (3 * len(groups)) + [VMEM] * (2 * len(groups) + 6 + len(everyone)),
         [
             (VMEM, shape(leaves, size)),
             (VMEM, shape(leaves, size)),
@@ -631,7 +650,9 @@
             pltpu.VMEM((reach, 8, size), F32),
         ],
     )(
-        *early[:3], *middle[:3], *late[:3], early[3], middle[3], late[3], early[4], middle[4], late[4],
+        *[table for done in passes for table in done[:3]],
+        *[done[3] for done in passes],
+        *[done[4] for done in passes],
         *everyone, to_skel, to_top, right_side, image, near_second, edges,
     )
 

time: 91.7 us -> 84.4 us (0.920)
  starting transfers between devices: 27 us -> 16.8 us
  waiting for transfers between devices: 21.9 us -> 26.4 us
  blocking collectives: 12.5 us -> 10.1 us
  local copies, waits for them, and re-layouts: 0.99 us -> 2.01 us
    ppermute x8, starting transfers between devices: 19.7 us -> 8.89 us  [passed_along(): lax.ppermute(block, axis, [((i - distance) % size, i) for i in range(size)])]
    ppermute x8, waiting for transfers between devices: 18.7 us -> 21.8 us  [passed_along(): lax.ppermute(block, axis, [((i - distance) % size, i) for i in range(size)])]
    pallas_call x2, Pallas kernels: 7.68 us -> 4.86 us  [near_apply(): kernel_call(functools.partial(near_kernel, halo), 'near_first' if halo el...]
    all_to_all x1, blocking collectives: 12.5 us -> 10.1 us  [exchanged(): return lax.all_to_all(blocks, axis, split_axis=0, concat_axis=0, tiled=True)]
    pallas_call x3 -> x4, Pallas kernels: 12.3 us -> 13.7 us  [group_call(): kernel_call(functools.partial(body, 'leaf', devices, capacity, places), n...]
    ppermute x15, waiting for transfers between devices: 3.2 us -> 4.61 us  [swapped(): lax.ppermute(block, axis, [(i, i ^ bit) for i in range(lax.axis_size(axis...]
    unnamed x16 -> x20, local copies, waits for them, and re-layouts: 0.99 us -> 2.01 us
  transfers between devices with their start and end apart: 23 -> 23, of which waited for: 8 -> 10; matrix products, arithmetic and copies ran while one was open for 0% -> 0% of each run, Pallas kernels for 19% -> 19%
where the time goes in v3:
time: 84.4 us; the launch traced here: 84.3 us
  Pallas kernels  28.1 us (33%)
  waiting for transfers between devices  26.4 us (31%)
  starting transfers between devices  16.8 us (20%)
  blocking collectives  10.1 us (12%)
  local copies, waits for them, and re-layouts  2.01 us (2%)
    ppermute x8, waiting for transfers between devices, passed_along(): lax.ppermute(block, axis, [((i - distance) % size, i) for i in range(size)])  21.8 us
    pallas_call x4, Pallas kernels, group_call(): kernel_call(functools.partial(body, 'leaf', devices, capacity, places), n...  13.7 us
    all_to_all x1, blocking collectives, exchanged(): return lax.all_to_all(blocks, axis, split_axis=0, concat_axis=0, tiled=True)  10.1 us
    ppermute x8, starting transfers between devices, passed_along(): lax.ppermute(block, axis, [((i - distance) % size, i) for i in range(size)])  8.89 us
    ppermute x15, starting transfers between devices, swapped(): lax.ppermute(block, axis, [(i, i ^ bit) for i in range(lax.axis_size(axis...  7.93 us
    pallas_call x2, Pallas kernels, near_apply(): kernel_call(functools.partial(near_kernel, halo), 'near_first' if halo el...  4.86 us
    pallas_call x1, Pallas kernels, on_device(): kernel_call(functools.partial(second_kernel, reach, 'leaf', devices, grou...  4.84 us
    ppermute x15, waiting for transfers between devices, swapped(): lax.ppermute(block, axis, [(i, i ^ bit) for i in range(lax.axis_size(axis...  4.61 us
  transfers between devices with their start and end apart: 23, of which 10 were waited for; matrix products, arithmetic and copies ran while one was open for 0% of the time, Pallas kernels for 19%

profile of v3, /device:TPU:0, one launch (start us, length us, event | category | flops | bytes accessed | tf_op | source)
XLA Modules:
  0.0 84.3 jit_solution(16148643565941521611)
XLA Ops:
  0.6 3.8 %prepare.1 = (f32[592,128]{1,0:T(8,128)}, f32[8,128,256]{2,1,0:T(8,128)}, f32[8,128,256]{2,1,0:T(8,128)}, bf16[9,208,128]{2,1,0:T(8,128)(2,1)}, f32[2,72,256]{2,1,0:T(8,128)}, /*index=5*/f32[2,72,256]{2,1,0:T(8,128)}) custom-call(f32[8,64,256]{2,1,0:T(8,128)} %points.3, f32[8,256]{1,0:T(8,128)} %values.3, s32[2,8]{1,0:T(2,128)} %bitcast.8, ...), custom_call_target="tpu_custom_call" | custom-call | flops 2000000000 | bytes 6000000 | tf_op jit(solution)/shard_map/prepare/pallas_call | solution.py:509
  4.4 3.1 %collective-permute-start.3 = (f32[592,128]{1,0:T(8,128)}, f32[592,128]{1,0:T(8,128)S(1)}, u32[]{:S(2)}, u32[]{:S(2)}) collective-permute-start(f32[592,128]{1,0:T(8,128)} %get-tuple-element.41.refs_0_.refs_1_), channel_id=1, source_target_pairs={{12,0},{13,1},{14,2},{15,3},{0,4},{1,5},{2,6},{3,7},{4,8},{5,9},{6... | collective-permute-start | bytes 909320 | tf_op jit(solution)/shard_map/ppermute | solution.py:477
  7.5 1.5 %collective-permute-start.1 = (f32[592,128]{1,0:T(8,128)}, f32[592,128]{1,0:T(8,128)S(1)}, u32[]{:S(2)}, u32[]{:S(2)}) collective-permute-start(f32[592,128]{1,0:T(8,128)} %get-tuple-element.41.refs_0_.refs_1_), channel_id=1, source_target_pairs={{0,2},{1,3},{2,0},{3,1},{4,6},{5,7},{6,4},{7,5},{8,10},{9,11},{10,... | collective-permute-start | bytes 909320 | tf_op jit(solution)/shard_map/ppermute | solution.py:481
  9.0 7.9 %collective-permute-done.3.refs_5_ = f32[592,128]{1,0:T(8,128)S(1)} collective-permute-done((f32[592,128]{1,0:T(8,128)}, f32[592,128]{1,0:T(8,128)S(1)}, u32[]{:S(2)}, u32[]{:S(2)}) %collective-permute-start.3) | collective-permute-done | bytes 303136 | tf_op jit(solution)/shard_map/ppermute | solution.py:477
  16.9 0.5 collective-permute-start.2
  18.0 1.5 %collective-permute-start.5 = (f32[592,128]{1,0:T(8,128)S(1)}, f32[592,128]{1,0:T(8,128)S(1)}, u32[]{:S(2)}, u32[]{:S(2)}) collective-permute-start(f32[592,128]{1,0:T(8,128)S(1)} %collective-permute-done.3.refs_5_), channel_id=1, source_target_pairs={{0,2},{1,3},{2,0},{3,1},{4,6},{5,7},{6,4},{7,5},{8,10},{9,11},{10,... | collective-permute-start | bytes 909320 | tf_op jit(solution)/shard_map/ppermute | solution.py:481
  19.5 1.0 %copy-done.4 = f32[592,128]{1,0:T(8,128)S(1)} copy-done((f32[592,128]{1,0:T(8,128)S(1)}, f32[592,128]{1,0:T(8,128)}, u32[]{:S(2)}) %copy-start.4) | copy-done | bytes 303128
  20.5 1.0 %copy-done.6 = bf16[9,208,128]{2,1,0:T(8,128)(2,1)S(1)} copy-done((bf16[9,208,128]{2,1,0:T(8,128)(2,1)S(1)}, bf16[9,208,128]{2,1,0:T(8,128)(2,1)}, u32[]{:S(2)}) %copy-start.6) | copy-done | bytes 479256
  21.5 4.6 %far_tiles_0.1 = (s32[60]{0:T(128)S(1)}, s32[60]{0:T(128)S(1)}, s32[1]{0:T(128)}, f32[60,128,128]{2,1,0:T(8,128)S(1)}, f32[6,128,128]{2,1,0:T(8,128)S(1)}, /*index=5*/f32[10,128,128]{2,1,0:T(8,128)S(1)}) custom-call(f32[592,128]{1,0:T(8,128)S(1)} %copy-done.4, f32[592,128]{1,0:T(8,128)S(1)} %copy-done.4, f32[592,128]{1,0:T(8,128)S(1)} %collective-permute-done.refs_2_, ...), custom_call_target="tpu_custom_call" | custom-call | flops 7000000000 | bytes 21000000 | tf_op jit(solution)/shard_map/far_tiles_0/pallas_call | solution.py:570
  26.1 2.3 %collective-permute-done.7.refs_3_ = f32[592,128]{1,0:T(8,128)S(1)} collective-permute-done((f32[592,128]{1,0:T(8,128)S(1)}, f32[592,128]{1,0:T(8,128)S(1)}, u32[]{:S(2)}, u32[]{:S(2)}) %collective-permute-start.7) | collective-permute-done | bytes 303136 | tf_op jit(solution)/shard_map/ppermute | solution.py:477
  28.3 0.5 collective-permute-start.8
  28.9 2.3 %collective-permute-start.14 = (f32[2,72,256]{2,1,0:T(8,128)S(1)}, f32[2,72,256]{2,1,0:T(8,128)S(1)}, u32[]{:S(2)}, u32[]{:S(2)}) collective-permute-start(f32[2,72,256]{2,1,0:T(8,128)S(1)} %copy-done.9), channel_id=1, source_target_pairs={{1,0},{2,1},{3,2},{4,3},{5,4},{6,5},{7,6},{8,7},{9,8},{10,9},{11,1... | collective-permute-start | bytes 442376 | tf_op jit(solution)/shard_map/ppermute | solution.py:477
  31.6 3.1 %far_tiles_1.1 = (s32[44]{0:T(128)S(1)}, s32[44]{0:T(128)S(1)}, s32[1]{0:T(128)}, f32[44,128,128]{2,1,0:T(8,128)S(1)}, f32[4,128,128]{2,1,0:T(8,128)S(1)}, /*index=5*/f32[10,128,128]{2,1,0:T(8,128)S(1)}) custom-call(f32[592,128]{1,0:T(8,128)S(1)} %copy-done.4, f32[592,128]{1,0:T(8,128)S(1)} %collective-permute-done.5.refs_1_, ...), custom_call_target="tpu_custom_call" | custom-call | flops 5000000000 | bytes 15000000 | tf_op jit(solution)/shard_map/far_tiles_1/pallas_call | solution.py:570
  34.7 6.9 %collective-permute-done.11.refs_3_ = f32[592,128]{1,0:T(8,128)S(1)} collective-permute-done((f32[592,128]{1,0:T(8,128)S(1)}, f32[592,128]{1,0:T(8,128)S(1)}, u32[]{:S(2)}, u32[]{:S(2)}) %collective-permute-start.11) | collective-permute-done | bytes 303136 | tf_op jit(solution)/shard_map/ppermute | solution.py:477
  41.6 0.7 collective-permute-done.9.refs_1_
  42.2 0.5 collective-permute-start.12
  42.8 1.5 %collective-permute-start.13 = (f32[592,128]{1,0:T(8,128)S(1)}, f32[592,128]{1,0:T(8,128)S(1)}, u32[]{:S(2)}, u32[]{:S(2)}) collective-permute-start(f32[592,128]{1,0:T(8,128)S(1)} %collective-permute-done.11.refs_3_), channel_id=1, source_target_pairs={{0,2},{1,3},{2,0},{3,1},{4,6},{5,7},{6,4},{7,5},{8,10},{9,11},{10,... | collective-permute-start | bytes 909320 | tf_op jit(solution)/shard_map/ppermute | solution.py:481
  44.3 2.6 %near_first.1 = (f32[8,256]{1,0:T(8,128)S(1)}, f32[6,256,256]{2,1,0:T(8,128)S(1)}) custom-call(f32[8,64,256]{2,1,0:T(8,128)S(1)} %copy-done.3, f32[8,256]{1,0:T(8,128)S(1)} %copy-done.2, s32[2,8]{1,0:T(2,128)S(1)} %bitcast.9, f32[2,72,256]{2,1,0:T(8,128)S(1)} %collective-permute-done.14.refs_0_, f32[2,72,256]{2,1,0:T(8,128)S(1)} %collective-permute-done.15.refs_1_), custom_call_target="tpu_custom_call" | custom-call | flops 3000000000 | bytes 9000000 | tf_op jit(solution)/shard_map/near_first/pallas_call | solution.py:543
  46.9 3.3 %far_tiles_2.1 = (s32[44]{0:T(128)S(1)}, s32[44]{0:T(128)S(1)}, s32[1]{0:T(128)}, f32[44,128,128]{2,1,0:T(8,128)S(1)}, f32[4,128,128]{2,1,0:T(8,128)S(1)}, /*index=5*/f32[10,128,128]{2,1,0:T(8,128)S(1)}) custom-call(f32[592,128]{1,0:T(8,128)S(1)} %copy-done.4, f32[592,128]{1,0:T(8,128)S(1)} %collective-permute-done.9.refs_1_, ...), custom_call_target="tpu_custom_call" | custom-call | flops 3000000000 | bytes 9000000 | tf_op jit(solution)/shard_map/far_tiles_2/pallas_call | solution.py:570
  50.3 1.8 %collective-permute-done.13.refs_1_ = f32[592,128]{1,0:T(8,128)S(1)} collective-permute-done((f32[592,128]{1,0:T(8,128)S(1)}, f32[592,128]{1,0:T(8,128)S(1)}, u32[]{:S(2)}, u32[]{:S(2)}) %collective-permute-start.13) | collective-permute-done | bytes 303136 | tf_op jit(solution)/shard_map/ppermute | solution.py:481
  52.1 1.6 %collective-permute-done.16.refs_2_ = f32[592,128]{1,0:T(8,128)S(1)} collective-permute-done((f32[592,128]{1,0:T(8,128)S(1)}, f32[592,128]{1,0:T(8,128)S(1)}, u32[]{:S(2)}, u32[]{:S(2)}) %collective-permute-start.16) | collective-permute-done | bytes 303136 | tf_op jit(solution)/shard_map/ppermute | solution.py:481
  53.7 2.8 %far_last.1 = (s32[28]{0:T(128)S(1)}, s32[28]{0:T(128)S(1)}, s32[1]{0:T(128)}, f32[28,128,128]{2,1,0:T(8,128)S(1)}, f32[2,128,128]{2,1,0:T(8,128)S(1)}, /*index=5*/f32[8,256]{1,0:T(8,128)S(1)}, f32[24,128]{1,0:T(8,128)S(1)}) custom-call(f32[592,128]{1,0:T(8,128)S(1)} %copy-done.4, f32[592,128]{1,0:T(8,128)S(1)} %collective-permute-done.13.refs_1_, ...), custom_call_target="tpu_custom_call" | custom-call | flops 3000000000 | bytes 9000000 | tf_op jit(solution)/shard_map/far_last/pallas_call | solution.py:570
  56.5 1.8 %collective-permute-start.19 = (f32[24,128]{1,0:T(8,128)S(1)}, f32[24,128]{1,0:T(8,128)S(1)}, u32[]{:S(2)}, u32[]{:S(2)}) collective-permute-start(f32[24,128]{1,0:T(8,128)S(1)} %get-tuple-element.74), channel_id=1, source_target_pairs={{4,0},{5,1},{6,2},{7,3},{8,4},{9,5},{10,6},{11,7},{12,8},{13,9},{1... | collective-permute-start | bytes 36872 | tf_op jit(solution)/shard_map/ppermute | solution.py:477
  58.3 0.8 collective-permute-start.17
  59.1 1.1 %collective-permute-done.19 = f32[24,128]{1,0:T(8,128)S(1)} collective-permute-done((f32[24,128]{1,0:T(8,128)S(1)}, f32[24,128]{1,0:T(8,128)S(1)}, u32[]{:S(2)}, u32[]{:S(2)}) %collective-permute-start.19) | collective-permute-done | bytes 12320 | tf_op jit(solution)/shard_map/ppermute | solution.py:477
  60.2 2.7 %collective-permute-done.18 = f32[24,128]{1,0:T(8,128)S(1)} collective-permute-done((f32[24,128]{1,0:T(8,128)S(1)}, f32[24,128]{1,0:T(8,128)S(1)}, u32[]{:S(2)}, u32[]{:S(2)}) %collective-permute-start.18) | collective-permute-done | bytes 12320 | tf_op jit(solution)/shard_map/ppermute | solution.py:477
  62.9 0.9 %collective-permute-done.17 = f32[24,128]{1,0:T(8,128)S(1)} collective-permute-done((f32[24,128]{1,0:T(8,128)S(1)}, f32[24,128]{1,0:T(8,128)S(1)}, u32[]{:S(2)}, u32[]{:S(2)}) %collective-permute-start.17) | collective-permute-done | bytes 12320 | tf_op jit(solution)/shard_map/ppermute | solution.py:477
  63.8 1.8 %collective-permute-start.21 = (f32[4,24,128]{2,1,0:T(8,128)S(1)}, f32[4,24,128]{2,1,0:T(8,128)S(1)}, u32[]{:S(2)}, u32[]{:S(2)}) collective-permute-start(f32[4,24,128]{2,1,0:T(8,128)S(1)} %pad_maximum_fusion.refs_20_), channel_id=1, source_target_pairs={{0,2},{1,3},{2,0},{3,1},{4,6},{5,7},{6,4},{7,5},{8,10},{9,11},{10,... | collective-permute-start | bytes 147464 | tf_op jit(solution)/shard_map/ppermute | solution.py:481
  65.7 2.3 %near_second.1.refs_28_ = f32[8,256]{1,0:T(8,128)S(1)} custom-call(f32[8,64,256]{2,1,0:T(8,128)S(1)} %copy-done.3, f32[8,256]{1,0:T(8,128)S(1)} %get-tuple-element.75.values.refs_27_.image, s32[2,8]{1,0:T(2,128)S(1)} %bitcast.10), custom_call_target="tpu_custom_call" | custom-call | flops 4000000000 | bytes 12000000 | tf_op jit(solution)/shard_map/near_second/pallas_call | solution.py:543
  68.4 4.8 %far_second.1 = (f32[8,256]{1,0:T(8,128)S(1)}, f32[8,256]{1,0:T(8,128)S(1)}, f32[16,1,128]{2,1,0:T(1,128)S(1)}) custom-call(s32[60]{0:T(128)S(1)} %get-tuple-element.43.refs_0_, s32[60]{0:T(128)S(1)} %get-tuple-element.44.refs_1_, s32[1]{0:T(128)} %get-tuple-element.45.refs_2_, s32[44]{0:T(128)S(1)} %get-tuple-element.48.refs_3_, ...), custom_call_target="tpu_custom_call" | custom-call | flops 1000000000 | bytes 3000000 | tf_op jit(solution)/shard_map/far_second/pallas_call | solution.py:637
  73.3 10.1 %all_to_all.5.everyone = f32[16,1,128]{2,1,0:T(1,128)S(1)} all-to-all(f32[16,1,128]{2,1,0:T(1,128)S(1)} %get-tuple-element.77), channel_id=1, replica_groups=mesh['groups'=2,'leaf'=16] {'leaf'}, dimensions={0} | all-to-all | bytes 16384 | tf_op jit(solution)/shard_map/all_to_all | solution.py:485
  83.4 0.9 %finish.1 = (f32[8,256]{1,0:T(8,128)}, f32[8,256]{1,0:T(8,128)}) custom-call(f32[16,1,128]{2,1,0:T(1,128)S(1)} %all_to_all.5.everyone, f32[8,256]{1,0:T(8,128)S(1)} %copy-done.2, f32[8,256]{1,0:T(8,128)S(1)} %get-tuple-element.75.values.refs_27_.image, f32[8,256]{1,0:T(8,128)S(1)} %get-tuple-element.78.residual, f32[8,256]{1,0:T(8,128)S(1)} %get-tuple-element.79.along), custom_call_target="tpu_custom_call" | custom-call | flops 1000000000 | bytes 3000000 | tf_op jit(solution)/shard_map/finish/pallas_call | solution.py:659
  (45 shorter events, 1.6 us)
Async XLA Ops:
  4.4 12.5 %collective-permute-start.3 = (f32[592,128]{1,0:T(8,128)}, f32[592,128]{1,0:T(8,128)S(1)}, u32[]{:S(2)}, u32[]{:S(2)}) collective-permute-start(f32[592,128]{1,0:T(8,128)} %get-tuple-element.41.refs_0_.refs_1_), channel_id=1, source_target_pairs={{12,0},{13,1},{14,2},{15,3},{0,4},{1,5},{2,6},{3,7},{4,8},{5,9},{6... | collective-permute-start | bytes 909320 | tf_op jit(solution)/shard_map/ppermute | solution.py:477
  7.5 9.4 %collective-permute-start.1 = (f32[592,128]{1,0:T(8,128)}, f32[592,128]{1,0:T(8,128)S(1)}, u32[]{:S(2)}, u32[]{:S(2)}) collective-permute-start(f32[592,128]{1,0:T(8,128)} %get-tuple-element.41.refs_0_.refs_1_), channel_id=1, source_target_pairs={{0,2},{1,3},{2,0},{3,1},{4,6},{5,7},{6,4},{7,5},{8,10},{9,11},{10,... | collective-permute-start | bytes 909320 | tf_op jit(solution)/shard_map/ppermute | solution.py:481
  9.0 10.4 %collective-permute-start = (f32[592,128]{1,0:T(8,128)}, f32[592,128]{1,0:T(8,128)S(1)}, u32[]{:S(2)}, u32[]{:S(2)}) collective-permute-start(f32[592,128]{1,0:T(8,128)} %get-tuple-element.41.refs_0_.refs_1_), channel_id=1, source_target_pairs={{0,1},{1,0},{2,3},{3,2},{4,5},{5,4},{6,7},{7,6},{8,9},{9,8},{10,11... | collective-permute-start | bytes 909320 | tf_op jit(solution)/shard_map/ppermute | solution.py:481
  16.9 2.5 %collective-permute-start.4 = (f32[592,128]{1,0:T(8,128)S(1)}, f32[592,128]{1,0:T(8,128)S(1)}, u32[]{:S(2)}, u32[]{:S(2)}) collective-permute-start(f32[592,128]{1,0:T(8,128)S(1)} %collective-permute-done.3.refs_5_), channel_id=1, source_target_pairs={{0,1},{1,0},{2,3},{3,2},{4,5},{5,4},{6,7},{7,6},{8,9},{9,8},{10,11... | collective-permute-start | bytes 909320 | tf_op jit(solution)/shard_map/ppermute | solution.py:481
  16.9 2.5 %collective-permute-start.2 = (f32[592,128]{1,0:T(8,128)S(1)}, f32[592,128]{1,0:T(8,128)S(1)}, u32[]{:S(2)}, u32[]{:S(2)}) collective-permute-start(f32[592,128]{1,0:T(8,128)S(1)} %collective-permute-done.1.refs_3_), channel_id=1, source_target_pairs={{0,1},{1,0},{2,3},{3,2},{4,5},{5,4},{6,7},{7,6},{8,9},{9,8},{10,11... | collective-permute-start | bytes 909320 | tf_op jit(solution)/shard_map/ppermute | solution.py:481
  17.4 10.9 %collective-permute-start.7 = (f32[592,128]{1,0:T(8,128)S(1)}, f32[592,128]{1,0:T(8,128)S(1)}, u32[]{:S(2)}, u32[]{:S(2)}) collective-permute-start(f32[592,128]{1,0:T(8,128)S(1)} %collective-permute-done.3.refs_5_), channel_id=1, source_target_pairs={{12,0},{13,1},{14,2},{15,3},{0,4},{1,5},{2,6},{3,7},{4,8},{5,9},{6... | collective-permute-start | bytes 909320 | tf_op jit(solution)/shard_map/ppermute | solution.py:477
  18.0 10.4 %collective-permute-start.5 = (f32[592,128]{1,0:T(8,128)S(1)}, f32[592,128]{1,0:T(8,128)S(1)}, u32[]{:S(2)}, u32[]{:S(2)}) collective-permute-start(f32[592,128]{1,0:T(8,128)S(1)} %collective-permute-done.3.refs_5_), channel_id=1, source_target_pairs={{0,2},{1,3},{2,0},{3,1},{4,6},{5,7},{6,4},{7,5},{8,10},{9,11},{10,... | collective-permute-start | bytes 909320 | tf_op jit(solution)/shard_map/ppermute | solution.py:481
  20.4 1.0 %copy-start.6 = (bf16[9,208,128]{2,1,0:T(8,128)(2,1)S(1)}, bf16[9,208,128]{2,1,0:T(8,128)(2,1)}, u32[]{:S(2)}) copy-start(bf16[9,208,128]{2,1,0:T(8,128)(2,1)} %get-tuple-element.42.refs_7_.refs_5_.refs_3_) | copy-start | bytes 1437700
  21.5 7.4 %copy-start.9 = (f32[2,72,256]{2,1,0:T(8,128)S(1)}, f32[2,72,256]{2,1,0:T(8,128)}, u32[]{:S(2)}) copy-start(f32[2,72,256]{2,1,0:T(8,128)} %get-tuple-element.57) | copy-start | bytes 442372
  21.5 9.7 %copy-start.8 = (f32[2,72,256]{2,1,0:T(8,128)S(1)}, f32[2,72,256]{2,1,0:T(8,128)}, u32[]{:S(2)}) copy-start(f32[2,72,256]{2,1,0:T(8,128)} %get-tuple-element.58) | copy-start | bytes 442372
  28.3 3.2 %collective-permute-start.6 = (f32[592,128]{1,0:T(8,128)S(1)}, f32[592,128]{1,0:T(8,128)S(1)}, u32[]{:S(2)}, u32[]{:S(2)}) collective-permute-start(f32[592,128]{1,0:T(8,128)S(1)} %collective-permute-done.5.refs_1_), channel_id=1, source_target_pairs={{0,1},{1,0},{2,3},{3,2},{4,5},{5,4},{6,7},{7,6},{8,9},{9,8},{10,11... | collective-permute-start | bytes 909320 | tf_op jit(solution)/shard_map/ppermute | solution.py:481
  28.3 3.2 %collective-permute-start.8 = (f32[592,128]{1,0:T(8,128)S(1)}, f32[592,128]{1,0:T(8,128)S(1)}, u32[]{:S(2)}, u32[]{:S(2)}) collective-permute-start(f32[592,128]{1,0:T(8,128)S(1)} %collective-permute-done.7.refs_3_), channel_id=1, source_target_pairs={{0,1},{1,0},{2,3},{3,2},{4,5},{5,4},{6,7},{7,6},{8,9},{9,8},{10,11... | collective-permute-start | bytes 909320 | tf_op jit(solution)/shard_map/ppermute | solution.py:481
  28.9 15.4 %collective-permute-start.14 = (f32[2,72,256]{2,1,0:T(8,128)S(1)}, f32[2,72,256]{2,1,0:T(8,128)S(1)}, u32[]{:S(2)}, u32[]{:S(2)}) collective-permute-start(f32[2,72,256]{2,1,0:T(8,128)S(1)} %copy-done.9), channel_id=1, source_target_pairs={{1,0},{2,1},{3,2},{4,3},{5,4},{6,5},{7,6},{8,7},{9,8},{10,9},{11,1... | collective-permute-start | bytes 442376 | tf_op jit(solution)/shard_map/ppermute | solution.py:477
  31.2 13.1 %copy-start.2 = (f32[8,256]{1,0:T(8,128)S(1)}, f32[8,256]{1,0:T(8,128)}, u32[]{:S(2)}) copy-start(f32[8,256]{1,0:T(8,128)} %values.3) | copy-start | bytes 24580
  31.2 13.1 %copy-start.3 = (f32[8,64,256]{2,1,0:T(8,128)S(1)}, f32[8,64,256]{2,1,0:T(8,128)}, u32[]{:S(2)}) copy-start(f32[8,64,256]{2,1,0:T(8,128)} %points.3) | copy-start | bytes 1572868
  31.2 13.1 %copy-start.5 = (s32[8,2]{0,1:T(2,128)S(1)}, s32[8,2]{0,1:T(2,128)}, u32[]{:S(2)}) copy-start(s32[8,2]{0,1:T(2,128)} %param.9) | copy-start | bytes 196
  31.2 13.0 %collective-permute-start.15 = (f32[2,72,256]{2,1,0:T(8,128)S(1)}, f32[2,72,256]{2,1,0:T(8,128)S(1)}, u32[]{:S(2)}, u32[]{:S(2)}) collective-permute-start(f32[2,72,256]{2,1,0:T(8,128)S(1)} %copy-done.8), channel_id=1, source_target_pairs={{15,0},{0,1},{1,2},{2,3},{3,4},{4,5},{5,6},{6,7},{7,8},{8,9},{9,10... | collective-permute-start | bytes 442376 | tf_op jit(solution)/shard_map/ppermute | solution.py:477
  31.2 10.3 %collective-permute-start.11 = (f32[592,128]{1,0:T(8,128)S(1)}, f32[592,128]{1,0:T(8,128)S(1)}, u32[]{:S(2)}, u32[]{:S(2)}) collective-permute-start(f32[592,128]{1,0:T(8,128)S(1)} %collective-permute-done.7.refs_3_), channel_id=1, source_target_pairs={{12,0},{13,1},{14,2},{15,3},{0,4},{1,5},{2,6},{3,7},{4,8},{5,9},{6... | collective-permute-start | bytes 909320 | tf_op jit(solution)/shard_map/ppermute | solution.py:477
  31.6 10.7 %collective-permute-start.9 = (f32[592,128]{1,0:T(8,128)S(1)}, f32[592,128]{1,0:T(8,128)S(1)}, u32[]{:S(2)}, u32[]{:S(2)}) collective-permute-start(f32[592,128]{1,0:T(8,128)S(1)} %collective-permute-done.7.refs_3_), channel_id=1, source_target_pairs={{0,2},{1,3},{2,0},{3,1},{4,6},{5,7},{6,4},{7,5},{8,10},{9,11},{10,... | collective-permute-start | bytes 909320 | tf_op jit(solution)/shard_map/ppermute | solution.py:481
  42.2 4.6 %collective-permute-start.10 = (f32[592,128]{1,0:T(8,128)S(1)}, f32[592,128]{1,0:T(8,128)S(1)}, u32[]{:S(2)}, u32[]{:S(2)}) collective-permute-start(f32[592,128]{1,0:T(8,128)S(1)} %collective-permute-done.9.refs_1_), channel_id=1, source_target_pairs={{0,1},{1,0},{2,3},{3,2},{4,5},{5,4},{6,7},{7,6},{8,9},{9,8},{10,11... | collective-permute-start | bytes 909320 | tf_op jit(solution)/shard_map/ppermute | solution.py:481
  42.2 4.6 %collective-permute-start.12 = (f32[592,128]{1,0:T(8,128)S(1)}, f32[592,128]{1,0:T(8,128)S(1)}, u32[]{:S(2)}, u32[]{:S(2)}) collective-permute-start(f32[592,128]{1,0:T(8,128)S(1)} %collective-permute-done.11.refs_3_), channel_id=1, source_target_pairs={{0,1},{1,0},{2,3},{3,2},{4,5},{5,4},{6,7},{7,6},{8,9},{9,8},{10,11... | collective-permute-start | bytes 909320 | tf_op jit(solution)/shard_map/ppermute | solution.py:481
  42.8 9.3 %collective-permute-start.13 = (f32[592,128]{1,0:T(8,128)S(1)}, f32[592,128]{1,0:T(8,128)S(1)}, u32[]{:S(2)}, u32[]{:S(2)}) collective-permute-start(f32[592,128]{1,0:T(8,128)S(1)} %collective-permute-done.11.refs_3_), channel_id=1, source_target_pairs={{0,2},{1,3},{2,0},{3,1},{4,6},{5,7},{6,4},{7,5},{8,10},{9,11},{10,... | collective-permute-start | bytes 909320 | tf_op jit(solution)/shard_map/ppermute | solution.py:481
  46.9 6.8 %copy-start = (f32[8,128,256]{2,1,0:T(8,128)S(1)}, f32[8,128,256]{2,1,0:T(8,128)}, u32[]{:S(2)}) copy-start(f32[8,128,256]{2,1,0:T(8,128)} %get-tuple-element.61.refs_5_.refs_24_) | copy-start | bytes 3145732
  46.9 6.8 %copy-start.1 = (f32[8,128,256]{2,1,0:T(8,128)S(1)}, f32[8,128,256]{2,1,0:T(8,128)}, u32[]{:S(2)}) copy-start(f32[8,128,256]{2,1,0:T(8,128)} %get-tuple-element.62.refs_6_.refs_25_) | copy-start | bytes 3145732
  46.9 6.8 %copy-start.7 = (bf16[9,208,128]{2,1,0:T(8,128)(2,1)S(1)}, bf16[9,208,128]{2,1,0:T(8,128)(2,1)}, u32[]{:S(2)}) copy-start(bf16[9,208,128]{2,1,0:T(8,128)(2,1)} %get-tuple-element.42.refs_7_.refs_5_.refs_3_) | copy-start | bytes 1437700
  52.1 1.6 %collective-permute-start.16 = (f32[592,128]{1,0:T(8,128)S(1)}, f32[592,128]{1,0:T(8,128)S(1)}, u32[]{:S(2)}, u32[]{:S(2)}) collective-permute-start(f32[592,128]{1,0:T(8,128)S(1)} %collective-permute-done.13.refs_1_), channel_id=1, source_target_pairs={{0,1},{1,0},{2,3},{3,2},{4,5},{5,4},{6,7},{7,6},{8,9},{9,8},{10,11... | collective-permute-start | bytes 909320 | tf_op jit(solution)/shard_map/ppermute | solution.py:481
  56.5 3.7 %collective-permute-start.19 = (f32[24,128]{1,0:T(8,128)S(1)}, f32[24,128]{1,0:T(8,128)S(1)}, u32[]{:S(2)}, u32[]{:S(2)}) collective-permute-start(f32[24,128]{1,0:T(8,128)S(1)} %get-tuple-element.74), channel_id=1, source_target_pairs={{4,0},{5,1},{6,2},{7,3},{8,4},{9,5},{10,6},{11,7},{12,8},{13,9},{1... | collective-permute-start | bytes 36872 | tf_op jit(solution)/shard_map/ppermute | solution.py:477
  58.3 4.6 %collective-permute-start.18 = (f32[24,128]{1,0:T(8,128)S(1)}, f32[24,128]{1,0:T(8,128)S(1)}, u32[]{:S(2)}, u32[]{:S(2)}) collective-permute-start(f32[24,128]{1,0:T(8,128)S(1)} %get-tuple-element.74), channel_id=1, source_target_pairs={{8,0},{9,1},{10,2},{11,3},{12,4},{13,5},{14,6},{15,7},{0,8},{1,9},... | collective-permute-start | bytes 36872 | tf_op jit(solution)/shard_map/ppermute | solution.py:477
  58.3 5.5 %collective-permute-start.17 = (f32[24,128]{1,0:T(8,128)S(1)}, f32[24,128]{1,0:T(8,128)S(1)}, u32[]{:S(2)}, u32[]{:S(2)}) collective-permute-start(f32[24,128]{1,0:T(8,128)S(1)} %get-tuple-element.74), channel_id=1, source_target_pairs={{12,0},{13,1},{14,2},{15,3},{0,4},{1,5},{2,6},{3,7},{4,8},{5,9},{6... | collective-permute-start | bytes 36872 | tf_op jit(solution)/shard_map/ppermute | solution.py:477
  63.8 4.2 %collective-permute-start.22 = (f32[4,24,128]{2,1,0:T(8,128)S(1)}, f32[4,24,128]{2,1,0:T(8,128)S(1)}, u32[]{:S(2)}, u32[]{:S(2)}) collective-permute-start(f32[4,24,128]{2,1,0:T(8,128)S(1)} %pad_maximum_fusion.refs_20_), channel_id=1, source_target_pairs={{0,3},{1,2},{2,1},{3,0},{4,7},{5,6},{6,5},{7,4},{8,11},{9,10},{10,... | collective-permute-start | bytes 147464 | tf_op jit(solution)/shard_map/ppermute | solution.py:481
  63.8 4.6 %collective-permute-start.21 = (f32[4,24,128]{2,1,0:T(8,128)S(1)}, f32[4,24,128]{2,1,0:T(8,128)S(1)}, u32[]{:S(2)}, u32[]{:S(2)}) collective-permute-start(f32[4,24,128]{2,1,0:T(8,128)S(1)} %pad_maximum_fusion.refs_20_), channel_id=1, source_target_pairs={{0,2},{1,3},{2,0},{3,1},{4,6},{5,7},{6,4},{7,5},{8,10},{9,11},{10,... | collective-permute-start | bytes 147464 | tf_op jit(solution)/shard_map/ppermute | solution.py:481
  65.6 2.9 %collective-permute-start.20 = (f32[4,24,128]{2,1,0:T(8,128)S(1)}, f32[4,24,128]{2,1,0:T(8,128)S(1)}, u32[]{:S(2)}, u32[]{:S(2)}) collective-permute-start(f32[4,24,128]{2,1,0:T(8,128)S(1)} %pad_maximum_fusion.refs_20_), channel_id=1, source_target_pairs={{0,1},{1,0},{2,3},{3,2},{4,5},{5,4},{6,7},{7,6},{8,9},{9,8},{10,11... | collective-permute-start | bytes 147464 | tf_op jit(solution)/shard_map/ppermute | solution.py:481
  (1 other events, 1.0 us)

commit v4 on v3

--- a/solution.py
+++ b/solution.py
@@ -166,7 +166,9 @@
     return jnp.sum((tile * wide(column, size)).reshape(-1, 8, size), axis=0)
 
 
-def near_kernel(halo, points, values, mask, *refs):
+def near_kernel(halo, extra, *refs):
+    points, values, mask = refs[extra:extra + 3]
+    refs = refs[extra + 3:]
     leaves, features, size = points.shape
     if halo:
         following, preceding, out, edges, lefts, rights, downs, across, along = refs
@@ -321,7 +323,8 @@
     return row
 
 
-def early_kernel(axis, devices, capacity, places, *refs):
+def early_kernel(extra, axis, devices, capacity, places, *refs):
+    refs = refs[extra:]
     n = len(places)
     own_piece, pieces, lefts = refs[0], refs[1:n + 1], refs[n + 1]
     start = None
@@ -535,15 +538,15 @@
 
     following = passed_along(first, "leaf", -1)
     preceding = passed_along(last, "leaf", 1)
-    def near_apply(halo, values, *others):
+    def near_apply(halo, follow, values, *others):
         before, after = edges_of(leaves, reach)
         outputs = [(VMEM, shape(leaves, size))]
         if halo:
             outputs.append((VMEM, shape(len(before) + len(after), size, size)))
         return kernel_call(
-            functools.partial(near_kernel, halo),
+            functools.partial(near_kernel, halo, len(follow)),
             "near_first" if halo else "near_second",
-            [VMEM, VMEM, SMEM] + [VMEM] * len(others),
+            [ANY] * len(follow) + [VMEM, VMEM, SMEM] + [VMEM] * len(others),
             outputs,
             [
                 pltpu.VMEM((leaves + reach, depth, size), BF16),
@@ -553,9 +556,8 @@
                 pltpu.VMEM((leaves, 8, size), F32),
             ],
             microseconds=3 if halo else 4,
-        )(points, values, near_mask.T, *others)
-
-    near, edges = near_apply(True, right_side, following, preceding)
+        )(*follow, points, values, near_mask.T, *others)
+
     cuts = [devices * cut // GRID_DEVICES for cut in CUTS]
     groups = [tuple(range(start, end)) for start, end in zip(cuts, cuts[1:])]
     if devices == GRID_DEVICES:
@@ -565,12 +567,12 @@
         pieces = {place: together[place] for place in range(devices)}
     sums = shape(leaves + 2, rank, rank)
 
-    def group_call(body, name, places, inputs, outputs, scratch):
+    def group_call(body, name, places, inputs, outputs, scratch, after=()):
         most = -(-(2 * capacity * len(places) + leaves + UNROLL) // UNROLL) * UNROLL
         return kernel_call(
             functools.partial(body, "leaf", devices, capacity, places),
             name,
-            [ANY] + [VMEM] * (len(places) + 1 + len(inputs)),
+            [ANY] * (len(after) + 1) + [VMEM] * (len(places) + 1 + len(inputs)),
             [
                 (SMEM, shape(most, dtype=integers)),
                 (SMEM, shape(most, dtype=integers)),
@@ -585,7 +587,7 @@
                 pltpu.SemaphoreType.DMA((len(places) + 1,)),
             ],
             microseconds={0: 7, 6: 5, 10: 3}.get(places[0], 3),
-        )(piece, *[pieces[place] for place in places], lefts, *inputs)
+        )(*after, piece, *[pieces[place] for place in places], lefts, *inputs)
 
     def hold(value, *others):
         return lax.optimization_barrier((value, *others))[0]
@@ -596,29 +598,39 @@
 
     passes = []
 
-    def tiles_of_group():
+    def tiles_of_group(*after):
         number = len(passes)
         start = [passes[-1][5]] if passes else []
         passes.append(
-            group_call(early_kernel, "far_tiles_%d" % number, groups[number], start, [(VMEM, sums)], [])
+            group_call(
+                functools.partial(early_kernel, len(after)),
+                "far_tiles_%d" % number,
+                groups[number],
+                start,
+                [(VMEM, sums)],
+                [],
+                after,
+            )
         )
         return passes[-1][5]
 
     if devices == GRID_DEVICES:
+        once = passed_along(piece, "leaf", 4)
+        twice = passed_along(once, "leaf", 4)
+        thrice = passed_along(twice, "leaf", 4)
+        near, edges = near_apply(True, (thrice,), right_side, following, preceding)
         put(0, piece)
         put(1, swapped(piece, "leaf", 2))
-        turned = passed_along(piece, "leaf", 4)
-        put(2, turned)
-        across = swapped(turned, "leaf", 2)
-        turned = hold(passed_along(turned, "leaf", 4), tiles_of_group())
-        put(3, across)
-        put(4, turned)
-        across = swapped(turned, "leaf", 2)
-        turned = hold(passed_along(turned, "leaf", 4), tiles_of_group())
-        put(5, across)
-        put(6, turned)
-        put(7, hold(swapped(turned, "leaf", 2), tiles_of_group(), near))
+        put(2, once)
+        tiles_of_group(twice)
+        put(3, swapped(once, "leaf", 2))
+        put(4, twice)
+        tiles_of_group(twice)
+        put(5, swapped(twice, "leaf", 2))
+        put(6, thrice)
+        put(7, hold(swapped(thrice, "leaf", 2), tiles_of_group(), near))
     else:
+        near, edges = near_apply(True, (), right_side, following, preceding)
         for _ in groups[:-1]:
             tiles_of_group()
     late = group_call(
@@ -633,7 +645,7 @@
     image, payload = late[5:]
 
     everyone = gathered_blocks(payload, "leaf")
-    near_second = near_apply(False, image)[0]
+    near_second = near_apply(False, (), image)[0]
     residual, along, numbers = kernel_call(
         functools.partial(second_kernel, reach, "leaf", devices, groups),
         "far_second",

time: 84.4 us -> 84.4 us (level); the launches traced: 84.3 us -> 83.1 us
  waiting for transfers between devices: 26.4 us -> 21.4 us
  starting transfers between devices: 16.8 us -> 20.1 us
    ppermute x8, starting transfers between devices: 8.89 us -> 11.7 us  [passed_along(): lax.ppermute(block, axis, [((i - distance) % size, i) for i in range(size)])]
    ppermute x15, waiting for transfers between devices: 4.61 us -> 2.05 us  [swapped(): lax.ppermute(block, axis, [(i, i ^ bit) for i in range(lax.axis_size(axis...]
    ppermute x8, waiting for transfers between devices: 21.8 us -> 19.3 us  [passed_along(): lax.ppermute(block, axis, [((i - distance) % size, i) for i in range(size)])]
    unnamed x20 -> x18, local copies, waits for them, and re-layouts: 2.01 us -> 2.02 us
  transfers between devices with their start and end apart: 23 -> 23, of which waited for: 10 -> 8; matrix products, arithmetic and copies ran while one was open for 0% -> 0% of each run, Pallas kernels for 19% -> 19%
where the time goes in v4:
time: 84.4 us; the launch traced here: 83.1 us
  Pallas kernels  28.3 us (34%)
  waiting for transfers between devices  21.4 us (25%)
  starting transfers between devices  20.1 us (24%)
  blocking collectives  10.5 us (12%)
  local copies, waits for them, and re-layouts  2.02 us (2%)
    ppermute x8, waiting for transfers between devices, passed_along(): lax.ppermute(block, axis, [((i - distance) % size, i) for i in range(size)])  19.3 us
    pallas_call x4, Pallas kernels, group_call(): kernel_call(functools.partial(body, 'leaf', devices, capacity, places), n...  13.7 us
    ppermute x8, starting transfers between devices, passed_along(): lax.ppermute(block, axis, [((i - distance) % size, i) for i in range(size)])  11.7 us
    all_to_all x1, blocking collectives, exchanged(): return lax.all_to_all(blocks, axis, split_axis=0, concat_axis=0, tiled=True)  10.5 us
    ppermute x15, starting transfers between devices, swapped(): lax.ppermute(block, axis, [(i, i ^ bit) for i in range(lax.axis_size(axis...  8.41 us
    pallas_call x2, Pallas kernels, near_apply(): kernel_call(functools.partial(near_kernel, halo, len(follow)), 'near_firs...  5.07 us
    pallas_call x1, Pallas kernels, on_device(): kernel_call(functools.partial(second_kernel, reach, 'leaf', devices, grou...  4.78 us
    pallas_call x1, Pallas kernels, on_device(): kernel_call(functools.partial(prepare_kernel, devices, capacity), 'prepar...  3.81 us
  transfers between devices with their start and end apart: 23, of which 8 were waited for; matrix products, arithmetic and copies ran while one was open for 0% of the time, Pallas kernels for 19%

profile of v4, /device:TPU:0, one launch (start us, length us, event | category | flops | bytes accessed | tf_op | source)
XLA Modules:
  0.0 83.1 jit_solution(6575413085294658529)
XLA Ops:
  0.6 3.8 %prepare.1 = (f32[592,128]{1,0:T(8,128)}, f32[8,128,256]{2,1,0:T(8,128)}, f32[8,128,256]{2,1,0:T(8,128)}, bf16[9,208,128]{2,1,0:T(8,128)(2,1)}, f32[2,72,256]{2,1,0:T(8,128)}, /*index=5*/f32[2,72,256]{2,1,0:T(8,128)}) custom-call(f32[8,64,256]{2,1,0:T(8,128)} %refs_0_.3, f32[8,256]{1,0:T(8,128)} %values.1, s32[2,8]{1,0:T(2,128)} %bitcast.8, ...), custom_call_target="tpu_custom_call" | custom-call | flops 2000000000 | bytes 6000000 | tf_op jit(solution)/shard_map/prepare/pallas_call | solution.py:512
  4.4 3.1 %collective-permute-start = (f32[592,128]{1,0:T(8,128)}, f32[592,128]{1,0:T(8,128)S(1)}, u32[]{:S(2)}, u32[]{:S(2)}) collective-permute-start(f32[592,128]{1,0:T(8,128)} %get-tuple-element.39.refs_1_.refs_2_.refs_0_), channel_id=1, source_target_pairs={{12,0},{13,1},{14,2},{15,3},{0,4},{1,5},{2,6},{3,7},{4,8},{5,9},{6... | collective-permute-start | bytes 909320 | tf_op jit(solution)/shard_map/ppermute | solution.py:480
  7.5 1.5 %collective-permute-start.3 = (f32[592,128]{1,0:T(8,128)}, f32[592,128]{1,0:T(8,128)S(1)}, u32[]{:S(2)}, u32[]{:S(2)}) collective-permute-start(f32[592,128]{1,0:T(8,128)} %get-tuple-element.39.refs_1_.refs_2_.refs_0_), channel_id=1, source_target_pairs={{0,2},{1,3},{2,0},{3,1},{4,6},{5,7},{6,4},{7,5},{8,10},{9,11},{10,... | collective-permute-start | bytes 909320 | tf_op jit(solution)/shard_map/ppermute | solution.py:484
  9.1 7.9 %collective-permute-done.refs_6_ = f32[592,128]{1,0:T(8,128)S(1)} collective-permute-done((f32[592,128]{1,0:T(8,128)}, f32[592,128]{1,0:T(8,128)S(1)}, u32[]{:S(2)}, u32[]{:S(2)}) %collective-permute-start) | collective-permute-done | bytes 303136 | tf_op jit(solution)/shard_map/ppermute | solution.py:480
  17.0 1.6 %collective-permute-start.6 = (f32[592,128]{1,0:T(8,128)S(1)}, f32[592,128]{1,0:T(8,128)S(1)}, u32[]{:S(2)}, u32[]{:S(2)}) collective-permute-start(f32[592,128]{1,0:T(8,128)S(1)} %collective-permute-done.refs_6_), channel_id=1, source_target_pairs={{0,2},{1,3},{2,0},{3,1},{4,6},{5,7},{6,4},{7,5},{8,10},{9,11},{10,... | collective-permute-start | bytes 909320 | tf_op jit(solution)/shard_map/ppermute | solution.py:484
  18.5 0.2 collective-permute-start.5
  18.7 3.6 %collective-permute-start.14 = (f32[2,72,256]{2,1,0:T(8,128)}, f32[2,72,256]{2,1,0:T(8,128)S(1)}, u32[]{:S(2)}, u32[]{:S(2)}) collective-permute-start(f32[2,72,256]{2,1,0:T(8,128)} %get-tuple-element.53), channel_id=1, source_target_pairs={{1,0},{2,1},{3,2},{4,3},{5,4},{6,5},{7,6},{8,7},{9,8},{10,9},{11,1... | collective-permute-start | bytes 442376 | tf_op jit(solution)/shard_map/ppermute | solution.py:480
  22.4 4.9 %collective-permute-done.1.refs_0_.refs_4_ = f32[592,128]{1,0:T(8,128)S(1)} collective-permute-done((f32[592,128]{1,0:T(8,128)S(1)}, f32[592,128]{1,0:T(8,128)S(1)}, u32[]{:S(2)}, u32[]{:S(2)}) %collective-permute-start.1) | collective-permute-done | bytes 303136 | tf_op jit(solution)/shard_map/ppermute | solution.py:480
  27.2 1.2 %collective-permute-start.9 = (f32[592,128]{1,0:T(8,128)S(1)}, f32[592,128]{1,0:T(8,128)S(1)}, u32[]{:S(2)}, u32[]{:S(2)}) collective-permute-start(f32[592,128]{1,0:T(8,128)S(1)} %collective-permute-done.1.refs_0_.refs_4_), channel_id=1, source_target_pairs={{0,2},{1,3},{2,0},{3,1},{4,6},{5,7},{6,4},{7,5},{8,10},{9,11},{10,... | collective-permute-start | bytes 909320 | tf_op jit(solution)/shard_map/ppermute | solution.py:484
  28.4 0.5 collective-permute-start.7
  28.9 1.0 %copy-done.4 = f32[592,128]{1,0:T(8,128)S(1)} copy-done((f32[592,128]{1,0:T(8,128)S(1)}, f32[592,128]{1,0:T(8,128)}, u32[]{:S(2)}) %copy-start.4) | copy-done | bytes 303128
  29.9 1.0 %copy-done.6 = bf16[9,208,128]{2,1,0:T(8,128)(2,1)S(1)} copy-done((bf16[9,208,128]{2,1,0:T(8,128)(2,1)S(1)}, bf16[9,208,128]{2,1,0:T(8,128)(2,1)}, u32[]{:S(2)}) %copy-start.6) | copy-done | bytes 479256
  30.9 4.6 %far_tiles_0.1 = (s32[60]{0:T(128)S(1)}, s32[60]{0:T(128)S(1)}, s32[1]{0:T(128)}, f32[60,128,128]{2,1,0:T(8,128)S(1)}, f32[6,128,128]{2,1,0:T(8,128)S(1)}, /*index=5*/f32[10,128,128]{2,1,0:T(8,128)S(1)}) custom-call(f32[592,128]{1,0:T(8,128)S(1)} %collective-permute-done.1.refs_0_.refs_4_, f32[592,128]{1,0:T(8,128)S(1)} %copy-done.4, ...), custom_call_target="tpu_custom_call" | custom-call | flops 7000000000 | bytes 21000000 | tf_op jit(solution)/shard_map/far_tiles_0/pallas_call | solution.py:572
  35.6 0.8 collective-permute-done.11.refs_3_.refs_0_
  36.4 1.0 %collective-permute-start.13 = (f32[592,128]{1,0:T(8,128)S(1)}, f32[592,128]{1,0:T(8,128)S(1)}, u32[]{:S(2)}, u32[]{:S(2)}) collective-permute-start(f32[592,128]{1,0:T(8,128)S(1)} %collective-permute-done.11.refs_3_.refs_0_), channel_id=1, source_target_pairs={{0,2},{1,3},{2,0},{3,1},{4,6},{5,7},{6,4},{7,5},{8,10},{9,11},{10,... | collective-permute-start | bytes 909320 | tf_op jit(solution)/shard_map/ppermute | solution.py:484
  37.5 0.4 collective-permute-start.10
  37.9 3.3 %far_tiles_1.1 = (s32[44]{0:T(128)S(1)}, s32[44]{0:T(128)S(1)}, s32[1]{0:T(128)}, f32[44,128,128]{2,1,0:T(8,128)S(1)}, f32[4,128,128]{2,1,0:T(8,128)S(1)}, /*index=5*/f32[10,128,128]{2,1,0:T(8,128)S(1)}) custom-call(f32[592,128]{1,0:T(8,128)S(1)} %collective-permute-done.1.refs_0_.refs_4_, f32[592,128]{1,0:T(8,128)S(1)} %copy-done.4, ...), custom_call_target="tpu_custom_call" | custom-call | flops 5000000000 | bytes 15000000 | tf_op jit(solution)/shard_map/far_tiles_1/pallas_call | solution.py:572
  41.3 1.7 %collective-permute-done.15.refs_5_ = f32[2,72,256]{2,1,0:T(8,128)S(1)} collective-permute-done((f32[2,72,256]{2,1,0:T(8,128)S(1)}, f32[2,72,256]{2,1,0:T(8,128)S(1)}, u32[]{:S(2)}, u32[]{:S(2)}) %collective-permute-start.15) | collective-permute-done | bytes 147488 | tf_op jit(solution)/shard_map/ppermute | solution.py:480
  43.0 2.8 %near_first.1 = (f32[8,256]{1,0:T(8,128)S(1)}, f32[6,256,256]{2,1,0:T(8,128)S(1)}) custom-call(f32[592,128]{1,0:T(8,128)S(1)} %collective-permute-done.11.refs_3_.refs_0_, f32[8,64,256]{2,1,0:T(8,128)S(1)} %copy-done.3, f32[8,256]{1,0:T(8,128)S(1)} %copy-done.2, s32[2,8]{1,0:T(2,128)S(1)} %bitcast.9, f32[2,72,256]{2,1,0:T(8,128)S(1)} %collective-permute-done.14.refs_4_, ...), custom_call_target="tpu_custom_call" | custom-call | flops 3000000000 | bytes 9000000 | tf_op jit(solution)/shard_map/near_first/pallas_call | solution.py:546
  45.9 3.0 %far_tiles_2.1 = (s32[44]{0:T(128)S(1)}, s32[44]{0:T(128)S(1)}, s32[1]{0:T(128)}, f32[44,128,128]{2,1,0:T(8,128)S(1)}, f32[4,128,128]{2,1,0:T(8,128)S(1)}, /*index=5*/f32[10,128,128]{2,1,0:T(8,128)S(1)}) custom-call(f32[592,128]{1,0:T(8,128)S(1)} %copy-done.4, f32[592,128]{1,0:T(8,128)S(1)} %collective-permute-done.9.refs_1_, ...), custom_call_target="tpu_custom_call" | custom-call | flops 3000000000 | bytes 9000000 | tf_op jit(solution)/shard_map/far_tiles_2/pallas_call | solution.py:572
  49.0 1.6 %collective-permute-done.16.refs_2_ = f32[592,128]{1,0:T(8,128)S(1)} collective-permute-done((f32[592,128]{1,0:T(8,128)S(1)}, f32[592,128]{1,0:T(8,128)S(1)}, u32[]{:S(2)}, u32[]{:S(2)}) %collective-permute-start.16) | collective-permute-done | bytes 303136 | tf_op jit(solution)/shard_map/ppermute | solution.py:484
  50.6 2.8 %far_last.1 = (s32[28]{0:T(128)S(1)}, s32[28]{0:T(128)S(1)}, s32[1]{0:T(128)}, f32[28,128,128]{2,1,0:T(8,128)S(1)}, f32[2,128,128]{2,1,0:T(8,128)S(1)}, /*index=5*/f32[8,256]{1,0:T(8,128)S(1)}, f32[24,128]{1,0:T(8,128)S(1)}) custom-call(f32[592,128]{1,0:T(8,128)S(1)} %copy-done.4, f32[592,128]{1,0:T(8,128)S(1)} %collective-permute-done.13.refs_1_, ...), custom_call_target="tpu_custom_call" | custom-call | flops 3000000000 | bytes 9000000 | tf_op jit(solution)/shard_map/far_last/pallas_call | solution.py:572
  53.4 3.4 %collective-permute-start.19 = (f32[24,128]{1,0:T(8,128)S(1)}, f32[24,128]{1,0:T(8,128)S(1)}, u32[]{:S(2)}, u32[]{:S(2)}) collective-permute-start(f32[24,128]{1,0:T(8,128)S(1)} %get-tuple-element.70), channel_id=1, source_target_pairs={{4,0},{5,1},{6,2},{7,3},{8,4},{9,5},{10,6},{11,7},{12,8},{13,9},{1... | collective-permute-start | bytes 36872 | tf_op jit(solution)/shard_map/ppermute | solution.py:480
  56.8 1.4 %collective-permute-start.17 = (f32[24,128]{1,0:T(8,128)S(1)}, f32[24,128]{1,0:T(8,128)S(1)}, u32[]{:S(2)}, u32[]{:S(2)}) collective-permute-start(f32[24,128]{1,0:T(8,128)S(1)} %get-tuple-element.70), channel_id=1, source_target_pairs={{12,0},{13,1},{14,2},{15,3},{0,4},{1,5},{2,6},{3,7},{4,8},{5,9},{6... | collective-permute-start | bytes 36872 | tf_op jit(solution)/shard_map/ppermute | solution.py:480
  58.3 3.2 %collective-permute-done.18 = f32[24,128]{1,0:T(8,128)S(1)} collective-permute-done((f32[24,128]{1,0:T(8,128)S(1)}, f32[24,128]{1,0:T(8,128)S(1)}, u32[]{:S(2)}, u32[]{:S(2)}) %collective-permute-start.18) | collective-permute-done | bytes 12320 | tf_op jit(solution)/shard_map/ppermute | solution.py:480
  61.4 0.9 %collective-permute-done.17 = f32[24,128]{1,0:T(8,128)S(1)} collective-permute-done((f32[24,128]{1,0:T(8,128)S(1)}, f32[24,128]{1,0:T(8,128)S(1)}, u32[]{:S(2)}, u32[]{:S(2)}) %collective-permute-start.17) | collective-permute-done | bytes 12320 | tf_op jit(solution)/shard_map/ppermute | solution.py:480
  62.3 1.8 %collective-permute-start.21 = (f32[4,24,128]{2,1,0:T(8,128)S(1)}, f32[4,24,128]{2,1,0:T(8,128)S(1)}, u32[]{:S(2)}, u32[]{:S(2)}) collective-permute-start(f32[4,24,128]{2,1,0:T(8,128)S(1)} %pad_maximum_fusion.refs_20_), channel_id=1, source_target_pairs={{0,2},{1,3},{2,0},{3,1},{4,6},{5,7},{6,4},{7,5},{8,10},{9,11},{10,... | collective-permute-start | bytes 147464 | tf_op jit(solution)/shard_map/ppermute | solution.py:484
  64.2 2.3 %near_second.1.refs_28_ = f32[8,256]{1,0:T(8,128)S(1)} custom-call(f32[8,64,256]{2,1,0:T(8,128)S(1)} %copy-done.3, f32[8,256]{1,0:T(8,128)S(1)} %get-tuple-element.71.refs_1_.refs_27_.image, s32[2,8]{1,0:T(2,128)S(1)} %bitcast.10), custom_call_target="tpu_custom_call" | custom-call | flops 4000000000 | bytes 12000000 | tf_op jit(solution)/shard_map/near_second/pallas_call | solution.py:546
  66.5 0.4 collective-permute-done.21.refs_22_
  67.0 4.8 %far_second.1 = (f32[8,256]{1,0:T(8,128)S(1)}, f32[8,256]{1,0:T(8,128)S(1)}, f32[16,1,128]{2,1,0:T(1,128)S(1)}) custom-call(s32[60]{0:T(128)S(1)} %get-tuple-element.41.refs_0_, s32[60]{0:T(128)S(1)} %get-tuple-element.42.refs_1_, s32[1]{0:T(128)} %get-tuple-element.43.refs_2_, s32[44]{0:T(128)S(1)} %get-tuple-element.45.refs_3_, ...), custom_call_target="tpu_custom_call" | custom-call | flops 1000000000 | bytes 3000000 | tf_op jit(solution)/shard_map/far_second/pallas_call | solution.py:649
  71.8 10.5 %all_to_all.5.everyone = f32[16,1,128]{2,1,0:T(1,128)S(1)} all-to-all(f32[16,1,128]{2,1,0:T(1,128)S(1)} %get-tuple-element.73), channel_id=1, replica_groups=mesh['groups'=2,'leaf'=16] {'leaf'}, dimensions={0} | all-to-all | bytes 16384 | tf_op jit(solution)/shard_map/all_to_all | solution.py:488
  82.3 0.9 %finish.1 = (f32[8,256]{1,0:T(8,128)}, f32[8,256]{1,0:T(8,128)}) custom-call(f32[16,1,128]{2,1,0:T(1,128)S(1)} %all_to_all.5.everyone, f32[8,256]{1,0:T(8,128)S(1)} %copy-done.2, f32[8,256]{1,0:T(8,128)S(1)} %get-tuple-element.71.refs_1_.refs_27_.image, f32[8,256]{1,0:T(8,128)S(1)} %get-tuple-element.74.residual, f32[8,256]{1,0:T(8,128)S(1)} %get-tuple-element.75.along), custom_call_target="tpu_custom_call" | custom-call | flops 1000000000 | bytes 3000000 | tf_op jit(solution)/shard_map/finish/pallas_call | solution.py:671
  (43 shorter events, 0.4 us)
Async XLA Ops:
  4.4 12.5 %collective-permute-start = (f32[592,128]{1,0:T(8,128)}, f32[592,128]{1,0:T(8,128)S(1)}, u32[]{:S(2)}, u32[]{:S(2)}) collective-permute-start(f32[592,128]{1,0:T(8,128)} %get-tuple-element.39.refs_1_.refs_2_.refs_0_), channel_id=1, source_target_pairs={{12,0},{13,1},{14,2},{15,3},{0,4},{1,5},{2,6},{3,7},{4,8},{5,9},{6... | collective-permute-start | bytes 909320 | tf_op jit(solution)/shard_map/ppermute | solution.py:480
  7.5 9.4 %collective-permute-start.3 = (f32[592,128]{1,0:T(8,128)}, f32[592,128]{1,0:T(8,128)S(1)}, u32[]{:S(2)}, u32[]{:S(2)}) collective-permute-start(f32[592,128]{1,0:T(8,128)} %get-tuple-element.39.refs_1_.refs_2_.refs_0_), channel_id=1, source_target_pairs={{0,2},{1,3},{2,0},{3,1},{4,6},{5,7},{6,4},{7,5},{8,10},{9,11},{10,... | collective-permute-start | bytes 909320 | tf_op jit(solution)/shard_map/ppermute | solution.py:484
  9.0 9.7 %collective-permute-start.2 = (f32[592,128]{1,0:T(8,128)}, f32[592,128]{1,0:T(8,128)S(1)}, u32[]{:S(2)}, u32[]{:S(2)}) collective-permute-start(f32[592,128]{1,0:T(8,128)} %get-tuple-element.39.refs_1_.refs_2_.refs_0_), channel_id=1, source_target_pairs={{0,1},{1,0},{2,3},{3,2},{4,5},{5,4},{6,7},{7,6},{8,9},{9,8},{10,11... | collective-permute-start | bytes 909320 | tf_op jit(solution)/shard_map/ppermute | solution.py:484
  16.9 10.3 %collective-permute-start.1 = (f32[592,128]{1,0:T(8,128)S(1)}, f32[592,128]{1,0:T(8,128)S(1)}, u32[]{:S(2)}, u32[]{:S(2)}) collective-permute-start(f32[592,128]{1,0:T(8,128)S(1)} %collective-permute-done.refs_6_), channel_id=1, source_target_pairs={{12,0},{13,1},{14,2},{15,3},{0,4},{1,5},{2,6},{3,7},{4,8},{5,9},{6... | collective-permute-start | bytes 909320 | tf_op jit(solution)/shard_map/ppermute | solution.py:480
  16.9 10.3 %collective-permute-start.4 = (f32[592,128]{1,0:T(8,128)S(1)}, f32[592,128]{1,0:T(8,128)S(1)}, u32[]{:S(2)}, u32[]{:S(2)}) collective-permute-start(f32[592,128]{1,0:T(8,128)S(1)} %collective-permute-done.3.refs_4_), channel_id=1, source_target_pairs={{0,1},{1,0},{2,3},{3,2},{4,5},{5,4},{6,7},{7,6},{8,9},{9,8},{10,11... | collective-permute-start | bytes 909320 | tf_op jit(solution)/shard_map/ppermute | solution.py:484
  17.0 11.4 %collective-permute-start.6 = (f32[592,128]{1,0:T(8,128)S(1)}, f32[592,128]{1,0:T(8,128)S(1)}, u32[]{:S(2)}, u32[]{:S(2)}) collective-permute-start(f32[592,128]{1,0:T(8,128)S(1)} %collective-permute-done.refs_6_), channel_id=1, source_target_pairs={{0,2},{1,3},{2,0},{3,1},{4,6},{5,7},{6,4},{7,5},{8,10},{9,11},{10,... | collective-permute-start | bytes 909320 | tf_op jit(solution)/shard_map/ppermute | solution.py:484
  18.5 9.9 %collective-permute-start.5 = (f32[592,128]{1,0:T(8,128)S(1)}, f32[592,128]{1,0:T(8,128)S(1)}, u32[]{:S(2)}, u32[]{:S(2)}) collective-permute-start(f32[592,128]{1,0:T(8,128)S(1)} %collective-permute-done.refs_6_), channel_id=1, source_target_pairs={{0,1},{1,0},{2,3},{3,2},{4,5},{5,4},{6,7},{7,6},{8,9},{9,8},{10,11... | collective-permute-start | bytes 909320 | tf_op jit(solution)/shard_map/ppermute | solution.py:484
  18.7 22.5 %collective-permute-start.14 = (f32[2,72,256]{2,1,0:T(8,128)}, f32[2,72,256]{2,1,0:T(8,128)S(1)}, u32[]{:S(2)}, u32[]{:S(2)}) collective-permute-start(f32[2,72,256]{2,1,0:T(8,128)} %get-tuple-element.53), channel_id=1, source_target_pairs={{1,0},{2,1},{3,2},{4,3},{5,4},{6,5},{7,6},{8,7},{9,8},{10,9},{11,1... | collective-permute-start | bytes 442376 | tf_op jit(solution)/shard_map/ppermute | solution.py:480
  27.2 9.2 %collective-permute-start.11 = (f32[592,128]{1,0:T(8,128)S(1)}, f32[592,128]{1,0:T(8,128)S(1)}, u32[]{:S(2)}, u32[]{:S(2)}) collective-permute-start(f32[592,128]{1,0:T(8,128)S(1)} %collective-permute-done.1.refs_0_.refs_4_), channel_id=1, source_target_pairs={{12,0},{13,1},{14,2},{15,3},{0,4},{1,5},{2,6},{3,7},{4,8},{5,9},{6... | collective-permute-start | bytes 909320 | tf_op jit(solution)/shard_map/ppermute | solution.py:480
  27.2 10.2 %collective-permute-start.9 = (f32[592,128]{1,0:T(8,128)S(1)}, f32[592,128]{1,0:T(8,128)S(1)}, u32[]{:S(2)}, u32[]{:S(2)}) collective-permute-start(f32[592,128]{1,0:T(8,128)S(1)} %collective-permute-done.1.refs_0_.refs_4_), channel_id=1, source_target_pairs={{0,2},{1,3},{2,0},{3,1},{4,6},{5,7},{6,4},{7,5},{8,10},{9,11},{10,... | collective-permute-start | bytes 909320 | tf_op jit(solution)/shard_map/ppermute | solution.py:484
  28.4 9.1 %collective-permute-start.8 = (f32[592,128]{1,0:T(8,128)S(1)}, f32[592,128]{1,0:T(8,128)S(1)}, u32[]{:S(2)}, u32[]{:S(2)}) collective-permute-start(f32[592,128]{1,0:T(8,128)S(1)} %collective-permute-done.1.refs_0_.refs_4_), channel_id=1, source_target_pairs={{0,1},{1,0},{2,3},{3,2},{4,5},{5,4},{6,7},{7,6},{8,9},{9,8},{10,11... | collective-permute-start | bytes 909320 | tf_op jit(solution)/shard_map/ppermute | solution.py:484
  28.4 7.1 %collective-permute-start.7 = (f32[592,128]{1,0:T(8,128)S(1)}, f32[592,128]{1,0:T(8,128)S(1)}, u32[]{:S(2)}, u32[]{:S(2)}) collective-permute-start(f32[592,128]{1,0:T(8,128)S(1)} %collective-permute-done.6.refs_2_), channel_id=1, source_target_pairs={{0,1},{1,0},{2,3},{3,2},{4,5},{5,4},{6,7},{7,6},{8,9},{9,8},{10,11... | collective-permute-start | bytes 909320 | tf_op jit(solution)/shard_map/ppermute | solution.py:484
  28.9 1.0 %copy-start.4 = (f32[592,128]{1,0:T(8,128)S(1)}, f32[592,128]{1,0:T(8,128)}, u32[]{:S(2)}) copy-start(f32[592,128]{1,0:T(8,128)} %get-tuple-element.39.refs_1_.refs_2_.refs_0_) | copy-start | bytes 909316
  29.9 1.0 %copy-start.6 = (bf16[9,208,128]{2,1,0:T(8,128)(2,1)S(1)}, bf16[9,208,128]{2,1,0:T(8,128)(2,1)}, u32[]{:S(2)}) copy-start(bf16[9,208,128]{2,1,0:T(8,128)(2,1)} %get-tuple-element.40.refs_8_.refs_6_.refs_5_.refs_3_) | copy-start | bytes 1437700
  30.9 4.6 %copy-start.8 = (f32[2,72,256]{2,1,0:T(8,128)S(1)}, f32[2,72,256]{2,1,0:T(8,128)}, u32[]{:S(2)}) copy-start(f32[2,72,256]{2,1,0:T(8,128)} %get-tuple-element.54) | copy-start | bytes 442372
  35.5 7.5 %collective-permute-start.15 = (f32[2,72,256]{2,1,0:T(8,128)S(1)}, f32[2,72,256]{2,1,0:T(8,128)S(1)}, u32[]{:S(2)}, u32[]{:S(2)}) collective-permute-start(f32[2,72,256]{2,1,0:T(8,128)S(1)} %copy-done.8), channel_id=1, source_target_pairs={{15,0},{0,1},{1,2},{2,3},{3,4},{4,5},{5,6},{6,7},{7,8},{8,9},{9,10... | collective-permute-start | bytes 442376 | tf_op jit(solution)/shard_map/ppermute | solution.py:480
  36.4 12.5 %collective-permute-start.13 = (f32[592,128]{1,0:T(8,128)S(1)}, f32[592,128]{1,0:T(8,128)S(1)}, u32[]{:S(2)}, u32[]{:S(2)}) collective-permute-start(f32[592,128]{1,0:T(8,128)S(1)} %collective-permute-done.11.refs_3_.refs_0_), channel_id=1, source_target_pairs={{0,2},{1,3},{2,0},{3,1},{4,6},{5,7},{6,4},{7,5},{8,10},{9,11},{10,... | collective-permute-start | bytes 909320 | tf_op jit(solution)/shard_map/ppermute | solution.py:484
  37.4 8.4 %collective-permute-start.12 = (f32[592,128]{1,0:T(8,128)S(1)}, f32[592,128]{1,0:T(8,128)S(1)}, u32[]{:S(2)}, u32[]{:S(2)}) collective-permute-start(f32[592,128]{1,0:T(8,128)S(1)} %collective-permute-done.11.refs_3_.refs_0_), channel_id=1, source_target_pairs={{0,1},{1,0},{2,3},{3,2},{4,5},{5,4},{6,7},{7,6},{8,9},{9,8},{10,11... | collective-permute-start | bytes 909320 | tf_op jit(solution)/shard_map/ppermute | solution.py:484
  37.5 8.4 %collective-permute-start.10 = (f32[592,128]{1,0:T(8,128)S(1)}, f32[592,128]{1,0:T(8,128)S(1)}, u32[]{:S(2)}, u32[]{:S(2)}) collective-permute-start(f32[592,128]{1,0:T(8,128)S(1)} %collective-permute-done.9.refs_1_), channel_id=1, source_target_pairs={{0,1},{1,0},{2,3},{3,2},{4,5},{5,4},{6,7},{7,6},{8,9},{9,8},{10,11... | collective-permute-start | bytes 909320 | tf_op jit(solution)/shard_map/ppermute | solution.py:484
  37.9 5.1 %copy-start.2 = (f32[8,256]{1,0:T(8,128)S(1)}, f32[8,256]{1,0:T(8,128)}, u32[]{:S(2)}) copy-start(f32[8,256]{1,0:T(8,128)} %values.1) | copy-start | bytes 24580
  37.9 5.1 %copy-start.3 = (f32[8,64,256]{2,1,0:T(8,128)S(1)}, f32[8,64,256]{2,1,0:T(8,128)}, u32[]{:S(2)}) copy-start(f32[8,64,256]{2,1,0:T(8,128)} %refs_0_.3) | copy-start | bytes 1572868
  37.9 5.1 %copy-start.5 = (s32[8,2]{0,1:T(2,128)S(1)}, s32[8,2]{0,1:T(2,128)}, u32[]{:S(2)}) copy-start(s32[8,2]{0,1:T(2,128)} %param.9) | copy-start | bytes 196
  45.8 4.8 %copy-start = (f32[8,128,256]{2,1,0:T(8,128)S(1)}, f32[8,128,256]{2,1,0:T(8,128)}, u32[]{:S(2)}) copy-start(f32[8,128,256]{2,1,0:T(8,128)} %get-tuple-element.57.refs_5_.refs_24_) | copy-start | bytes 3145732
  45.9 4.8 %copy-start.1 = (f32[8,128,256]{2,1,0:T(8,128)S(1)}, f32[8,128,256]{2,1,0:T(8,128)}, u32[]{:S(2)}) copy-start(f32[8,128,256]{2,1,0:T(8,128)} %get-tuple-element.58.refs_6_.refs_25_) | copy-start | bytes 3145732
  45.9 4.7 %copy-start.7 = (bf16[9,208,128]{2,1,0:T(8,128)(2,1)S(1)}, bf16[9,208,128]{2,1,0:T(8,128)(2,1)}, u32[]{:S(2)}) copy-start(bf16[9,208,128]{2,1,0:T(8,128)(2,1)} %get-tuple-element.40.refs_8_.refs_6_.refs_5_.refs_3_) | copy-start | bytes 1437700
  48.9 1.7 %collective-permute-start.16 = (f32[592,128]{1,0:T(8,128)S(1)}, f32[592,128]{1,0:T(8,128)S(1)}, u32[]{:S(2)}, u32[]{:S(2)}) collective-permute-start(f32[592,128]{1,0:T(8,128)S(1)} %collective-permute-done.13.refs_1_), channel_id=1, source_target_pairs={{0,1},{1,0},{2,3},{3,2},{4,5},{5,4},{6,7},{7,6},{8,9},{9,8},{10,11... | collective-permute-start | bytes 909320 | tf_op jit(solution)/shard_map/ppermute | solution.py:484
  53.4 4.9 %collective-permute-start.19 = (f32[24,128]{1,0:T(8,128)S(1)}, f32[24,128]{1,0:T(8,128)S(1)}, u32[]{:S(2)}, u32[]{:S(2)}) collective-permute-start(f32[24,128]{1,0:T(8,128)S(1)} %get-tuple-element.70), channel_id=1, source_target_pairs={{4,0},{5,1},{6,2},{7,3},{8,4},{9,5},{10,6},{11,7},{12,8},{13,9},{1... | collective-permute-start | bytes 36872 | tf_op jit(solution)/shard_map/ppermute | solution.py:480
  56.8 4.6 %collective-permute-start.18 = (f32[24,128]{1,0:T(8,128)S(1)}, f32[24,128]{1,0:T(8,128)S(1)}, u32[]{:S(2)}, u32[]{:S(2)}) collective-permute-start(f32[24,128]{1,0:T(8,128)S(1)} %get-tuple-element.70), channel_id=1, source_target_pairs={{8,0},{9,1},{10,2},{11,3},{12,4},{13,5},{14,6},{15,7},{0,8},{1,9},... | collective-permute-start | bytes 36872 | tf_op jit(solution)/shard_map/ppermute | solution.py:480
  56.8 5.5 %collective-permute-start.17 = (f32[24,128]{1,0:T(8,128)S(1)}, f32[24,128]{1,0:T(8,128)S(1)}, u32[]{:S(2)}, u32[]{:S(2)}) collective-permute-start(f32[24,128]{1,0:T(8,128)S(1)} %get-tuple-element.70), channel_id=1, source_target_pairs={{12,0},{13,1},{14,2},{15,3},{0,4},{1,5},{2,6},{3,7},{4,8},{5,9},{6... | collective-permute-start | bytes 36872 | tf_op jit(solution)/shard_map/ppermute | solution.py:480
  62.3 4.2 %collective-permute-start.22 = (f32[4,24,128]{2,1,0:T(8,128)S(1)}, f32[4,24,128]{2,1,0:T(8,128)S(1)}, u32[]{:S(2)}, u32[]{:S(2)}) collective-permute-start(f32[4,24,128]{2,1,0:T(8,128)S(1)} %pad_maximum_fusion.refs_20_), channel_id=1, source_target_pairs={{0,3},{1,2},{2,1},{3,0},{4,7},{5,6},{6,5},{7,4},{8,11},{9,10},{10,... | collective-permute-start | bytes 147464 | tf_op jit(solution)/shard_map/ppermute | solution.py:484
  62.3 4.6 %collective-permute-start.21 = (f32[4,24,128]{2,1,0:T(8,128)S(1)}, f32[4,24,128]{2,1,0:T(8,128)S(1)}, u32[]{:S(2)}, u32[]{:S(2)}) collective-permute-start(f32[4,24,128]{2,1,0:T(8,128)S(1)} %pad_maximum_fusion.refs_20_), channel_id=1, source_target_pairs={{0,2},{1,3},{2,0},{3,1},{4,6},{5,7},{6,4},{7,5},{8,10},{9,11},{10,... | collective-permute-start | bytes 147464 | tf_op jit(solution)/shard_map/ppermute | solution.py:484
  64.2 2.8 %collective-permute-start.20 = (f32[4,24,128]{2,1,0:T(8,128)S(1)}, f32[4,24,128]{2,1,0:T(8,128)S(1)}, u32[]{:S(2)}, u32[]{:S(2)}) collective-permute-start(f32[4,24,128]{2,1,0:T(8,128)S(1)} %pad_maximum_fusion.refs_20_), channel_id=1, source_target_pairs={{0,1},{1,0},{2,3},{3,2},{4,5},{5,4},{6,7},{7,6},{8,9},{9,8},{10,11... | collective-permute-start | bytes 147464 | tf_op jit(solution)/shard_map/ppermute | solution.py:484

commit v5 on v4

--- a/solution.py
+++ b/solution.py
@@ -586,7 +586,7 @@
                 pltpu.SMEM((len(places) + 1, 8, 128), F32),
                 pltpu.SemaphoreType.DMA((len(places) + 1,)),
             ],
-            microseconds={0: 7, 6: 5, 10: 3}.get(places[0], 3),
+            microseconds={0: 9, 6: 5, 10: 3}.get(places[0], 3),
         )(*after, piece, *[pieces[place] for place in places], lefts, *inputs)
 
     def hold(value, *others):
@@ -618,7 +618,7 @@
         once = passed_along(piece, "leaf", 4)
         twice = passed_along(once, "leaf", 4)
         thrice = passed_along(twice, "leaf", 4)
-        near, edges = near_apply(True, (thrice,), right_side, following, preceding)
+        near, edges = near_apply(True, (once,), right_side, following, preceding)
         put(0, piece)
         put(1, swapped(piece, "leaf", 2))
         put(2, once)

time: 84.4 us -> 77.1 us (0.914); the launches traced: 83.1 us -> 77.2 us
  starting transfers between devices: 20.1 us -> 17.5 us
  local copies, waits for them, and re-layouts: 2.02 us -> 0.03 us
  blocking collectives: 10.5 us -> 9.45 us
  waiting for transfers between devices: 21.4 us -> 20.4 us
    ppermute x8, starting transfers between devices: 11.7 us -> 8.93 us  [passed_along(): lax.ppermute(block, axis, [((i - distance) % size, i) for i in range(size)])]
    ppermute x8, waiting for transfers between devices: 19.3 us -> 16.9 us  [passed_along(): lax.ppermute(block, axis, [((i - distance) % size, i) for i in range(size)])]
    unnamed x18 -> x14, local copies, waits for them, and re-layouts: 2.02 us -> 0.03 us
    ppermute x15, waiting for transfers between devices: 2.05 us -> 3.54 us  [swapped(): lax.ppermute(block, axis, [(i, i ^ bit) for i in range(lax.axis_size(axis...]
    all_to_all x1, blocking collectives: 10.5 us -> 9.45 us  [exchanged(): return lax.all_to_all(blocks, axis, split_axis=0, concat_axis=0, tiled=True)]
    pallas_call x2, Pallas kernels: 5.07 us -> 6 us  [near_apply(): kernel_call(functools.partial(near_kernel, halo, len(follow)), 'near_firs...]
  transfers between devices with their start and end apart: 23 -> 23, of which waited for: 8 -> 9; matrix products, arithmetic and copies ran while one was open for 0% -> 0% of each run, Pallas kernels for 19% -> 22%
where the time goes in v5:
time: 77.1 us; the launch traced here: 77.2 us
  Pallas kernels  29 us (38%)
  waiting for transfers between devices  20.4 us (26%)
  starting transfers between devices  17.5 us (23%)
  blocking collectives  9.45 us (12%)
  between operations  0.82 us (1%)
    ppermute x8, waiting for transfers between devices, passed_along(): lax.ppermute(block, axis, [((i - distance) % size, i) for i in range(size)])  16.9 us
    pallas_call x4, Pallas kernels, group_call(): kernel_call(functools.partial(body, 'leaf', devices, capacity, places), n...  13.4 us
    all_to_all x1, blocking collectives, exchanged(): return lax.all_to_all(blocks, axis, split_axis=0, concat_axis=0, tiled=True)  9.45 us
    ppermute x8, starting transfers between devices, passed_along(): lax.ppermute(block, axis, [((i - distance) % size, i) for i in range(size)])  8.93 us
    ppermute x15, starting transfers between devices, swapped(): lax.ppermute(block, axis, [(i, i ^ bit) for i in range(lax.axis_size(axis...  8.55 us
    pallas_call x2, Pallas kernels, near_apply(): kernel_call(functools.partial(near_kernel, halo, len(follow)), 'near_firs...  6 us
    pallas_call x1, Pallas kernels, on_device(): kernel_call(functools.partial(second_kernel, reach, 'leaf', devices, grou...  4.86 us
    pallas_call x1, Pallas kernels, on_device(): kernel_call(functools.partial(prepare_kernel, devices, capacity), 'prepar...  3.86 us
  transfers between devices with their start and end apart: 23, of which 9 were waited for; matrix products, arithmetic and copies ran while one was open for 0% of the time, Pallas kernels for 22%

profile of v5, /device:TPU:0, one launch (start us, length us, event | category | flops | bytes accessed | tf_op | source)
XLA Modules:
  0.0 77.2 jit_solution(16910248215294849341)
XLA Ops:
  0.7 3.9 %prepare.1 = (f32[592,128]{1,0:T(8,128)}, f32[8,128,256]{2,1,0:T(8,128)}, f32[8,128,256]{2,1,0:T(8,128)}, bf16[9,208,128]{2,1,0:T(8,128)(2,1)}, f32[2,72,256]{2,1,0:T(8,128)}, /*index=5*/f32[2,72,256]{2,1,0:T(8,128)}) custom-call(f32[8,64,256]{2,1,0:T(8,128)} %refs_0_.3, f32[8,256]{1,0:T(8,128)} %values.1, s32[2,8]{1,0:T(2,128)} %bitcast.8, ...), custom_call_target="tpu_custom_call" | custom-call | flops 2000000000 | bytes 6000000 | tf_op jit(solution)/shard_map/prepare/pallas_call | solution.py:512
  4.5 3.1 %collective-permute-start = (f32[592,128]{1,0:T(8,128)}, f32[592,128]{1,0:T(8,128)S(1)}, u32[]{:S(2)}, u32[]{:S(2)}) collective-permute-start(f32[592,128]{1,0:T(8,128)} %get-tuple-element.39.refs_1_.refs_2_.refs_0_), channel_id=1, source_target_pairs={{12,0},{13,1},{14,2},{15,3},{0,4},{1,5},{2,6},{3,7},{4,8},{5,9},{6... | collective-permute-start | bytes 909320 | tf_op jit(solution)/shard_map/ppermute | solution.py:480
  7.6 1.5 %collective-permute-start.3 = (f32[592,128]{1,0:T(8,128)}, f32[592,128]{1,0:T(8,128)S(1)}, u32[]{:S(2)}, u32[]{:S(2)}) collective-permute-start(f32[592,128]{1,0:T(8,128)} %get-tuple-element.39.refs_1_.refs_2_.refs_0_), channel_id=1, source_target_pairs={{0,2},{1,3},{2,0},{3,1},{4,6},{5,7},{6,4},{7,5},{8,10},{9,11},{10,... | collective-permute-start | bytes 909320 | tf_op jit(solution)/shard_map/ppermute | solution.py:484
  9.1 1.2 %collective-permute-start.14 = (f32[2,72,256]{2,1,0:T(8,128)}, f32[2,72,256]{2,1,0:T(8,128)S(1)}, u32[]{:S(2)}, u32[]{:S(2)}) collective-permute-start(f32[2,72,256]{2,1,0:T(8,128)} %get-tuple-element.53), channel_id=1, source_target_pairs={{1,0},{2,1},{3,2},{4,3},{5,4},{6,5},{7,6},{8,7},{9,8},{10,9},{11,1... | collective-permute-start | bytes 442376 | tf_op jit(solution)/shard_map/ppermute | solution.py:480
  10.3 6.8 %collective-permute-done.refs_6_.refs_0_ = f32[592,128]{1,0:T(8,128)S(1)} collective-permute-done((f32[592,128]{1,0:T(8,128)}, f32[592,128]{1,0:T(8,128)S(1)}, u32[]{:S(2)}, u32[]{:S(2)}) %collective-permute-start) | collective-permute-done | bytes 303136 | tf_op jit(solution)/shard_map/ppermute | solution.py:480
  17.1 1.5 %collective-permute-done.3.refs_4_ = f32[592,128]{1,0:T(8,128)S(1)} collective-permute-done((f32[592,128]{1,0:T(8,128)}, f32[592,128]{1,0:T(8,128)S(1)}, u32[]{:S(2)}, u32[]{:S(2)}) %collective-permute-start.3) | collective-permute-done | bytes 303136 | tf_op jit(solution)/shard_map/ppermute | solution.py:484
  18.7 2.4 %collective-permute-start.6 = (f32[592,128]{1,0:T(8,128)S(1)}, f32[592,128]{1,0:T(8,128)S(1)}, u32[]{:S(2)}, u32[]{:S(2)}) collective-permute-start(f32[592,128]{1,0:T(8,128)S(1)} %collective-permute-done.refs_6_.refs_0_), channel_id=1, source_target_pairs={{0,2},{1,3},{2,0},{3,1},{4,6},{5,7},{6,4},{7,5},{8,10},{9,11},{10,... | collective-permute-start | bytes 909320 | tf_op jit(solution)/shard_map/ppermute | solution.py:484
  21.0 0.2 collective-permute-start.5
  21.3 3.3 %near_first.1 = (f32[8,256]{1,0:T(8,128)S(1)}, f32[6,256,256]{2,1,0:T(8,128)S(1)}) custom-call(f32[592,128]{1,0:T(8,128)S(1)} %collective-permute-done.refs_6_.refs_0_, f32[8,64,256]{2,1,0:T(8,128)S(1)} %copy-done.3, f32[8,256]{1,0:T(8,128)S(1)} %copy-done.2, s32[2,8]{1,0:T(2,128)S(1)} %bitcast.9, f32[2,72,256]{2,1,0:T(8,128)S(1)} %collective-permute-done.14.refs_4_, ...), custom_call_target="tpu_custom_call" | custom-call | flops 3000000000 | bytes 9000000 | tf_op jit(solution)/shard_map/near_first/pallas_call | solution.py:546
  24.6 2.7 %collective-permute-done.1.refs_0_.refs_4_ = f32[592,128]{1,0:T(8,128)S(1)} collective-permute-done((f32[592,128]{1,0:T(8,128)S(1)}, f32[592,128]{1,0:T(8,128)S(1)}, u32[]{:S(2)}, u32[]{:S(2)}) %collective-permute-start.1) | collective-permute-done | bytes 303136 | tf_op jit(solution)/shard_map/ppermute | solution.py:480
  27.2 1.2 %collective-permute-start.9 = (f32[592,128]{1,0:T(8,128)S(1)}, f32[592,128]{1,0:T(8,128)S(1)}, u32[]{:S(2)}, u32[]{:S(2)}) collective-permute-start(f32[592,128]{1,0:T(8,128)S(1)} %collective-permute-done.1.refs_0_.refs_4_), channel_id=1, source_target_pairs={{0,2},{1,3},{2,0},{3,1},{4,6},{5,7},{6,4},{7,5},{8,10},{9,11},{10,... | collective-permute-start | bytes 909320 | tf_op jit(solution)/shard_map/ppermute | solution.py:484
  28.5 0.4 collective-permute-done.6.refs_2_
  28.9 0.1 collective-permute-start.7
  29.0 4.6 %far_tiles_0.1 = (s32[60]{0:T(128)S(1)}, s32[60]{0:T(128)S(1)}, s32[1]{0:T(128)}, f32[60,128,128]{2,1,0:T(8,128)S(1)}, f32[6,128,128]{2,1,0:T(8,128)S(1)}, /*index=5*/f32[10,128,128]{2,1,0:T(8,128)S(1)}) custom-call(f32[592,128]{1,0:T(8,128)S(1)} %collective-permute-done.1.refs_0_.refs_4_, f32[592,128]{1,0:T(8,128)S(1)} %copy-done.4, ...), custom_call_target="tpu_custom_call" | custom-call | flops 8999999488 | bytes 27000000 | tf_op jit(solution)/shard_map/far_tiles_0/pallas_call | solution.py:572
  33.6 2.8 %collective-permute-done.11.refs_3_ = f32[592,128]{1,0:T(8,128)S(1)} collective-permute-done((f32[592,128]{1,0:T(8,128)S(1)}, f32[592,128]{1,0:T(8,128)S(1)}, u32[]{:S(2)}, u32[]{:S(2)}) %collective-permute-start.11) | collective-permute-done | bytes 303136 | tf_op jit(solution)/shard_map/ppermute | solution.py:480
  36.4 0.6 collective-permute-start.13
  37.1 0.5 collective-permute-start.10
  37.6 3.0 %far_tiles_1.1 = (s32[44]{0:T(128)S(1)}, s32[44]{0:T(128)S(1)}, s32[1]{0:T(128)}, f32[44,128,128]{2,1,0:T(8,128)S(1)}, f32[4,128,128]{2,1,0:T(8,128)S(1)}, /*index=5*/f32[10,128,128]{2,1,0:T(8,128)S(1)}) custom-call(f32[592,128]{1,0:T(8,128)S(1)} %collective-permute-done.1.refs_0_.refs_4_, f32[592,128]{1,0:T(8,128)S(1)} %copy-done.4, ...), custom_call_target="tpu_custom_call" | custom-call | flops 5000000000 | bytes 15000000 | tf_op jit(solution)/shard_map/far_tiles_1/pallas_call | solution.py:572
  40.7 3.3 %far_tiles_2.1 = (s32[44]{0:T(128)S(1)}, s32[44]{0:T(128)S(1)}, s32[1]{0:T(128)}, f32[44,128,128]{2,1,0:T(8,128)S(1)}, f32[4,128,128]{2,1,0:T(8,128)S(1)}, /*index=5*/f32[10,128,128]{2,1,0:T(8,128)S(1)}) custom-call(f32[592,128]{1,0:T(8,128)S(1)} %copy-done.4, f32[592,128]{1,0:T(8,128)S(1)} %collective-permute-done.9.refs_1_, ...), custom_call_target="tpu_custom_call" | custom-call | flops 3000000000 | bytes 9000000 | tf_op jit(solution)/shard_map/far_tiles_2/pallas_call | solution.py:572
  44.1 1.6 %collective-permute-done.16.refs_2_ = f32[592,128]{1,0:T(8,128)S(1)} collective-permute-done((f32[592,128]{1,0:T(8,128)S(1)}, f32[592,128]{1,0:T(8,128)S(1)}, u32[]{:S(2)}, u32[]{:S(2)}) %collective-permute-start.16) | collective-permute-done | bytes 303136 | tf_op jit(solution)/shard_map/ppermute | solution.py:484
  45.7 2.5 %far_last.1 = (s32[28]{0:T(128)S(1)}, s32[28]{0:T(128)S(1)}, s32[1]{0:T(128)}, f32[28,128,128]{2,1,0:T(8,128)S(1)}, f32[2,128,128]{2,1,0:T(8,128)S(1)}, /*index=5*/f32[8,256]{1,0:T(8,128)S(1)}, f32[24,128]{1,0:T(8,128)S(1)}) custom-call(f32[592,128]{1,0:T(8,128)S(1)} %copy-done.4, f32[592,128]{1,0:T(8,128)S(1)} %collective-permute-done.13.refs_1_, ...), custom_call_target="tpu_custom_call" | custom-call | flops 3000000000 | bytes 9000000 | tf_op jit(solution)/shard_map/far_last/pallas_call | solution.py:572
  48.2 3.7 %collective-permute-start.19 = (f32[24,128]{1,0:T(8,128)S(1)}, f32[24,128]{1,0:T(8,128)S(1)}, u32[]{:S(2)}, u32[]{:S(2)}) collective-permute-start(f32[24,128]{1,0:T(8,128)S(1)} %get-tuple-element.70), channel_id=1, source_target_pairs={{4,0},{5,1},{6,2},{7,3},{8,4},{9,5},{10,6},{11,7},{12,8},{13,9},{1... | collective-permute-start | bytes 36872 | tf_op jit(solution)/shard_map/ppermute | solution.py:480
  51.9 0.9 %collective-permute-start.17 = (f32[24,128]{1,0:T(8,128)S(1)}, f32[24,128]{1,0:T(8,128)S(1)}, u32[]{:S(2)}, u32[]{:S(2)}) collective-permute-start(f32[24,128]{1,0:T(8,128)S(1)} %get-tuple-element.70), channel_id=1, source_target_pairs={{12,0},{13,1},{14,2},{15,3},{0,4},{1,5},{2,6},{3,7},{4,8},{5,9},{6... | collective-permute-start | bytes 36872 | tf_op jit(solution)/shard_map/ppermute | solution.py:480
  52.8 0.5 collective-permute-done.19
  53.3 3.2 %collective-permute-done.18 = f32[24,128]{1,0:T(8,128)S(1)} collective-permute-done((f32[24,128]{1,0:T(8,128)S(1)}, f32[24,128]{1,0:T(8,128)S(1)}, u32[]{:S(2)}, u32[]{:S(2)}) %collective-permute-start.18) | collective-permute-done | bytes 12320 | tf_op jit(solution)/shard_map/ppermute | solution.py:480
  56.5 0.9 %collective-permute-done.17 = f32[24,128]{1,0:T(8,128)S(1)} collective-permute-done((f32[24,128]{1,0:T(8,128)S(1)}, f32[24,128]{1,0:T(8,128)S(1)}, u32[]{:S(2)}, u32[]{:S(2)}) %collective-permute-start.17) | collective-permute-done | bytes 12320 | tf_op jit(solution)/shard_map/ppermute | solution.py:480
  57.4 1.1 %collective-permute-start.21 = (f32[4,24,128]{2,1,0:T(8,128)S(1)}, f32[4,24,128]{2,1,0:T(8,128)S(1)}, u32[]{:S(2)}, u32[]{:S(2)}) collective-permute-start(f32[4,24,128]{2,1,0:T(8,128)S(1)} %pad_maximum_fusion.refs_20_), channel_id=1, source_target_pairs={{0,2},{1,3},{2,0},{3,1},{4,6},{5,7},{6,4},{7,5},{8,10},{9,11},{10,... | collective-permute-start | bytes 147464 | tf_op jit(solution)/shard_map/ppermute | solution.py:484
  58.5 0.8 collective-permute-start.20
  59.3 2.7 %near_second.1.refs_28_ = f32[8,256]{1,0:T(8,128)S(1)} custom-call(f32[8,64,256]{2,1,0:T(8,128)S(1)} %copy-done.3, f32[8,256]{1,0:T(8,128)S(1)} %get-tuple-element.71.refs_1_.refs_27_.image, s32[2,8]{1,0:T(2,128)S(1)} %bitcast.10), custom_call_target="tpu_custom_call" | custom-call | flops 4000000000 | bytes 12000000 | tf_op jit(solution)/shard_map/near_second/pallas_call | solution.py:546
  62.1 4.9 %far_second.1 = (f32[8,256]{1,0:T(8,128)S(1)}, f32[8,256]{1,0:T(8,128)S(1)}, f32[16,1,128]{2,1,0:T(1,128)S(1)}) custom-call(s32[60]{0:T(128)S(1)} %get-tuple-element.41.refs_0_, s32[60]{0:T(128)S(1)} %get-tuple-element.42.refs_1_, s32[1]{0:T(128)} %get-tuple-element.43.refs_2_, s32[44]{0:T(128)S(1)} %get-tuple-element.45.refs_3_, ...), custom_call_target="tpu_custom_call" | custom-call | flops 1000000000 | bytes 3000000 | tf_op jit(solution)/shard_map/far_second/pallas_call | solution.py:649
  66.9 9.5 %all_to_all.5.everyone = f32[16,1,128]{2,1,0:T(1,128)S(1)} all-to-all(f32[16,1,128]{2,1,0:T(1,128)S(1)} %get-tuple-element.73), channel_id=1, replica_groups=mesh['groups'=2,'leaf'=16] {'leaf'}, dimensions={0} | all-to-all | bytes 16384 | tf_op jit(solution)/shard_map/all_to_all | solution.py:488
  76.4 0.9 %finish.1 = (f32[8,256]{1,0:T(8,128)}, f32[8,256]{1,0:T(8,128)}) custom-call(f32[16,1,128]{2,1,0:T(1,128)S(1)} %all_to_all.5.everyone, f32[8,256]{1,0:T(8,128)S(1)} %copy-done.2, f32[8,256]{1,0:T(8,128)S(1)} %get-tuple-element.71.refs_1_.refs_27_.image, f32[8,256]{1,0:T(8,128)S(1)} %get-tuple-element.74.residual, f32[8,256]{1,0:T(8,128)S(1)} %get-tuple-element.75.along), custom_call_target="tpu_custom_call" | custom-call | flops 1000000000 | bytes 3000000 | tf_op jit(solution)/shard_map/finish/pallas_call | solution.py:671
  (39 shorter events, 0.2 us)
Async XLA Ops:
  0.6 20.6 %copy-start.2 = (f32[8,256]{1,0:T(8,128)S(1)}, f32[8,256]{1,0:T(8,128)}, u32[]{:S(2)}) copy-start(f32[8,256]{1,0:T(8,128)} %values.1) | copy-start | bytes 24580
  0.6 20.6 %copy-start.3 = (f32[8,64,256]{2,1,0:T(8,128)S(1)}, f32[8,64,256]{2,1,0:T(8,128)}, u32[]{:S(2)}) copy-start(f32[8,64,256]{2,1,0:T(8,128)} %refs_0_.3) | copy-start | bytes 1572868
  0.7 20.6 %copy-start.5 = (s32[8,2]{0,1:T(2,128)S(1)}, s32[8,2]{0,1:T(2,128)}, u32[]{:S(2)}) copy-start(s32[8,2]{0,1:T(2,128)} %param.9) | copy-start | bytes 196
  4.5 12.6 %collective-permute-start = (f32[592,128]{1,0:T(8,128)}, f32[592,128]{1,0:T(8,128)S(1)}, u32[]{:S(2)}, u32[]{:S(2)}) collective-permute-start(f32[592,128]{1,0:T(8,128)} %get-tuple-element.39.refs_1_.refs_2_.refs_0_), channel_id=1, source_target_pairs={{12,0},{13,1},{14,2},{15,3},{0,4},{1,5},{2,6},{3,7},{4,8},{5,9},{6... | collective-permute-start | bytes 909320 | tf_op jit(solution)/shard_map/ppermute | solution.py:480
  7.6 11.0 %collective-permute-start.3 = (f32[592,128]{1,0:T(8,128)}, f32[592,128]{1,0:T(8,128)S(1)}, u32[]{:S(2)}, u32[]{:S(2)}) collective-permute-start(f32[592,128]{1,0:T(8,128)} %get-tuple-element.39.refs_1_.refs_2_.refs_0_), channel_id=1, source_target_pairs={{0,2},{1,3},{2,0},{3,1},{4,6},{5,7},{6,4},{7,5},{8,10},{9,11},{10,... | collective-permute-start | bytes 909320 | tf_op jit(solution)/shard_map/ppermute | solution.py:484
  9.1 9.5 %collective-permute-start.14 = (f32[2,72,256]{2,1,0:T(8,128)}, f32[2,72,256]{2,1,0:T(8,128)S(1)}, u32[]{:S(2)}, u32[]{:S(2)}) collective-permute-start(f32[2,72,256]{2,1,0:T(8,128)} %get-tuple-element.53), channel_id=1, source_target_pairs={{1,0},{2,1},{3,2},{4,3},{5,4},{6,5},{7,6},{8,7},{9,8},{10,9},{11,1... | collective-permute-start | bytes 442376 | tf_op jit(solution)/shard_map/ppermute | solution.py:480
  10.3 18.7 %copy-start.4 = (f32[592,128]{1,0:T(8,128)S(1)}, f32[592,128]{1,0:T(8,128)}, u32[]{:S(2)}) copy-start(f32[592,128]{1,0:T(8,128)} %get-tuple-element.39.refs_1_.refs_2_.refs_0_) | copy-start | bytes 909316
  10.3 18.7 %copy-start.6 = (bf16[9,208,128]{2,1,0:T(8,128)(2,1)S(1)}, bf16[9,208,128]{2,1,0:T(8,128)(2,1)}, u32[]{:S(2)}) copy-start(bf16[9,208,128]{2,1,0:T(8,128)(2,1)} %get-tuple-element.40.refs_8_.refs_6_.refs_5_.refs_3_) | copy-start | bytes 1437700
  10.3 10.7 %collective-permute-start.15 = (f32[2,72,256]{2,1,0:T(8,128)}, f32[2,72,256]{2,1,0:T(8,128)S(1)}, u32[]{:S(2)}, u32[]{:S(2)}) collective-permute-start(f32[2,72,256]{2,1,0:T(8,128)} %get-tuple-element.54), channel_id=1, source_target_pairs={{15,0},{0,1},{1,2},{2,3},{3,4},{4,5},{5,6},{6,7},{7,8},{8,9},{9,10... | collective-permute-start | bytes 442376 | tf_op jit(solution)/shard_map/ppermute | solution.py:480
  17.1 10.1 %collective-permute-start.1 = (f32[592,128]{1,0:T(8,128)S(1)}, f32[592,128]{1,0:T(8,128)S(1)}, u32[]{:S(2)}, u32[]{:S(2)}) collective-permute-start(f32[592,128]{1,0:T(8,128)S(1)} %collective-permute-done.refs_6_.refs_0_), channel_id=1, source_target_pairs={{12,0},{13,1},{14,2},{15,3},{0,4},{1,5},{2,6},{3,7},{4,8},{5,9},{6... | collective-permute-start | bytes 909320 | tf_op jit(solution)/shard_map/ppermute | solution.py:480
  17.1 10.1 %collective-permute-start.2 = (f32[592,128]{1,0:T(8,128)}, f32[592,128]{1,0:T(8,128)S(1)}, u32[]{:S(2)}, u32[]{:S(2)}) collective-permute-start(f32[592,128]{1,0:T(8,128)} %get-tuple-element.39.refs_1_.refs_2_.refs_0_), channel_id=1, source_target_pairs={{0,1},{1,0},{2,3},{3,2},{4,5},{5,4},{6,7},{7,6},{8,9},{9,8},{10,11... | collective-permute-start | bytes 909320 | tf_op jit(solution)/shard_map/ppermute | solution.py:484
  18.6 9.8 %collective-permute-start.4 = (f32[592,128]{1,0:T(8,128)S(1)}, f32[592,128]{1,0:T(8,128)S(1)}, u32[]{:S(2)}, u32[]{:S(2)}) collective-permute-start(f32[592,128]{1,0:T(8,128)S(1)} %collective-permute-done.3.refs_4_), channel_id=1, source_target_pairs={{0,1},{1,0},{2,3},{3,2},{4,5},{5,4},{6,7},{7,6},{8,9},{9,8},{10,11... | collective-permute-start | bytes 909320 | tf_op jit(solution)/shard_map/ppermute | solution.py:484
  18.7 10.2 %collective-permute-start.6 = (f32[592,128]{1,0:T(8,128)S(1)}, f32[592,128]{1,0:T(8,128)S(1)}, u32[]{:S(2)}, u32[]{:S(2)}) collective-permute-start(f32[592,128]{1,0:T(8,128)S(1)} %collective-permute-done.refs_6_.refs_0_), channel_id=1, source_target_pairs={{0,2},{1,3},{2,0},{3,1},{4,6},{5,7},{6,4},{7,5},{8,10},{9,11},{10,... | collective-permute-start | bytes 909320 | tf_op jit(solution)/shard_map/ppermute | solution.py:484
  21.0 8.0 %collective-permute-start.5 = (f32[592,128]{1,0:T(8,128)S(1)}, f32[592,128]{1,0:T(8,128)S(1)}, u32[]{:S(2)}, u32[]{:S(2)}) collective-permute-start(f32[592,128]{1,0:T(8,128)S(1)} %collective-permute-done.refs_6_.refs_0_), channel_id=1, source_target_pairs={{0,1},{1,0},{2,3},{3,2},{4,5},{5,4},{6,7},{7,6},{8,9},{9,8},{10,11... | collective-permute-start | bytes 909320 | tf_op jit(solution)/shard_map/ppermute | solution.py:484
  27.2 9.2 %collective-permute-start.11 = (f32[592,128]{1,0:T(8,128)S(1)}, f32[592,128]{1,0:T(8,128)S(1)}, u32[]{:S(2)}, u32[]{:S(2)}) collective-permute-start(f32[592,128]{1,0:T(8,128)S(1)} %collective-permute-done.1.refs_0_.refs_4_), channel_id=1, source_target_pairs={{12,0},{13,1},{14,2},{15,3},{0,4},{1,5},{2,6},{3,7},{4,8},{5,9},{6... | collective-permute-start | bytes 909320 | tf_op jit(solution)/shard_map/ppermute | solution.py:480
  27.2 9.8 %collective-permute-start.9 = (f32[592,128]{1,0:T(8,128)S(1)}, f32[592,128]{1,0:T(8,128)S(1)}, u32[]{:S(2)}, u32[]{:S(2)}) collective-permute-start(f32[592,128]{1,0:T(8,128)S(1)} %collective-permute-done.1.refs_0_.refs_4_), channel_id=1, source_target_pairs={{0,2},{1,3},{2,0},{3,1},{4,6},{5,7},{6,4},{7,5},{8,10},{9,11},{10,... | collective-permute-start | bytes 909320 | tf_op jit(solution)/shard_map/ppermute | solution.py:484
  28.5 9.1 %collective-permute-start.8 = (f32[592,128]{1,0:T(8,128)S(1)}, f32[592,128]{1,0:T(8,128)S(1)}, u32[]{:S(2)}, u32[]{:S(2)}) collective-permute-start(f32[592,128]{1,0:T(8,128)S(1)} %collective-permute-done.1.refs_0_.refs_4_), channel_id=1, source_target_pairs={{0,1},{1,0},{2,3},{3,2},{4,5},{5,4},{6,7},{7,6},{8,9},{9,8},{10,11... | collective-permute-start | bytes 909320 | tf_op jit(solution)/shard_map/ppermute | solution.py:484
  28.9 8.7 %collective-permute-start.7 = (f32[592,128]{1,0:T(8,128)S(1)}, f32[592,128]{1,0:T(8,128)S(1)}, u32[]{:S(2)}, u32[]{:S(2)}) collective-permute-start(f32[592,128]{1,0:T(8,128)S(1)} %collective-permute-done.6.refs_2_), channel_id=1, source_target_pairs={{0,1},{1,0},{2,3},{3,2},{4,5},{5,4},{6,7},{7,6},{8,9},{9,8},{10,11... | collective-permute-start | bytes 909320 | tf_op jit(solution)/shard_map/ppermute | solution.py:484
  36.4 7.6 %collective-permute-start.13 = (f32[592,128]{1,0:T(8,128)S(1)}, f32[592,128]{1,0:T(8,128)S(1)}, u32[]{:S(2)}, u32[]{:S(2)}) collective-permute-start(f32[592,128]{1,0:T(8,128)S(1)} %collective-permute-done.11.refs_3_), channel_id=1, source_target_pairs={{0,2},{1,3},{2,0},{3,1},{4,6},{5,7},{6,4},{7,5},{8,10},{9,11},{10,... | collective-permute-start | bytes 909320 | tf_op jit(solution)/shard_map/ppermute | solution.py:484
  37.1 3.6 %collective-permute-start.12 = (f32[592,128]{1,0:T(8,128)S(1)}, f32[592,128]{1,0:T(8,128)S(1)}, u32[]{:S(2)}, u32[]{:S(2)}) collective-permute-start(f32[592,128]{1,0:T(8,128)S(1)} %collective-permute-done.11.refs_3_), channel_id=1, source_target_pairs={{0,1},{1,0},{2,3},{3,2},{4,5},{5,4},{6,7},{7,6},{8,9},{9,8},{10,11... | collective-permute-start | bytes 909320 | tf_op jit(solution)/shard_map/ppermute | solution.py:484
  37.1 3.6 %collective-permute-start.10 = (f32[592,128]{1,0:T(8,128)S(1)}, f32[592,128]{1,0:T(8,128)S(1)}, u32[]{:S(2)}, u32[]{:S(2)}) collective-permute-start(f32[592,128]{1,0:T(8,128)S(1)} %collective-permute-done.9.refs_1_), channel_id=1, source_target_pairs={{0,1},{1,0},{2,3},{3,2},{4,5},{5,4},{6,7},{7,6},{8,9},{9,8},{10,11... | collective-permute-start | bytes 909320 | tf_op jit(solution)/shard_map/ppermute | solution.py:484
  40.7 5.0 %copy-start = (f32[8,128,256]{2,1,0:T(8,128)S(1)}, f32[8,128,256]{2,1,0:T(8,128)}, u32[]{:S(2)}) copy-start(f32[8,128,256]{2,1,0:T(8,128)} %get-tuple-element.57.refs_5_.refs_24_) | copy-start | bytes 3145732
  40.7 5.0 %copy-start.1 = (f32[8,128,256]{2,1,0:T(8,128)S(1)}, f32[8,128,256]{2,1,0:T(8,128)}, u32[]{:S(2)}) copy-start(f32[8,128,256]{2,1,0:T(8,128)} %get-tuple-element.58.refs_6_.refs_25_) | copy-start | bytes 3145732
  44.0 1.7 %collective-permute-start.16 = (f32[592,128]{1,0:T(8,128)S(1)}, f32[592,128]{1,0:T(8,128)S(1)}, u32[]{:S(2)}, u32[]{:S(2)}) collective-permute-start(f32[592,128]{1,0:T(8,128)S(1)} %collective-permute-done.13.refs_1_), channel_id=1, source_target_pairs={{0,1},{1,0},{2,3},{3,2},{4,5},{5,4},{6,7},{7,6},{8,9},{9,8},{10,11... | collective-permute-start | bytes 909320 | tf_op jit(solution)/shard_map/ppermute | solution.py:484
  48.2 5.1 %collective-permute-start.19 = (f32[24,128]{1,0:T(8,128)S(1)}, f32[24,128]{1,0:T(8,128)S(1)}, u32[]{:S(2)}, u32[]{:S(2)}) collective-permute-start(f32[24,128]{1,0:T(8,128)S(1)} %get-tuple-element.70), channel_id=1, source_target_pairs={{4,0},{5,1},{6,2},{7,3},{8,4},{9,5},{10,6},{11,7},{12,8},{13,9},{1... | collective-permute-start | bytes 36872 | tf_op jit(solution)/shard_map/ppermute | solution.py:480
  51.9 4.6 %collective-permute-start.18 = (f32[24,128]{1,0:T(8,128)S(1)}, f32[24,128]{1,0:T(8,128)S(1)}, u32[]{:S(2)}, u32[]{:S(2)}) collective-permute-start(f32[24,128]{1,0:T(8,128)S(1)} %get-tuple-element.70), channel_id=1, source_target_pairs={{8,0},{9,1},{10,2},{11,3},{12,4},{13,5},{14,6},{15,7},{0,8},{1,9},... | collective-permute-start | bytes 36872 | tf_op jit(solution)/shard_map/ppermute | solution.py:480
  51.9 5.5 %collective-permute-start.17 = (f32[24,128]{1,0:T(8,128)S(1)}, f32[24,128]{1,0:T(8,128)S(1)}, u32[]{:S(2)}, u32[]{:S(2)}) collective-permute-start(f32[24,128]{1,0:T(8,128)S(1)} %get-tuple-element.70), channel_id=1, source_target_pairs={{12,0},{13,1},{14,2},{15,3},{0,4},{1,5},{2,6},{3,7},{4,8},{5,9},{6... | collective-permute-start | bytes 36872 | tf_op jit(solution)/shard_map/ppermute | solution.py:480
  57.4 4.6 %collective-permute-start.22 = (f32[4,24,128]{2,1,0:T(8,128)S(1)}, f32[4,24,128]{2,1,0:T(8,128)S(1)}, u32[]{:S(2)}, u32[]{:S(2)}) collective-permute-start(f32[4,24,128]{2,1,0:T(8,128)S(1)} %pad_maximum_fusion.refs_20_), channel_id=1, source_target_pairs={{0,3},{1,2},{2,1},{3,0},{4,7},{5,6},{6,5},{7,4},{8,11},{9,10},{10,... | collective-permute-start | bytes 147464 | tf_op jit(solution)/shard_map/ppermute | solution.py:484
  57.4 4.6 %collective-permute-start.21 = (f32[4,24,128]{2,1,0:T(8,128)S(1)}, f32[4,24,128]{2,1,0:T(8,128)S(1)}, u32[]{:S(2)}, u32[]{:S(2)}) collective-permute-start(f32[4,24,128]{2,1,0:T(8,128)S(1)} %pad_maximum_fusion.refs_20_), channel_id=1, source_target_pairs={{0,2},{1,3},{2,0},{3,1},{4,6},{5,7},{6,4},{7,5},{8,10},{9,11},{10,... | collective-permute-start | bytes 147464 | tf_op jit(solution)/shard_map/ppermute | solution.py:484
  58.5 3.5 %collective-permute-start.20 = (f32[4,24,128]{2,1,0:T(8,128)S(1)}, f32[4,24,128]{2,1,0:T(8,128)S(1)}, u32[]{:S(2)}, u32[]{:S(2)}) collective-permute-start(f32[4,24,128]{2,1,0:T(8,128)S(1)} %pad_maximum_fusion.refs_20_), channel_id=1, source_target_pairs={{0,1},{1,0},{2,3},{3,2},{4,5},{5,4},{6,7},{7,6},{8,9},{9,8},{10,11... | collective-permute-start | bytes 147464 | tf_op jit(solution)/shard_map/ppermute | solution.py:484

commit v6 on v5

--- a/solution.py
+++ b/solution.py
@@ -12,6 +12,7 @@
 BF16 = jnp.bfloat16
 VMEM_LIMIT = 20 * 1024 * 1024
 UNROLL = 4
+PARTS = 4
 GRID_DEVICES = 16
 ORDER = ((0, 0), (0, 1), (1, 0), (1, 1), (2, 0), (2, 1), (3, 0), (3, 1))
 CUTS = (0, 6, 10, 14, 16)
@@ -301,12 +302,12 @@
     lax.fori_loop(0, (filled + UNROLL - 1) // UNROLL, step, 0)
 
 
-def far_rows(sums, to_skel, to_top):
+def far_rows(sum_of, mixed, to_skel, to_top):
     leaves = to_skel.shape[0]
-    mixed = jnp.sum(sums[leaves + 1], axis=1, keepdims=True)
+    mixed = jnp.sum(mixed, axis=1, keepdims=True)
     far, top = [], []
     for l in range(leaves):
-        far.append(jnp.sum(to_skel[l] * jnp.sum(sums[l], axis=1, keepdims=True), axis=0, keepdims=True))
+        far.append(jnp.sum(to_skel[l] * jnp.sum(sum_of(l), axis=1, keepdims=True), axis=0, keepdims=True))
         top.append(jnp.sum(to_top[l] * mixed, axis=0, keepdims=True))
     return jnp.concatenate(far, axis=0), jnp.concatenate(top, axis=0)
 
@@ -350,7 +351,7 @@
         (targets, vectors, count), tiles, tops, sums, refs[n + 15:],
     )
     leaves, rank, size = to_skel.shape
-    far, top = far_rows(sums, to_skel, to_top)
+    far, top = far_rows(lambda l: sums[l], sums[leaves + 1], to_skel, to_top)
     start = values[...]
     result = start + 0.25 * near[...] + 0.125 * far + 0.25 * top
     image[...] = result
@@ -377,7 +378,7 @@
     tiles, refs = refs[:len(groups)], refs[len(groups):]
     tops, refs = refs[:len(groups)], refs[len(groups):]
     received, refs = refs[:1 if devices != GRID_DEVICES else 4], refs[1 if devices != GRID_DEVICES else 4:]
-    to_skel, to_top, values, image, near, edges, residual, along, numbers, everyone, sums, across, beside = refs
+    to_skel, to_top, values, image, near, edges, residual, along, numbers, everyone, *sums, across, beside = refs
     leaves, rank, size = to_skel.shape
     me = lax.axis_index(axis)
     if devices != GRID_DEVICES:
@@ -387,7 +388,9 @@
             for turn in range(4):
                 source = (((me >> 2) - turn + 4) & 3) * 4 + ((me & 3) ^ other)
                 everyone[source] = blocks[turn]
-    sums[...] = jnp.zeros_like(sums)
+    for part in sums:
+        part[...] = jnp.zeros_like(part)
+    mixed = jnp.zeros((rank, rank), F32)
     for g, places in enumerate(groups):
         targets, vectors, count = lists[3 * g:3 * g + 3]
 
@@ -397,14 +400,14 @@
                 vector = vectors[n * UNROLL + k]
                 products.append(tiles[g][n * UNROLL + k] * everyone[lax.div(vector, leaves), pl.ds(lax.rem(vector, leaves), 1), :])
             for k in range(UNROLL):
-                sums[targets[n * UNROLL + k]] += products[k]
+                sums[k % len(sums)][targets[n * UNROLL + k]] += products[k]
             return carry
 
         lax.fori_loop(0, (count[0] + UNROLL - 1) // UNROLL, step, 0)
         for n, place in enumerate(places):
             device = owner_of(place, me, devices)
-            sums[leaves + 1] += tops[g][n] * everyone[device, leaves:leaves + 1, :]
-    far, top = far_rows(sums, to_skel, to_top)
+            mixed = mixed + tops[g][n] * everyone[device, leaves:leaves + 1, :]
+    far, top = far_rows(lambda l: sum(part[l] for part in sums), mixed, to_skel, to_top)
 
     before, after = edges_of(leaves, reach)
     across[...] = jnp.zeros_like(across)
@@ -657,7 +660,9 @@
         ],
         [
             pltpu.VMEM((devices, payload_rows, rank), F32),
-            pltpu.VMEM(sums.shape, F32),
+        ]
+        + [pltpu.VMEM((leaves + 1, rank, rank), F32)] * PARTS
+        + [
             pltpu.VMEM((reach, size, 128), F32),
             pltpu.VMEM((reach, 8, size), F32),
         ],

time: 77.1 us -> 77.3 us (level)
  Pallas kernels: 29 us -> 26.9 us
  waiting for transfers between devices: 20.4 us -> 21.4 us
    pallas_call x2, Pallas kernels: 6 us -> 4.86 us  [near_apply(): kernel_call(functools.partial(near_kernel, halo, len(follow)), 'near_firs...]
    pallas_call x4, Pallas kernels: 13.4 us -> 12.6 us  [group_call(): kernel_call(functools.partial(body, 'leaf', devices, capacity, places), n...]
  transfers between devices with their start and end apart: 23 -> 23, of which waited for: 9 -> 11; matrix products, arithmetic and copies ran while one was open for 0% -> 0% of each run, Pallas kernels for 22% -> 19%
where the time goes in v6:
time: 77.3 us; the launch traced here: 76.9 us
  Pallas kernels  26.9 us (35%)
  waiting for transfers between devices  21.4 us (28%)
  starting transfers between devices  17.6 us (23%)
  blocking collectives  10.2 us (13%)
  between operations  0.8 us (1%)
    ppermute x8, waiting for transfers between devices, passed_along(): lax.ppermute(block, axis, [((i - distance) % size, i) for i in range(size)])  17.4 us
    pallas_call x4, Pallas kernels, group_call(): kernel_call(functools.partial(body, 'leaf', devices, capacity, places), n...  12.6 us
    all_to_all x1, blocking collectives, exchanged(): return lax.all_to_all(blocks, axis, split_axis=0, concat_axis=0, tiled=True)  10.2 us
    ppermute x15, starting transfers between devices, swapped(): lax.ppermute(block, axis, [(i, i ^ bit) for i in range(lax.axis_size(axis...  8.85 us
    ppermute x8, starting transfers between devices, passed_along(): lax.ppermute(block, axis, [((i - distance) % size, i) for i in range(size)])  8.75 us
    pallas_call x2, Pallas kernels, near_apply(): kernel_call(functools.partial(near_kernel, halo, len(follow)), 'near_firs...  4.86 us
    pallas_call x1, Pallas kernels, on_device(): kernel_call(functools.partial(second_kernel, reach, 'leaf', devices, grou...  4.7 us
    ppermute x15, waiting for transfers between devices, swapped(): lax.ppermute(block, axis, [(i, i ^ bit) for i in range(lax.axis_size(axis...  4.06 us
  transfers between devices with their start and end apart: 23, of which 11 were waited for; matrix products, arithmetic and copies ran while one was open for 0% of the time, Pallas kernels for 19%

profile of v6, /device:TPU:0, one launch (start us, length us, event | category | flops | bytes accessed | tf_op | source)
XLA Modules:
  0.0 76.9 jit_solution(257354521366572619)
XLA Ops:
  0.7 3.9 %prepare.1 = (f32[592,128]{1,0:T(8,128)}, f32[8,128,256]{2,1,0:T(8,128)}, f32[8,128,256]{2,1,0:T(8,128)}, bf16[9,208,128]{2,1,0:T(8,128)(2,1)}, f32[2,72,256]{2,1,0:T(8,128)}, /*index=5*/f32[2,72,256]{2,1,0:T(8,128)}) custom-call(f32[8,64,256]{2,1,0:T(8,128)} %refs_0_.3, f32[8,256]{1,0:T(8,128)} %values.1, s32[2,8]{1,0:T(2,128)} %bitcast.8, ...), custom_call_target="tpu_custom_call" | custom-call | flops 2000000000 | bytes 6000000 | tf_op jit(solution)/shard_map/prepare/pallas_call | solution.py:515
  4.5 3.1 %collective-permute-start = (f32[592,128]{1,0:T(8,128)}, f32[592,128]{1,0:T(8,128)S(1)}, u32[]{:S(2)}, u32[]{:S(2)}) collective-permute-start(f32[592,128]{1,0:T(8,128)} %get-tuple-element.39.refs_1_.refs_2_.refs_0_), channel_id=1, source_target_pairs={{12,0},{13,1},{14,2},{15,3},{0,4},{1,5},{2,6},{3,7},{4,8},{5,9},{6... | collective-permute-start | bytes 909320 | tf_op jit(solution)/shard_map/ppermute | solution.py:483
  7.6 1.5 %collective-permute-start.3 = (f32[592,128]{1,0:T(8,128)}, f32[592,128]{1,0:T(8,128)S(1)}, u32[]{:S(2)}, u32[]{:S(2)}) collective-permute-start(f32[592,128]{1,0:T(8,128)} %get-tuple-element.39.refs_1_.refs_2_.refs_0_), channel_id=1, source_target_pairs={{0,2},{1,3},{2,0},{3,1},{4,6},{5,7},{6,4},{7,5},{8,10},{9,11},{10,... | collective-permute-start | bytes 909320 | tf_op jit(solution)/shard_map/ppermute | solution.py:487
  9.1 1.2 %collective-permute-start.14 = (f32[2,72,256]{2,1,0:T(8,128)}, f32[2,72,256]{2,1,0:T(8,128)S(1)}, u32[]{:S(2)}, u32[]{:S(2)}) collective-permute-start(f32[2,72,256]{2,1,0:T(8,128)} %get-tuple-element.53), channel_id=1, source_target_pairs={{1,0},{2,1},{3,2},{4,3},{5,4},{6,5},{7,6},{8,7},{9,8},{10,9},{11,1... | collective-permute-start | bytes 442376 | tf_op jit(solution)/shard_map/ppermute | solution.py:483
  10.3 6.8 %collective-permute-done.refs_6_.refs_0_ = f32[592,128]{1,0:T(8,128)S(1)} collective-permute-done((f32[592,128]{1,0:T(8,128)}, f32[592,128]{1,0:T(8,128)S(1)}, u32[]{:S(2)}, u32[]{:S(2)}) %collective-permute-start) | collective-permute-done | bytes 303136 | tf_op jit(solution)/shard_map/ppermute | solution.py:483
  17.1 1.5 %collective-permute-done.3.refs_4_ = f32[592,128]{1,0:T(8,128)S(1)} collective-permute-done((f32[592,128]{1,0:T(8,128)}, f32[592,128]{1,0:T(8,128)S(1)}, u32[]{:S(2)}, u32[]{:S(2)}) %collective-permute-start.3) | collective-permute-done | bytes 303136 | tf_op jit(solution)/shard_map/ppermute | solution.py:487
  18.7 2.4 %collective-permute-start.6 = (f32[592,128]{1,0:T(8,128)S(1)}, f32[592,128]{1,0:T(8,128)S(1)}, u32[]{:S(2)}, u32[]{:S(2)}) collective-permute-start(f32[592,128]{1,0:T(8,128)S(1)} %collective-permute-done.refs_6_.refs_0_), channel_id=1, source_target_pairs={{0,2},{1,3},{2,0},{3,1},{4,6},{5,7},{6,4},{7,5},{8,10},{9,11},{10,... | collective-permute-start | bytes 909320 | tf_op jit(solution)/shard_map/ppermute | solution.py:487
  21.0 0.2 collective-permute-start.5
  21.3 2.6 %near_first.1 = (f32[8,256]{1,0:T(8,128)S(1)}, f32[6,256,256]{2,1,0:T(8,128)S(1)}) custom-call(f32[592,128]{1,0:T(8,128)S(1)} %collective-permute-done.refs_6_.refs_0_, f32[8,64,256]{2,1,0:T(8,128)S(1)} %copy-done.3, f32[8,256]{1,0:T(8,128)S(1)} %copy-done.2, s32[2,8]{1,0:T(2,128)S(1)} %bitcast.9, f32[2,72,256]{2,1,0:T(8,128)S(1)} %collective-permute-done.14.refs_4_, ...), custom_call_target="tpu_custom_call" | custom-call | flops 3000000000 | bytes 9000000 | tf_op jit(solution)/shard_map/near_first/pallas_call | solution.py:549
  23.9 3.4 %collective-permute-done.1.refs_0_.refs_4_ = f32[592,128]{1,0:T(8,128)S(1)} collective-permute-done((f32[592,128]{1,0:T(8,128)S(1)}, f32[592,128]{1,0:T(8,128)S(1)}, u32[]{:S(2)}, u32[]{:S(2)}) %collective-permute-start.1) | collective-permute-done | bytes 303136 | tf_op jit(solution)/shard_map/ppermute | solution.py:483
  27.2 1.2 %collective-permute-start.9 = (f32[592,128]{1,0:T(8,128)S(1)}, f32[592,128]{1,0:T(8,128)S(1)}, u32[]{:S(2)}, u32[]{:S(2)}) collective-permute-start(f32[592,128]{1,0:T(8,128)S(1)} %collective-permute-done.1.refs_0_.refs_4_), channel_id=1, source_target_pairs={{0,2},{1,3},{2,0},{3,1},{4,6},{5,7},{6,4},{7,5},{8,10},{9,11},{10,... | collective-permute-start | bytes 909320 | tf_op jit(solution)/shard_map/ppermute | solution.py:487
  28.5 0.6 collective-permute-done.6.refs_2_
  29.1 4.3 %far_tiles_0.1 = (s32[60]{0:T(128)S(1)}, s32[60]{0:T(128)S(1)}, s32[1]{0:T(128)}, f32[60,128,128]{2,1,0:T(8,128)S(1)}, f32[6,128,128]{2,1,0:T(8,128)S(1)}, /*index=5*/f32[10,128,128]{2,1,0:T(8,128)S(1)}) custom-call(f32[592,128]{1,0:T(8,128)S(1)} %collective-permute-done.1.refs_0_.refs_4_, f32[592,128]{1,0:T(8,128)S(1)} %copy-done.4, ...), custom_call_target="tpu_custom_call" | custom-call | flops 8999999488 | bytes 27000000 | tf_op jit(solution)/shard_map/far_tiles_0/pallas_call | solution.py:575
  33.4 3.0 %collective-permute-done.11.refs_3_ = f32[592,128]{1,0:T(8,128)S(1)} collective-permute-done((f32[592,128]{1,0:T(8,128)S(1)}, f32[592,128]{1,0:T(8,128)S(1)}, u32[]{:S(2)}, u32[]{:S(2)}) %collective-permute-start.11) | collective-permute-done | bytes 303136 | tf_op jit(solution)/shard_map/ppermute | solution.py:483
  36.4 0.6 collective-permute-start.13
  37.1 0.5 collective-permute-start.10
  37.6 3.0 %far_tiles_1.1 = (s32[44]{0:T(128)S(1)}, s32[44]{0:T(128)S(1)}, s32[1]{0:T(128)}, f32[44,128,128]{2,1,0:T(8,128)S(1)}, f32[4,128,128]{2,1,0:T(8,128)S(1)}, /*index=5*/f32[10,128,128]{2,1,0:T(8,128)S(1)}) custom-call(f32[592,128]{1,0:T(8,128)S(1)} %collective-permute-done.1.refs_0_.refs_4_, f32[592,128]{1,0:T(8,128)S(1)} %copy-done.4, ...), custom_call_target="tpu_custom_call" | custom-call | flops 5000000000 | bytes 15000000 | tf_op jit(solution)/shard_map/far_tiles_1/pallas_call | solution.py:575
  40.7 2.8 %far_tiles_2.1 = (s32[44]{0:T(128)S(1)}, s32[44]{0:T(128)S(1)}, s32[1]{0:T(128)}, f32[44,128,128]{2,1,0:T(8,128)S(1)}, f32[4,128,128]{2,1,0:T(8,128)S(1)}, /*index=5*/f32[10,128,128]{2,1,0:T(8,128)S(1)}) custom-call(f32[592,128]{1,0:T(8,128)S(1)} %copy-done.4, f32[592,128]{1,0:T(8,128)S(1)} %collective-permute-done.9.refs_1_, ...), custom_call_target="tpu_custom_call" | custom-call | flops 3000000000 | bytes 9000000 | tf_op jit(solution)/shard_map/far_tiles_2/pallas_call | solution.py:575
  43.5 0.4 collective-permute-done.13.refs_1_
  43.8 0.3 collective-permute-start.16
  44.1 1.3 %collective-permute-done.16.refs_2_ = f32[592,128]{1,0:T(8,128)S(1)} collective-permute-done((f32[592,128]{1,0:T(8,128)S(1)}, f32[592,128]{1,0:T(8,128)S(1)}, u32[]{:S(2)}, u32[]{:S(2)}) %collective-permute-start.16) | collective-permute-done | bytes 303136 | tf_op jit(solution)/shard_map/ppermute | solution.py:487
  45.4 2.5 %far_last.1 = (s32[28]{0:T(128)S(1)}, s32[28]{0:T(128)S(1)}, s32[1]{0:T(128)}, f32[28,128,128]{2,1,0:T(8,128)S(1)}, f32[2,128,128]{2,1,0:T(8,128)S(1)}, /*index=5*/f32[8,256]{1,0:T(8,128)S(1)}, f32[24,128]{1,0:T(8,128)S(1)}) custom-call(f32[592,128]{1,0:T(8,128)S(1)} %copy-done.4, f32[592,128]{1,0:T(8,128)S(1)} %collective-permute-done.13.refs_1_, ...), custom_call_target="tpu_custom_call" | custom-call | flops 3000000000 | bytes 9000000 | tf_op jit(solution)/shard_map/far_last/pallas_call | solution.py:575
  47.9 3.1 %collective-permute-start.19 = (f32[24,128]{1,0:T(8,128)S(1)}, f32[24,128]{1,0:T(8,128)S(1)}, u32[]{:S(2)}, u32[]{:S(2)}) collective-permute-start(f32[24,128]{1,0:T(8,128)S(1)} %get-tuple-element.70), channel_id=1, source_target_pairs={{4,0},{5,1},{6,2},{7,3},{8,4},{9,5},{10,6},{11,7},{12,8},{13,9},{1... | collective-permute-start | bytes 36872 | tf_op jit(solution)/shard_map/ppermute | solution.py:483
  51.1 1.3 %collective-permute-start.17 = (f32[24,128]{1,0:T(8,128)S(1)}, f32[24,128]{1,0:T(8,128)S(1)}, u32[]{:S(2)}, u32[]{:S(2)}) collective-permute-start(f32[24,128]{1,0:T(8,128)S(1)} %get-tuple-element.70), channel_id=1, source_target_pairs={{12,0},{13,1},{14,2},{15,3},{0,4},{1,5},{2,6},{3,7},{4,8},{5,9},{6... | collective-permute-start | bytes 36872 | tf_op jit(solution)/shard_map/ppermute | solution.py:483
  52.5 3.2 %collective-permute-done.18 = f32[24,128]{1,0:T(8,128)S(1)} collective-permute-done((f32[24,128]{1,0:T(8,128)S(1)}, f32[24,128]{1,0:T(8,128)S(1)}, u32[]{:S(2)}, u32[]{:S(2)}) %collective-permute-start.18) | collective-permute-done | bytes 12320 | tf_op jit(solution)/shard_map/ppermute | solution.py:483
  55.7 0.9 %collective-permute-done.17 = f32[24,128]{1,0:T(8,128)S(1)} collective-permute-done((f32[24,128]{1,0:T(8,128)S(1)}, f32[24,128]{1,0:T(8,128)S(1)}, u32[]{:S(2)}, u32[]{:S(2)}) %collective-permute-start.17) | collective-permute-done | bytes 12320 | tf_op jit(solution)/shard_map/ppermute | solution.py:483
  56.6 2.0 %collective-permute-start.21 = (f32[4,24,128]{2,1,0:T(8,128)S(1)}, f32[4,24,128]{2,1,0:T(8,128)S(1)}, u32[]{:S(2)}, u32[]{:S(2)}) collective-permute-start(f32[4,24,128]{2,1,0:T(8,128)S(1)} %pad_maximum_fusion.refs_20_), channel_id=1, source_target_pairs={{0,2},{1,3},{2,0},{3,1},{4,6},{5,7},{6,4},{7,5},{8,10},{9,11},{10,... | collective-permute-start | bytes 147464 | tf_op jit(solution)/shard_map/ppermute | solution.py:487
  58.6 2.3 %near_second.1.refs_28_ = f32[8,256]{1,0:T(8,128)S(1)} custom-call(f32[8,64,256]{2,1,0:T(8,128)S(1)} %copy-done.3, f32[8,256]{1,0:T(8,128)S(1)} %get-tuple-element.71.refs_1_.refs_27_.image, s32[2,8]{1,0:T(2,128)S(1)} %bitcast.10), custom_call_target="tpu_custom_call" | custom-call | flops 4000000000 | bytes 12000000 | tf_op jit(solution)/shard_map/near_second/pallas_call | solution.py:549
  60.9 0.2 collective-permute-done.21.refs_22_
  61.2 4.7 %far_second.1 = (f32[8,256]{1,0:T(8,128)S(1)}, f32[8,256]{1,0:T(8,128)S(1)}, f32[16,1,128]{2,1,0:T(1,128)S(1)}) custom-call(s32[60]{0:T(128)S(1)} %get-tuple-element.41.refs_0_, s32[60]{0:T(128)S(1)} %get-tuple-element.42.refs_1_, s32[1]{0:T(128)} %get-tuple-element.43.refs_2_, s32[44]{0:T(128)S(1)} %get-tuple-element.45.refs_3_, ...), custom_call_target="tpu_custom_call" | custom-call | flops 1000000000 | bytes 3000000 | tf_op jit(solution)/shard_map/far_second/pallas_call | solution.py:652
  65.9 10.2 %all_to_all.5.everyone = f32[16,1,128]{2,1,0:T(1,128)S(1)} all-to-all(f32[16,1,128]{2,1,0:T(1,128)S(1)} %get-tuple-element.73), channel_id=1, replica_groups=mesh['groups'=2,'leaf'=16] {'leaf'}, dimensions={0} | all-to-all | bytes 16384 | tf_op jit(solution)/shard_map/all_to_all | solution.py:491
  76.1 0.9 %finish.1 = (f32[8,256]{1,0:T(8,128)}, f32[8,256]{1,0:T(8,128)}) custom-call(f32[16,1,128]{2,1,0:T(1,128)S(1)} %all_to_all.5.everyone, f32[8,256]{1,0:T(8,128)S(1)} %copy-done.2, f32[8,256]{1,0:T(8,128)S(1)} %get-tuple-element.71.refs_1_.refs_27_.image, f32[8,256]{1,0:T(8,128)S(1)} %get-tuple-element.74.residual, f32[8,256]{1,0:T(8,128)S(1)} %get-tuple-element.75.along), custom_call_target="tpu_custom_call" | custom-call | flops 1000000000 | bytes 3000000 | tf_op jit(solution)/shard_map/finish/pallas_call | solution.py:676
  (39 shorter events, 0.2 us)
Async XLA Ops:
  0.6 20.6 %copy-start.2 = (f32[8,256]{1,0:T(8,128)S(1)}, f32[8,256]{1,0:T(8,128)}, u32[]{:S(2)}) copy-start(f32[8,256]{1,0:T(8,128)} %values.1) | copy-start | bytes 24580
  0.6 20.6 %copy-start.3 = (f32[8,64,256]{2,1,0:T(8,128)S(1)}, f32[8,64,256]{2,1,0:T(8,128)}, u32[]{:S(2)}) copy-start(f32[8,64,256]{2,1,0:T(8,128)} %refs_0_.3) | copy-start | bytes 1572868
  0.7 20.6 %copy-start.5 = (s32[8,2]{0,1:T(2,128)S(1)}, s32[8,2]{0,1:T(2,128)}, u32[]{:S(2)}) copy-start(s32[8,2]{0,1:T(2,128)} %param.9) | copy-start | bytes 196
  4.5 12.6 %collective-permute-start = (f32[592,128]{1,0:T(8,128)}, f32[592,128]{1,0:T(8,128)S(1)}, u32[]{:S(2)}, u32[]{:S(2)}) collective-permute-start(f32[592,128]{1,0:T(8,128)} %get-tuple-element.39.refs_1_.refs_2_.refs_0_), channel_id=1, source_target_pairs={{12,0},{13,1},{14,2},{15,3},{0,4},{1,5},{2,6},{3,7},{4,8},{5,9},{6... | collective-permute-start | bytes 909320 | tf_op jit(solution)/shard_map/ppermute | solution.py:483
  7.6 11.0 %collective-permute-start.3 = (f32[592,128]{1,0:T(8,128)}, f32[592,128]{1,0:T(8,128)S(1)}, u32[]{:S(2)}, u32[]{:S(2)}) collective-permute-start(f32[592,128]{1,0:T(8,128)} %get-tuple-element.39.refs_1_.refs_2_.refs_0_), channel_id=1, source_target_pairs={{0,2},{1,3},{2,0},{3,1},{4,6},{5,7},{6,4},{7,5},{8,10},{9,11},{10,... | collective-permute-start | bytes 909320 | tf_op jit(solution)/shard_map/ppermute | solution.py:487
  9.1 9.5 %collective-permute-start.14 = (f32[2,72,256]{2,1,0:T(8,128)}, f32[2,72,256]{2,1,0:T(8,128)S(1)}, u32[]{:S(2)}, u32[]{:S(2)}) collective-permute-start(f32[2,72,256]{2,1,0:T(8,128)} %get-tuple-element.53), channel_id=1, source_target_pairs={{1,0},{2,1},{3,2},{4,3},{5,4},{6,5},{7,6},{8,7},{9,8},{10,9},{11,1... | collective-permute-start | bytes 442376 | tf_op jit(solution)/shard_map/ppermute | solution.py:483
  10.3 18.7 %copy-start.4 = (f32[592,128]{1,0:T(8,128)S(1)}, f32[592,128]{1,0:T(8,128)}, u32[]{:S(2)}) copy-start(f32[592,128]{1,0:T(8,128)} %get-tuple-element.39.refs_1_.refs_2_.refs_0_) | copy-start | bytes 909316
  10.3 18.7 %copy-start.6 = (bf16[9,208,128]{2,1,0:T(8,128)(2,1)S(1)}, bf16[9,208,128]{2,1,0:T(8,128)(2,1)}, u32[]{:S(2)}) copy-start(bf16[9,208,128]{2,1,0:T(8,128)(2,1)} %get-tuple-element.40.refs_8_.refs_6_.refs_5_.refs_3_) | copy-start | bytes 1437700
  10.3 10.7 %collective-permute-start.15 = (f32[2,72,256]{2,1,0:T(8,128)}, f32[2,72,256]{2,1,0:T(8,128)S(1)}, u32[]{:S(2)}, u32[]{:S(2)}) collective-permute-start(f32[2,72,256]{2,1,0:T(8,128)} %get-tuple-element.54), channel_id=1, source_target_pairs={{15,0},{0,1},{1,2},{2,3},{3,4},{4,5},{5,6},{6,7},{7,8},{8,9},{9,10... | collective-permute-start | bytes 442376 | tf_op jit(solution)/shard_map/ppermute | solution.py:483
  17.1 10.1 %collective-permute-start.1 = (f32[592,128]{1,0:T(8,128)S(1)}, f32[592,128]{1,0:T(8,128)S(1)}, u32[]{:S(2)}, u32[]{:S(2)}) collective-permute-start(f32[592,128]{1,0:T(8,128)S(1)} %collective-permute-done.refs_6_.refs_0_), channel_id=1, source_target_pairs={{12,0},{13,1},{14,2},{15,3},{0,4},{1,5},{2,6},{3,7},{4,8},{5,9},{6... | collective-permute-start | bytes 909320 | tf_op jit(solution)/shard_map/ppermute | solution.py:483
  17.1 10.1 %collective-permute-start.2 = (f32[592,128]{1,0:T(8,128)}, f32[592,128]{1,0:T(8,128)S(1)}, u32[]{:S(2)}, u32[]{:S(2)}) collective-permute-start(f32[592,128]{1,0:T(8,128)} %get-tuple-element.39.refs_1_.refs_2_.refs_0_), channel_id=1, source_target_pairs={{0,1},{1,0},{2,3},{3,2},{4,5},{5,4},{6,7},{7,6},{8,9},{9,8},{10,11... | collective-permute-start | bytes 909320 | tf_op jit(solution)/shard_map/ppermute | solution.py:487
  18.6 9.8 %collective-permute-start.4 = (f32[592,128]{1,0:T(8,128)S(1)}, f32[592,128]{1,0:T(8,128)S(1)}, u32[]{:S(2)}, u32[]{:S(2)}) collective-permute-start(f32[592,128]{1,0:T(8,128)S(1)} %collective-permute-done.3.refs_4_), channel_id=1, source_target_pairs={{0,1},{1,0},{2,3},{3,2},{4,5},{5,4},{6,7},{7,6},{8,9},{9,8},{10,11... | collective-permute-start | bytes 909320 | tf_op jit(solution)/shard_map/ppermute | solution.py:487
  18.7 10.4 %collective-permute-start.6 = (f32[592,128]{1,0:T(8,128)S(1)}, f32[592,128]{1,0:T(8,128)S(1)}, u32[]{:S(2)}, u32[]{:S(2)}) collective-permute-start(f32[592,128]{1,0:T(8,128)S(1)} %collective-permute-done.refs_6_.refs_0_), channel_id=1, source_target_pairs={{0,2},{1,3},{2,0},{3,1},{4,6},{5,7},{6,4},{7,5},{8,10},{9,11},{10,... | collective-permute-start | bytes 909320 | tf_op jit(solution)/shard_map/ppermute | solution.py:487
  21.0 8.0 %collective-permute-start.5 = (f32[592,128]{1,0:T(8,128)S(1)}, f32[592,128]{1,0:T(8,128)S(1)}, u32[]{:S(2)}, u32[]{:S(2)}) collective-permute-start(f32[592,128]{1,0:T(8,128)S(1)} %collective-permute-done.refs_6_.refs_0_), channel_id=1, source_target_pairs={{0,1},{1,0},{2,3},{3,2},{4,5},{5,4},{6,7},{7,6},{8,9},{9,8},{10,11... | collective-permute-start | bytes 909320 | tf_op jit(solution)/shard_map/ppermute | solution.py:487
  27.2 9.2 %collective-permute-start.11 = (f32[592,128]{1,0:T(8,128)S(1)}, f32[592,128]{1,0:T(8,128)S(1)}, u32[]{:S(2)}, u32[]{:S(2)}) collective-permute-start(f32[592,128]{1,0:T(8,128)S(1)} %collective-permute-done.1.refs_0_.refs_4_), channel_id=1, source_target_pairs={{12,0},{13,1},{14,2},{15,3},{0,4},{1,5},{2,6},{3,7},{4,8},{5,9},{6... | collective-permute-start | bytes 909320 | tf_op jit(solution)/shard_map/ppermute | solution.py:483
  27.2 9.8 %collective-permute-start.9 = (f32[592,128]{1,0:T(8,128)S(1)}, f32[592,128]{1,0:T(8,128)S(1)}, u32[]{:S(2)}, u32[]{:S(2)}) collective-permute-start(f32[592,128]{1,0:T(8,128)S(1)} %collective-permute-done.1.refs_0_.refs_4_), channel_id=1, source_target_pairs={{0,2},{1,3},{2,0},{3,1},{4,6},{5,7},{6,4},{7,5},{8,10},{9,11},{10,... | collective-permute-start | bytes 909320 | tf_op jit(solution)/shard_map/ppermute | solution.py:487
  28.5 9.1 %collective-permute-start.8 = (f32[592,128]{1,0:T(8,128)S(1)}, f32[592,128]{1,0:T(8,128)S(1)}, u32[]{:S(2)}, u32[]{:S(2)}) collective-permute-start(f32[592,128]{1,0:T(8,128)S(1)} %collective-permute-done.1.refs_0_.refs_4_), channel_id=1, source_target_pairs={{0,1},{1,0},{2,3},{3,2},{4,5},{5,4},{6,7},{7,6},{8,9},{9,8},{10,11... | collective-permute-start | bytes 909320 | tf_op jit(solution)/shard_map/ppermute | solution.py:487
  29.1 8.5 %collective-permute-start.7 = (f32[592,128]{1,0:T(8,128)S(1)}, f32[592,128]{1,0:T(8,128)S(1)}, u32[]{:S(2)}, u32[]{:S(2)}) collective-permute-start(f32[592,128]{1,0:T(8,128)S(1)} %collective-permute-done.6.refs_2_), channel_id=1, source_target_pairs={{0,1},{1,0},{2,3},{3,2},{4,5},{5,4},{6,7},{7,6},{8,9},{9,8},{10,11... | collective-permute-start | bytes 909320 | tf_op jit(solution)/shard_map/ppermute | solution.py:487
  36.4 7.4 %collective-permute-start.13 = (f32[592,128]{1,0:T(8,128)S(1)}, f32[592,128]{1,0:T(8,128)S(1)}, u32[]{:S(2)}, u32[]{:S(2)}) collective-permute-start(f32[592,128]{1,0:T(8,128)S(1)} %collective-permute-done.11.refs_3_), channel_id=1, source_target_pairs={{0,2},{1,3},{2,0},{3,1},{4,6},{5,7},{6,4},{7,5},{8,10},{9,11},{10,... | collective-permute-start | bytes 909320 | tf_op jit(solution)/shard_map/ppermute | solution.py:487
  37.1 3.6 %collective-permute-start.12 = (f32[592,128]{1,0:T(8,128)S(1)}, f32[592,128]{1,0:T(8,128)S(1)}, u32[]{:S(2)}, u32[]{:S(2)}) collective-permute-start(f32[592,128]{1,0:T(8,128)S(1)} %collective-permute-done.11.refs_3_), channel_id=1, source_target_pairs={{0,1},{1,0},{2,3},{3,2},{4,5},{5,4},{6,7},{7,6},{8,9},{9,8},{10,11... | collective-permute-start | bytes 909320 | tf_op jit(solution)/shard_map/ppermute | solution.py:487
  37.1 3.6 %collective-permute-start.10 = (f32[592,128]{1,0:T(8,128)S(1)}, f32[592,128]{1,0:T(8,128)S(1)}, u32[]{:S(2)}, u32[]{:S(2)}) collective-permute-start(f32[592,128]{1,0:T(8,128)S(1)} %collective-permute-done.9.refs_1_), channel_id=1, source_target_pairs={{0,1},{1,0},{2,3},{3,2},{4,5},{5,4},{6,7},{7,6},{8,9},{9,8},{10,11... | collective-permute-start | bytes 909320 | tf_op jit(solution)/shard_map/ppermute | solution.py:487
  40.7 4.8 %copy-start = (f32[8,128,256]{2,1,0:T(8,128)S(1)}, f32[8,128,256]{2,1,0:T(8,128)}, u32[]{:S(2)}) copy-start(f32[8,128,256]{2,1,0:T(8,128)} %get-tuple-element.57.refs_5_.refs_24_) | copy-start | bytes 3145732
  40.7 4.8 %copy-start.1 = (f32[8,128,256]{2,1,0:T(8,128)S(1)}, f32[8,128,256]{2,1,0:T(8,128)}, u32[]{:S(2)}) copy-start(f32[8,128,256]{2,1,0:T(8,128)} %get-tuple-element.58.refs_6_.refs_25_) | copy-start | bytes 3145732
  43.8 1.6 %collective-permute-start.16 = (f32[592,128]{1,0:T(8,128)S(1)}, f32[592,128]{1,0:T(8,128)S(1)}, u32[]{:S(2)}, u32[]{:S(2)}) collective-permute-start(f32[592,128]{1,0:T(8,128)S(1)} %collective-permute-done.13.refs_1_), channel_id=1, source_target_pairs={{0,1},{1,0},{2,3},{3,2},{4,5},{5,4},{6,7},{7,6},{8,9},{9,8},{10,11... | collective-permute-start | bytes 909320 | tf_op jit(solution)/shard_map/ppermute | solution.py:487
  47.9 4.6 %collective-permute-start.19 = (f32[24,128]{1,0:T(8,128)S(1)}, f32[24,128]{1,0:T(8,128)S(1)}, u32[]{:S(2)}, u32[]{:S(2)}) collective-permute-start(f32[24,128]{1,0:T(8,128)S(1)} %get-tuple-element.70), channel_id=1, source_target_pairs={{4,0},{5,1},{6,2},{7,3},{8,4},{9,5},{10,6},{11,7},{12,8},{13,9},{1... | collective-permute-start | bytes 36872 | tf_op jit(solution)/shard_map/ppermute | solution.py:483
  51.1 4.6 %collective-permute-start.18 = (f32[24,128]{1,0:T(8,128)S(1)}, f32[24,128]{1,0:T(8,128)S(1)}, u32[]{:S(2)}, u32[]{:S(2)}) collective-permute-start(f32[24,128]{1,0:T(8,128)S(1)} %get-tuple-element.70), channel_id=1, source_target_pairs={{8,0},{9,1},{10,2},{11,3},{12,4},{13,5},{14,6},{15,7},{0,8},{1,9},... | collective-permute-start | bytes 36872 | tf_op jit(solution)/shard_map/ppermute | solution.py:483
  51.1 5.5 %collective-permute-start.17 = (f32[24,128]{1,0:T(8,128)S(1)}, f32[24,128]{1,0:T(8,128)S(1)}, u32[]{:S(2)}, u32[]{:S(2)}) collective-permute-start(f32[24,128]{1,0:T(8,128)S(1)} %get-tuple-element.70), channel_id=1, source_target_pairs={{12,0},{13,1},{14,2},{15,3},{0,4},{1,5},{2,6},{3,7},{4,8},{5,9},{6... | collective-permute-start | bytes 36872 | tf_op jit(solution)/shard_map/ppermute | solution.py:483
  56.6 4.3 %collective-permute-start.22 = (f32[4,24,128]{2,1,0:T(8,128)S(1)}, f32[4,24,128]{2,1,0:T(8,128)S(1)}, u32[]{:S(2)}, u32[]{:S(2)}) collective-permute-start(f32[4,24,128]{2,1,0:T(8,128)S(1)} %pad_maximum_fusion.refs_20_), channel_id=1, source_target_pairs={{0,3},{1,2},{2,1},{3,0},{4,7},{5,6},{6,5},{7,4},{8,11},{9,10},{10,... | collective-permute-start | bytes 147464 | tf_op jit(solution)/shard_map/ppermute | solution.py:487
  56.6 4.6 %collective-permute-start.21 = (f32[4,24,128]{2,1,0:T(8,128)S(1)}, f32[4,24,128]{2,1,0:T(8,128)S(1)}, u32[]{:S(2)}, u32[]{:S(2)}) collective-permute-start(f32[4,24,128]{2,1,0:T(8,128)S(1)} %pad_maximum_fusion.refs_20_), channel_id=1, source_target_pairs={{0,2},{1,3},{2,0},{3,1},{4,6},{5,7},{6,4},{7,5},{8,10},{9,11},{10,... | collective-permute-start | bytes 147464 | tf_op jit(solution)/shard_map/ppermute | solution.py:487
  58.6 2.6 %collective-permute-start.20 = (f32[4,24,128]{2,1,0:T(8,128)S(1)}, f32[4,24,128]{2,1,0:T(8,128)S(1)}, u32[]{:S(2)}, u32[]{:S(2)}) collective-permute-start(f32[4,24,128]{2,1,0:T(8,128)S(1)} %pad_maximum_fusion.refs_20_), channel_id=1, source_target_pairs={{0,1},{1,0},{2,3},{3,2},{4,5},{5,4},{6,7},{7,6},{8,9},{9,8},{10,11... | collective-permute-start | bytes 147464 | tf_op jit(solution)/shard_map/ppermute | solution.py:487
